TPU v7x, 512 devices: a whole 4x4x16 slice. The times are simulated.
512 devices in a mesh: ctx: 64 (over z, y), head: 8 (over x, core).
Axes of the slice: x: 4, y: 4, z: 16, core: 2. Of those that a mesh axis runs over, the one named last changes fastest.
Arguments:
- queries: bfloat16 [8192, 16, 128], P('ctx', 'head'), may hold values from -6 to 6
- key_rows: bfloat16 [8192, 2, 16, 128], P('ctx', None, 'head'), may hold values from -6 to 6
- value_rows: bfloat16 [8192, 2, 16, 128], P('ctx', None, 'head'), may hold values from -6 to 6
- strengths: float32 [8192, 2, 16], P('ctx', None, 'head'), may hold values from 0 to 2
- log_decay: float32 [8192, 16], P('ctx', 'head'), may hold values from -2 to 0
- norm_gain: float32 [16, 128], P('head'), may hold values from 0.1 to 1.9
- out_weight: bfloat16 [2048, 2048], P('head'), may hold values from -0.125 to 0.125
Outputs:
- mixer_out: bfloat16 [8192, 2048], P(('ctx', 'head'))
All inputs are finite; a program needn't handle non-finite values.
Results may differ from a plain program's by a relative error of at most 0.0049.
Values sent between devices are 32-bit elements; how exact they have to be, the bound alone decides.
No kernel may reach another device: no remote copies, remote signals or barrier semaphores. Data moves between devices by JAX's collectives and lax.ppermute only.
A program may use at most 64 MiB of HBM per device.

v0:
```python
import jax
import jax.numpy as jnp
from jax import lax
from jax.sharding import PartitionSpec as P

HIGHEST = lax.Precision.HIGHEST


def from_behind(value, axis, steps):
    count = lax.axis_size(axis)
    leading, last = (max(0, -steps), min(count, count - steps))
    return lax.ppermute(value, axis, [(source, source + steps) for source in range(leading, last)])


def unit_rows(values_in):
    return values_in * lax.rsqrt(jnp.sum(values_in * values_in, axis=-1, keepdims=True) + 1e-06)


def group_parts(keys_c, values_c, beta_c, decay_c):
    length = keys_c.shape[1]
    cumul_log = jnp.cumsum(decay_c, axis=1)
    row_ids = lax.broadcasted_iota(jnp.int32, (length, length), 0)
    col_ids = lax.broadcasted_iota(jnp.int32, (length, length), 1)
    weight = jnp.exp(
        jnp.where(row_ids >= col_ids, cumul_log[:, :, None] - cumul_log[:, None, :], -1e30)
    )
    key_inner = jnp.einsum("hrk,hik->hri", keys_c, keys_c, precision=HIGHEST)
    system = jnp.where(row_ids > col_ids, beta_c[:, :, None] * weight * key_inner, 0.0) + jnp.eye(
        length, dtype=jnp.float32
    )
    right_side = jnp.concatenate(
        [beta_c[:, :, None] * values_c, (beta_c * jnp.exp(cumul_log))[:, :, None] * keys_c], axis=2
    )
    solved = jax.scipy.linalg.solve_triangular(system, right_side, lower=True, unit_diagonal=True)
    width_v = values_c.shape[2]
    fresh_vals = solved[:, :, :width_v]
    pulled = solved[:, :, width_v:]
    tail_keys = jnp.exp(cumul_log[:, -1:] - cumul_log)[:, :, None] * keys_c
    identity = jnp.eye(keys_c.shape[2], dtype=jnp.float32)
    carry_mat = jnp.exp(cumul_log[:, -1])[:, None, None] * identity - jnp.einsum(
        "hik,hij->hkj", pulled, tail_keys, precision=HIGHEST
    )
    write_mat = jnp.einsum("hiv,hij->hvj", fresh_vals, tail_keys, precision=HIGHEST)
    return (cumul_log, weight, fresh_vals, pulled, carry_mat, write_mat)


def group_output(query_c, keys_c, pieces, start_state):
    cumul_log, weight, fresh_vals, pulled = (pieces[0], pieces[1], pieces[2], pieces[3])
    scores = jnp.einsum("htk,hik->hti", query_c, keys_c, precision=HIGHEST) * weight[:, 1::2, :]
    through = jnp.exp(cumul_log[:, 1::2])[:, :, None] * query_c - jnp.einsum(
        "hti,hik->htk", scores, pulled, precision=HIGHEST
    )
    own_out = jnp.einsum("hti,hiv->htv", scores, fresh_vals, precision=HIGHEST)
    return (own_out + jnp.einsum("htk,hvk->htv", through, start_state, precision=HIGHEST), through)


def advance(state_now, carry_mat, write_mat):
    return jnp.einsum("hvk,hkj->hvj", state_now, carry_mat, precision=HIGHEST) + write_mat


def per_device(queries, key_rows, value_rows, strengths, log_decay, norm_gain, out_weight):
    tok_count = queries.shape[0]
    heads_here = queries.shape[1]
    width_k = queries.shape[2]
    width_v = value_rows.shape[3]
    block_tokens = min(tok_count, 256)
    blocks = tok_count // block_tokens
    span_rows = 2 * block_tokens
    query_b = (
        unit_rows(queries.astype(jnp.float32))
        .reshape(blocks, block_tokens, heads_here, width_k)
        .transpose(0, 2, 1, 3)
    )
    keys_b = (
        unit_rows(key_rows.astype(jnp.float32))
        .reshape(blocks, span_rows, heads_here, width_k)
        .transpose(0, 2, 1, 3)
    )
    values_b = (
        value_rows.astype(jnp.float32)
        .reshape(blocks, span_rows, heads_here, width_v)
        .transpose(0, 2, 1, 3)
    )
    beta_b = strengths.reshape(blocks, span_rows, heads_here).transpose(0, 2, 1)
    decay_full = jnp.stack([log_decay, jnp.zeros_like(log_decay)], axis=1)
    decay_b = decay_full.reshape(blocks, span_rows, heads_here).transpose(0, 2, 1)
    zero_state = jnp.zeros((heads_here, width_v, width_k), jnp.float32)
    unit_state = jnp.broadcast_to(
        jnp.eye(width_k, dtype=jnp.float32), (heads_here, width_k, width_k)
    )
    block_inputs = (query_b, keys_b, values_b, beta_b, decay_b)

    def store_step(carried, block_data):
        state_now, prefix = carried
        query_c, keys_c, values_c, beta_c, decay_c = block_data
        pieces = group_parts(keys_c, values_c, beta_c, decay_c)
        own_out, through = group_output(query_c, keys_c, pieces, state_now)
        mapped = jnp.einsum("htk,hjk->htj", through, prefix, precision=HIGHEST)
        next_prefix = jnp.einsum("hkj,hjl->hkl", prefix, pieces[4], precision=HIGHEST)
        return ((advance(state_now, pieces[4], pieces[5]), next_prefix), (own_out, mapped))

    first_pass = lax.scan(store_step, (zero_state, unit_state), block_inputs)
    write_dev, carry_dev = first_pass[0]
    own_blocks, mapped_blocks = first_pass[1]

    def relay_step(turn_index, pair):
        arrived = from_behind(pair[1], "ctx", 1)
        return (arrived, advance(arrived, carry_dev, write_dev))

    incoming = lax.fori_loop(0, lax.axis_size("ctx") - 1, relay_step, (zero_state, write_dev))[0]
    outputs = own_blocks + jnp.einsum("bhtk,hvk->bhtv", mapped_blocks, incoming, precision=HIGHEST)
    outputs = outputs.transpose(0, 2, 1, 3).reshape(tok_count, heads_here, width_v)
    scaled = (
        outputs
        * lax.rsqrt(jnp.mean(outputs * outputs, axis=-1, keepdims=True) + 1e-05)
        * norm_gain[None, :, :]
    )
    hidden = scaled.reshape(tok_count, heads_here * width_v).astype(jnp.bfloat16)
    mixer_rows = lax.psum_scatter(
        jnp.dot(hidden, out_weight, preferred_element_type=jnp.float32),
        "head",
        scatter_dimension=0,
        tiled=True,
    )
    return mixer_rows.astype(jnp.bfloat16)


def solution(mesh):
    in_specs = (
        P("ctx", "head", None),
        P("ctx", None, "head", None),
        P("ctx", None, "head", None),
        P("ctx", None, "head"),
        P("ctx", "head"),
        P("head", None),
        P("head", None),
    )
    out_specs = P(("ctx", "head"), None)
    return jax.shard_map(
        per_device, mesh=mesh, in_specs=in_specs, out_specs=out_specs, check_vma=False
    )
```

profile of v0, /device:TPU:16, one launch (start us, length us, event | category | flops | bytes accessed | tf_op | source)
XLA Modules:
  0.0 808.0 jit_solution(1168550771570529127)
XLA Ops:
  15.9 39.3 %custom-call.5 = f32[2,2,128,128]{2,3,1,0:T(8,128)S(1)} custom-call(f32[2,2,128,128]{3,2,1,0:T(8,128)S(1)} %bitcast.124), custom_call_target="InvertDiagBlocksLowerTriangular" | custom-call | tf_op jit(solution)/shard_map/while/body/eval_jaxpr/jit(_solve_triangular)/vmap()/triangular_solve | solution.py:34
  62.3 634.0 %while.10 = (s32[]{:T(128)}, f32[2,128,128]{2,1,0:T(8,128)}, f32[2,128,128]{2,1,0:T(8,128)S(1)}, f32[2,128,128]{2,1,0:T(8,128)S(1)}, f32[2,128,128]{2,1,0:T(8,128)S(1)}) while((s32[]{:T(128)}, f32[2,128,128]{2,1,0:T(8,128)}, f32[2,128,128]{2,1,0:T(8,128)S(1)}, f32[2,128,128]{2,1,0:T(8,128)S(1)}, f32[2,128,128]{2,1,0:T(8,128)S(1)}) %tuple.49), condition=%wide.region_5.6_spmd.clone, body=%wide.region_4.5_spmd.sunk.clone | while | flops 50364416 | bytes 1572993 | solution.py:110
  349.8 6.8 collective-permute-start
  476.6 7.1 collective-permute-start
  486.9 7.8 collective-permute-start
  497.9 7.7 collective-permute-start
  509.4 7.5 collective-permute-start
  521.2 7.6 collective-permute-start
  532.1 7.6 collective-permute-start
  542.8 7.7 collective-permute-start
  553.7 7.9 collective-permute-start
  564.7 7.4 collective-permute-start
  575.2 7.7 collective-permute-start
  586.1 7.9 collective-permute-start
  597.1 7.4 collective-permute-start
  608.0 8.4 %collective-permute-start = (f32[2,128,128]{2,1,0:T(8,128)S(1)}, f32[2,128,128]{2,1,0:T(8,128)S(1)}, u32[]{:S(2)}, u32[]{:S(2)}) collective-permute-start(f32[2,128,128]{2,1,0:T(8,128)S(1)} %get-tuple-element.200), channel_id=1, source_target_pairs={{0,8},{8,16},{16,24},{24,32},{32,40},{40,48},{48,56},{56,64},{64,7... | collective-permute-start | bytes 393224 | tf_op jit(solution)/shard_map/while/body/eval_jaxpr/ppermute | solution.py:12
  620.5 7.5 collective-permute-start
  631.3 7.7 collective-permute-start
  642.2 7.8 collective-permute-start
  653.1 7.8 collective-permute-start
  664.0 7.5 collective-permute-start
  674.6 7.9 collective-permute-start
  685.6 7.6 collective-permute-start
  699.9 99.8 %reduce-scatter.2.cloned.1.call-done = f32[16,2048]{1,0:T(8,128)} async-done(((f32[128,2048]{1,0:T(8,128)}), f32[16,2048]{1,0:T(8,128)}) %reduce-scatter.2.cloned.1.call-update) | async-done | bytes 131088 | tf_op jit(solution)/shard_map/reduce_scatter | solution.py:119
  (371 shorter events, 497.9 us)
Async XLA Ops:
  6.5 793.1 %reduce-scatter.2.cloned.1.call-start = ((), (), s32[]{:S(2)}) async-start(), calls=%async_computation.1 | async-start | bytes 1179648 | tf_op jit(solution)/shard_map/reduce_scatter | solution.py:119
  124.0 10.5 %collective-permute-start = (f32[2,128,128]{2,1,0:T(8,128)S(1)}, f32[2,128,128]{2,1,0:T(8,128)S(1)}, u32[]{:S(2)}, u32[]{:S(2)}) collective-permute-start(f32[2,128,128]{2,1,0:T(8,128)S(1)} %get-tuple-element.200), channel_id=1, source_target_pairs={{0,8},{8,16},{16,24},{24,32},{32,40},{40,48},{48,56},{56,64},{64,7... | collective-permute-start | bytes 393224 | tf_op jit(solution)/shard_map/while/body/eval_jaxpr/ppermute | solution.py:12
  202.7 10.3 %collective-permute-start = (f32[2,128,128]{2,1,0:T(8,128)S(1)}, f32[2,128,128]{2,1,0:T(8,128)S(1)}, u32[]{:S(2)}, u32[]{:S(2)}) collective-permute-start(f32[2,128,128]{2,1,0:T(8,128)S(1)} %get-tuple-element.200), channel_id=1, source_target_pairs={{0,8},{8,16},{16,24},{24,32},{32,40},{40,48},{48,56},{56,64},{64,7... | collective-permute-start | bytes 393224 | tf_op jit(solution)/shard_map/while/body/eval_jaxpr/ppermute | solution.py:12
  271.0 10.2 %collective-permute-start = (f32[2,128,128]{2,1,0:T(8,128)S(1)}, f32[2,128,128]{2,1,0:T(8,128)S(1)}, u32[]{:S(2)}, u32[]{:S(2)}) collective-permute-start(f32[2,128,128]{2,1,0:T(8,128)S(1)} %get-tuple-element.200), channel_id=1, source_target_pairs={{0,8},{8,16},{16,24},{24,32},{32,40},{40,48},{48,56},{56,64},{64,7... | collective-permute-start | bytes 393224 | tf_op jit(solution)/shard_map/while/body/eval_jaxpr/ppermute | solution.py:12
  349.8 10.5 %collective-permute-start = (f32[2,128,128]{2,1,0:T(8,128)S(1)}, f32[2,128,128]{2,1,0:T(8,128)S(1)}, u32[]{:S(2)}, u32[]{:S(2)}) collective-permute-start(f32[2,128,128]{2,1,0:T(8,128)S(1)} %get-tuple-element.200), channel_id=1, source_target_pairs={{0,8},{8,16},{16,24},{24,32},{32,40},{40,48},{48,56},{56,64},{64,7... | collective-permute-start | bytes 393224 | tf_op jit(solution)/shard_map/while/body/eval_jaxpr/ppermute | solution.py:12
  486.9 10.4 %collective-permute-start = (f32[2,128,128]{2,1,0:T(8,128)S(1)}, f32[2,128,128]{2,1,0:T(8,128)S(1)}, u32[]{:S(2)}, u32[]{:S(2)}) collective-permute-start(f32[2,128,128]{2,1,0:T(8,128)S(1)} %get-tuple-element.200), channel_id=1, source_target_pairs={{0,8},{8,16},{16,24},{24,32},{32,40},{40,48},{48,56},{56,64},{64,7... | collective-permute-start | bytes 393224 | tf_op jit(solution)/shard_map/while/body/eval_jaxpr/ppermute | solution.py:12
  497.9 10.8 %collective-permute-start = (f32[2,128,128]{2,1,0:T(8,128)S(1)}, f32[2,128,128]{2,1,0:T(8,128)S(1)}, u32[]{:S(2)}, u32[]{:S(2)}) collective-permute-start(f32[2,128,128]{2,1,0:T(8,128)S(1)} %get-tuple-element.200), channel_id=1, source_target_pairs={{0,8},{8,16},{16,24},{24,32},{32,40},{40,48},{48,56},{56,64},{64,7... | collective-permute-start | bytes 393224 | tf_op jit(solution)/shard_map/while/body/eval_jaxpr/ppermute | solution.py:12
  509.4 11.2 %collective-permute-start = (f32[2,128,128]{2,1,0:T(8,128)S(1)}, f32[2,128,128]{2,1,0:T(8,128)S(1)}, u32[]{:S(2)}, u32[]{:S(2)}) collective-permute-start(f32[2,128,128]{2,1,0:T(8,128)S(1)} %get-tuple-element.200), channel_id=1, source_target_pairs={{0,8},{8,16},{16,24},{24,32},{32,40},{40,48},{48,56},{56,64},{64,7... | collective-permute-start | bytes 393224 | tf_op jit(solution)/shard_map/while/body/eval_jaxpr/ppermute | solution.py:12
  521.2 10.2 %collective-permute-start = (f32[2,128,128]{2,1,0:T(8,128)S(1)}, f32[2,128,128]{2,1,0:T(8,128)S(1)}, u32[]{:S(2)}, u32[]{:S(2)}) collective-permute-start(f32[2,128,128]{2,1,0:T(8,128)S(1)} %get-tuple-element.200), channel_id=1, source_target_pairs={{0,8},{8,16},{16,24},{24,32},{32,40},{40,48},{48,56},{56,64},{64,7... | collective-permute-start | bytes 393224 | tf_op jit(solution)/shard_map/while/body/eval_jaxpr/ppermute | solution.py:12
  532.1 10.1 %collective-permute-start = (f32[2,128,128]{2,1,0:T(8,128)S(1)}, f32[2,128,128]{2,1,0:T(8,128)S(1)}, u32[]{:S(2)}, u32[]{:S(2)}) collective-permute-start(f32[2,128,128]{2,1,0:T(8,128)S(1)} %get-tuple-element.200), channel_id=1, source_target_pairs={{0,8},{8,16},{16,24},{24,32},{32,40},{40,48},{48,56},{56,64},{64,7... | collective-permute-start | bytes 393224 | tf_op jit(solution)/shard_map/while/body/eval_jaxpr/ppermute | solution.py:12
  542.8 10.2 %collective-permute-start = (f32[2,128,128]{2,1,0:T(8,128)S(1)}, f32[2,128,128]{2,1,0:T(8,128)S(1)}, u32[]{:S(2)}, u32[]{:S(2)}) collective-permute-start(f32[2,128,128]{2,1,0:T(8,128)S(1)} %get-tuple-element.200), channel_id=1, source_target_pairs={{0,8},{8,16},{16,24},{24,32},{32,40},{40,48},{48,56},{56,64},{64,7... | collective-permute-start | bytes 393224 | tf_op jit(solution)/shard_map/while/body/eval_jaxpr/ppermute | solution.py:12
  553.7 10.4 %collective-permute-start = (f32[2,128,128]{2,1,0:T(8,128)S(1)}, f32[2,128,128]{2,1,0:T(8,128)S(1)}, u32[]{:S(2)}, u32[]{:S(2)}) collective-permute-start(f32[2,128,128]{2,1,0:T(8,128)S(1)} %get-tuple-element.200), channel_id=1, source_target_pairs={{0,8},{8,16},{16,24},{24,32},{32,40},{40,48},{48,56},{56,64},{64,7... | collective-permute-start | bytes 393224 | tf_op jit(solution)/shard_map/while/body/eval_jaxpr/ppermute | solution.py:12
  564.7 9.9 %collective-permute-start = (f32[2,128,128]{2,1,0:T(8,128)S(1)}, f32[2,128,128]{2,1,0:T(8,128)S(1)}, u32[]{:S(2)}, u32[]{:S(2)}) collective-permute-start(f32[2,128,128]{2,1,0:T(8,128)S(1)} %get-tuple-element.200), channel_id=1, source_target_pairs={{0,8},{8,16},{16,24},{24,32},{32,40},{40,48},{48,56},{56,64},{64,7... | collective-permute-start | bytes 393224 | tf_op jit(solution)/shard_map/while/body/eval_jaxpr/ppermute | solution.py:12
  575.2 10.2 %collective-permute-start = (f32[2,128,128]{2,1,0:T(8,128)S(1)}, f32[2,128,128]{2,1,0:T(8,128)S(1)}, u32[]{:S(2)}, u32[]{:S(2)}) collective-permute-start(f32[2,128,128]{2,1,0:T(8,128)S(1)} %get-tuple-element.200), channel_id=1, source_target_pairs={{0,8},{8,16},{16,24},{24,32},{32,40},{40,48},{48,56},{56,64},{64,7... | collective-permute-start | bytes 393224 | tf_op jit(solution)/shard_map/while/body/eval_jaxpr/ppermute | solution.py:12
  586.1 10.4 %collective-permute-start = (f32[2,128,128]{2,1,0:T(8,128)S(1)}, f32[2,128,128]{2,1,0:T(8,128)S(1)}, u32[]{:S(2)}, u32[]{:S(2)}) collective-permute-start(f32[2,128,128]{2,1,0:T(8,128)S(1)} %get-tuple-element.200), channel_id=1, source_target_pairs={{0,8},{8,16},{16,24},{24,32},{32,40},{40,48},{48,56},{56,64},{64,7... | collective-permute-start | bytes 393224 | tf_op jit(solution)/shard_map/while/body/eval_jaxpr/ppermute | solution.py:12
  597.1 10.3 %collective-permute-start = (f32[2,128,128]{2,1,0:T(8,128)S(1)}, f32[2,128,128]{2,1,0:T(8,128)S(1)}, u32[]{:S(2)}, u32[]{:S(2)}) collective-permute-start(f32[2,128,128]{2,1,0:T(8,128)S(1)} %get-tuple-element.200), channel_id=1, source_target_pairs={{0,8},{8,16},{16,24},{24,32},{32,40},{40,48},{48,56},{56,64},{64,7... | collective-permute-start | bytes 393224 | tf_op jit(solution)/shard_map/while/body/eval_jaxpr/ppermute | solution.py:12
  608.0 11.8 %collective-permute-start = (f32[2,128,128]{2,1,0:T(8,128)S(1)}, f32[2,128,128]{2,1,0:T(8,128)S(1)}, u32[]{:S(2)}, u32[]{:S(2)}) collective-permute-start(f32[2,128,128]{2,1,0:T(8,128)S(1)} %get-tuple-element.200), channel_id=1, source_target_pairs={{0,8},{8,16},{16,24},{24,32},{32,40},{40,48},{48,56},{56,64},{64,7... | collective-permute-start | bytes 393224 | tf_op jit(solution)/shard_map/while/body/eval_jaxpr/ppermute | solution.py:12
  620.5 10.2 %collective-permute-start = (f32[2,128,128]{2,1,0:T(8,128)S(1)}, f32[2,128,128]{2,1,0:T(8,128)S(1)}, u32[]{:S(2)}, u32[]{:S(2)}) collective-permute-start(f32[2,128,128]{2,1,0:T(8,128)S(1)} %get-tuple-element.200), channel_id=1, source_target_pairs={{0,8},{8,16},{16,24},{24,32},{32,40},{40,48},{48,56},{56,64},{64,7... | collective-permute-start | bytes 393224 | tf_op jit(solution)/shard_map/while/body/eval_jaxpr/ppermute | solution.py:12
  631.3 10.2 %collective-permute-start = (f32[2,128,128]{2,1,0:T(8,128)S(1)}, f32[2,128,128]{2,1,0:T(8,128)S(1)}, u32[]{:S(2)}, u32[]{:S(2)}) collective-permute-start(f32[2,128,128]{2,1,0:T(8,128)S(1)} %get-tuple-element.200), channel_id=1, source_target_pairs={{0,8},{8,16},{16,24},{24,32},{32,40},{40,48},{48,56},{56,64},{64,7... | collective-permute-start | bytes 393224 | tf_op jit(solution)/shard_map/while/body/eval_jaxpr/ppermute | solution.py:12
  642.2 10.3 %collective-permute-start = (f32[2,128,128]{2,1,0:T(8,128)S(1)}, f32[2,128,128]{2,1,0:T(8,128)S(1)}, u32[]{:S(2)}, u32[]{:S(2)}) collective-permute-start(f32[2,128,128]{2,1,0:T(8,128)S(1)} %get-tuple-element.200), channel_id=1, source_target_pairs={{0,8},{8,16},{16,24},{24,32},{32,40},{40,48},{48,56},{56,64},{64,7... | collective-permute-start | bytes 393224 | tf_op jit(solution)/shard_map/while/body/eval_jaxpr/ppermute | solution.py:12
  653.1 10.3 %collective-permute-start = (f32[2,128,128]{2,1,0:T(8,128)S(1)}, f32[2,128,128]{2,1,0:T(8,128)S(1)}, u32[]{:S(2)}, u32[]{:S(2)}) collective-permute-start(f32[2,128,128]{2,1,0:T(8,128)S(1)} %get-tuple-element.200), channel_id=1, source_target_pairs={{0,8},{8,16},{16,24},{24,32},{32,40},{40,48},{48,56},{56,64},{64,7... | collective-permute-start | bytes 393224 | tf_op jit(solution)/shard_map/while/body/eval_jaxpr/ppermute | solution.py:12
  664.0 10.0 %collective-permute-start = (f32[2,128,128]{2,1,0:T(8,128)S(1)}, f32[2,128,128]{2,1,0:T(8,128)S(1)}, u32[]{:S(2)}, u32[]{:S(2)}) collective-permute-start(f32[2,128,128]{2,1,0:T(8,128)S(1)} %get-tuple-element.200), channel_id=1, source_target_pairs={{0,8},{8,16},{16,24},{24,32},{32,40},{40,48},{48,56},{56,64},{64,7... | collective-permute-start | bytes 393224 | tf_op jit(solution)/shard_map/while/body/eval_jaxpr/ppermute | solution.py:12
  674.6 10.4 %collective-permute-start = (f32[2,128,128]{2,1,0:T(8,128)S(1)}, f32[2,128,128]{2,1,0:T(8,128)S(1)}, u32[]{:S(2)}, u32[]{:S(2)}) collective-permute-start(f32[2,128,128]{2,1,0:T(8,128)S(1)} %get-tuple-element.200), channel_id=1, source_target_pairs={{0,8},{8,16},{16,24},{24,32},{32,40},{40,48},{48,56},{56,64},{64,7... | collective-permute-start | bytes 393224 | tf_op jit(solution)/shard_map/while/body/eval_jaxpr/ppermute | solution.py:12
  685.6 10.1 %collective-permute-start = (f32[2,128,128]{2,1,0:T(8,128)S(1)}, f32[2,128,128]{2,1,0:T(8,128)S(1)}, u32[]{:S(2)}, u32[]{:S(2)}) collective-permute-start(f32[2,128,128]{2,1,0:T(8,128)S(1)} %get-tuple-element.200), channel_id=1, source_target_pairs={{0,8},{8,16},{16,24},{24,32},{32,40},{40,48},{48,56},{56,64},{64,7... | collective-permute-start | bytes 393224 | tf_op jit(solution)/shard_map/while/body/eval_jaxpr/ppermute | solution.py:12
  (110 other events, 1134.7 us)
Sparse Core Ops, SparseCore 0:
  700.0 99.6 reduce-scatter.1
where the time goes:
time: 811 us; the launch traced here: 808 us
  starting transfers between devices  419 us (52%)
  waiting for transfers between devices  274 us (34%)
  other arithmetic  43.4 us (5%)
  local copies, waits for them, and re-layouts  31.2 us (4%)
  matrix products  25.4 us (3%)
  between operations  13.7 us (2%)
    ppermute x63, starting transfers between devices, from_behind(): lax.ppermute(value, axis, [(source, source + steps) for source in range(l...  419 us
    ppermute x63, waiting for transfers between devices, from_behind(): lax.ppermute(value, axis, [(source, source + steps) for source in range(l...  174 us
    reduce_scatter x1, waiting for transfers between devices, per_device(): lax.psum_scatter(jnp.dot(hidden, out_weight, preferred_element_type=jnp.f...  99.8 us
    another operation x4, other arithmetic, group_parts(): jax.scipy.linalg.solve_triangular(system, right_side, lower=True, unit_di...  39.4 us
    while x126, local copies, waits for them, and re-layouts  22.9 us
    dot_general x64, matrix products, advance(): jnp.einsum('hvk,hkj->hvj', state_now, carry_mat, precision=HIGHEST)  17 us
  transfers between devices with their start and end apart: 64, of which 64 were waited for; matrix products, arithmetic and copies ran while one was open for 0% of the time, Pallas kernels for 0%

commit v1 on v0

v1 whole, which is shorter than its diff:
```python
import functools

import jax
import jax.numpy as jnp
from jax import lax
from jax.experimental import pallas as pl
from jax.experimental.pallas import tpu as pltpu
from jax.sharding import PartitionSpec as P

F32 = jnp.float32
HIGHEST = lax.Precision.HIGHEST
GROUP = 8


def dot(left, right, left_dim=1, right_dim=0):
    return lax.dot_general(
        left,
        right,
        (((left_dim,), (right_dim,)), ((), ())),
        precision=HIGHEST,
        preferred_element_type=F32,
    )


def unit_rows(rows):
    return rows * lax.rsqrt(jnp.sum(rows * rows, axis=-1, keepdims=True) + 1e-06)


def inverse_blocks(lower, row_ids, col_ids, start, stop):
    size = lower.shape[0]
    eye = jnp.where(row_ids == col_ids, 1.0, 0.0).astype(F32)
    base = jnp.where(row_ids // start == col_ids // start, lower, 0.0)
    square = dot(base, base)
    first = eye - base + square - dot(base, square)
    inverse = first + dot(first, dot(square, square))
    width = start
    while width < stop:
        below = (row_ids // (2 * width) == col_ids // (2 * width)) & (
            row_ids // width != col_ids // width
        )
        corner = jnp.where(below, lower, 0.0)
        inverse = inverse - dot(inverse, dot(corner, inverse))
        width *= 2
    return inverse


def local_kernel(heads, q_ref, k_ref, v_ref, beta_ref, decay_ref, decay_t_ref, msg_ref, own_ref, through_ref):
    tokens = q_ref.shape[0]
    rows = k_ref.shape[0]
    width = k_ref.shape[1] // heads
    row_ids = lax.broadcasted_iota(jnp.int32, (rows, rows), 0)
    col_ids = lax.broadcasted_iota(jnp.int32, (rows, rows), 1)
    tok_ids = lax.broadcasted_iota(jnp.int32, (tokens, rows), 0)
    tok_cols = lax.broadcasted_iota(jnp.int32, (tokens, rows), 1)
    row_tok = lax.broadcasted_iota(jnp.int32, (rows, tokens), 0) // 2
    up_to = jnp.where(row_tok >= lax.broadcasted_iota(jnp.int32, (rows, tokens), 1), 1.0, 0.0).astype(F32)
    tok_up_to = jnp.where(
        lax.broadcasted_iota(jnp.int32, (tokens, tokens), 0)
        >= lax.broadcasted_iota(jnp.int32, (tokens, tokens), 1),
        1.0,
        0.0,
    ).astype(F32)
    cumul_rows = dot(up_to, decay_ref[...])
    cumul_toks = dot(tok_up_to, decay_ref[...])
    cumul_line = dot(decay_t_ref[...], up_to, 1, 1)
    eye_k = jnp.where(
        lax.broadcasted_iota(jnp.int32, (width, width), 0)
        == lax.broadcasted_iota(jnp.int32, (width, width), 1),
        1.0,
        0.0,
    ).astype(F32)
    half = rows // 2
    quarter = width // (GROUP // heads)
    for head in range(heads):
        lanes = slice(head * width, (head + 1) * width)
        keys = unit_rows(k_ref[:, lanes].astype(F32))
        query = unit_rows(q_ref[:, lanes].astype(F32))
        beta = beta_ref[:, head : head + 1]
        cumul = cumul_rows[:, head : head + 1]
        line = cumul_line[head : head + 1, :]
        weight = jnp.exp(jnp.where(row_ids >= col_ids, cumul - line, -1e30))
        lower = jnp.where(row_ids > col_ids, beta * weight * dot(keys, keys, 1, 1), 0.0)
        inverse = inverse_blocks(lower, row_ids, col_ids, 8, half)
        right = jnp.concatenate([beta * v_ref[:, lanes].astype(F32), (beta * jnp.exp(cumul)) * keys], axis=1)
        upper = dot(inverse[:half, :half], right[:half])
        under = dot(inverse[half:, half:], right[half:] - dot(lower[half:, :half], upper))
        solved = jnp.concatenate([upper, under], axis=0)
        last = cumul[rows - 1 : rows, :]
        tail = jnp.exp(last - cumul) * keys
        pair = dot(solved, tail, 0, 0)
        write = pair[:width]
        carry = jnp.exp(last) * eye_k - pair[width:]
        for part in range(GROUP // heads):
            member = head * (GROUP // heads) + part
            msg_ref[member, :width, :] = carry
            msg_ref[member, width:, :] = write[part * quarter : (part + 1) * quarter]
        cumul_tok = cumul_toks[:, head : head + 1]
        scores = dot(query, keys, 1, 1) * jnp.exp(
            jnp.where(tok_ids >= tok_cols // 2, cumul_tok - line, -1e30)
        )
        mixed = dot(scores, solved)
        own_ref[:, lanes] = mixed[:, :width]
        through_ref[:, lanes] = jnp.exp(cumul_tok) * query - mixed[:, width:]


def compose(earlier, later, width):
    both = dot(earlier, later[:width])
    return jnp.concatenate([both[:width], both[width:] + later[width:]], axis=0)


def group_kernel(width, parts_ref, prefix_ref, total_ref):
    count = parts_ref.shape[0]
    runs = [parts_ref[i] for i in range(count)]
    step = 1
    while step < count:
        for start in range(step, count, 2 * step):
            for i in range(start, start + step):
                runs[i] = compose(runs[start - 1], runs[i], width)
        step *= 2
    for i in range(count - 1):
        prefix_ref[i] = runs[i]
    total_ref[...] = runs[count - 1]


def start_kernel(width, place_ref, totals_ref, prefix_ref, state_ref):
    place = place_ref[0]
    count = totals_ref.shape[0]
    state = jnp.zeros((totals_ref.shape[1] - width, width), F32)
    for i in range(count - 1):
        moved = dot(state, totals_ref[i, :width]) + totals_ref[i, width:]
        state = jnp.where(i < place, moved, state)
    state_ref[0] = state
    for i in range(prefix_ref.shape[0]):
        state_ref[i + 1] = dot(state, prefix_ref[i, :width]) + prefix_ref[i, width:]


def output_kernel(heads, own_ref, through_ref, state_ref, gain_ref, weight_ref, out_ref):
    width = own_ref.shape[1] // heads
    hidden = []
    for head in range(heads):
        lanes = slice(head * width, (head + 1) * width)
        outputs = own_ref[:, lanes] + dot(through_ref[:, lanes], state_ref[head], 1, 1)
        scale = lax.rsqrt(jnp.mean(outputs * outputs, axis=-1, keepdims=True) + 1e-05)
        hidden.append((outputs * scale * gain_ref[head : head + 1, :]).astype(jnp.bfloat16))
    hidden = jnp.concatenate(hidden, axis=1)
    out_ref[...] = jnp.dot(hidden, weight_ref[...], preferred_element_type=F32)


def per_device(queries, key_rows, value_rows, strengths, log_decay, norm_gain, out_weight):
    tokens, heads, width = queries.shape
    rows = 2 * tokens
    columns = out_weight.shape[1]
    groups = lax.axis_size("ctx") // GROUP
    spread = lax.axis_size("head")
    inner = [[g * GROUP + j for j in range(GROUP)] for g in range(groups)]
    outer = [[g * GROUP + j for g in range(groups)] for j in range(GROUP)]
    part_rows = width + width * heads // GROUP
    params = pltpu.CompilerParams(vmem_limit_bytes=48 * 1024 * 1024)

    decay_t = jnp.concatenate([log_decay.T, jnp.zeros((8 - heads, tokens), F32)], axis=0)
    msg, own, through = pl.pallas_call(
        functools.partial(local_kernel, heads),
        out_shape=(
            jax.ShapeDtypeStruct((GROUP, part_rows, width), F32),
            jax.ShapeDtypeStruct((tokens, heads * width), F32),
            jax.ShapeDtypeStruct((tokens, heads * width), F32),
        ),
        compiler_params=params,
        name="local_chunk",
    )(
        queries.reshape(tokens, heads * width),
        key_rows.reshape(rows, heads * width),
        value_rows.reshape(rows, heads * width),
        strengths.reshape(rows, heads),
        log_decay,
        decay_t,
    )
    parts = lax.all_to_all(msg, "ctx", 0, 0, axis_index_groups=inner)
    prefix, total = pl.pallas_call(
        functools.partial(group_kernel, width),
        out_shape=(
            jax.ShapeDtypeStruct((GROUP - 1, part_rows, width), F32),
            jax.ShapeDtypeStruct((part_rows, width), F32),
        ),
        compiler_params=params,
        name="group_scan",
    )(parts)
    totals = lax.all_gather(total, "ctx", axis_index_groups=outer)
    place = (lax.axis_index("ctx") // GROUP).astype(jnp.int32).reshape(1)
    starts = pl.pallas_call(
        functools.partial(start_kernel, width),
        out_shape=jax.ShapeDtypeStruct((GROUP, part_rows - width, width), F32),
        in_specs=[
            pl.BlockSpec(memory_space=pltpu.SMEM),
            pl.BlockSpec(memory_space=pltpu.VMEM),
            pl.BlockSpec(memory_space=pltpu.VMEM),
        ],
        compiler_params=params,
        name="start_states",
    )(place, totals, prefix)
    states = lax.all_to_all(starts, "ctx", 0, 0, axis_index_groups=inner)
    sums = pl.pallas_call(
        functools.partial(output_kernel, heads),
        out_shape=jax.ShapeDtypeStruct((tokens, columns), F32),
        compiler_params=params,
        name="project",
    )(own, through, states.reshape(heads, width, width), norm_gain, out_weight)
    shares = lax.all_to_all(sums.reshape(spread, tokens // spread, columns), "head", 0, 0)
    return jnp.sum(shares, axis=0).astype(jnp.bfloat16)


def solution(mesh):
    in_specs = (
        P("ctx", "head", None),
        P("ctx", None, "head", None),
        P("ctx", None, "head", None),
        P("ctx", None, "head"),
        P("ctx", "head"),
        P("head", None),
        P("head", None),
    )
    out_specs = P(("ctx", "head"), None)
    return jax.shard_map(
        per_device, mesh=mesh, in_specs=in_specs, out_specs=out_specs, check_vma=False
    )
```

time: 811 us -> 109 us (0.13)
  the two profiles are of different devices: /device:TPU:16 before, /device:TPU:1 now
where the time goes in v1:
time: 109 us; the launch traced here: 108 us
  blocking collectives  70.8 us (65%)
  Pallas kernels  20.3 us (19%)
  waiting for transfers between devices  7.66 us (7%)
  starting transfers between devices  6.37 us (6%)
  local copies, waits for them, and re-layouts  2.5 us (2%)
    all_gather x1, blocking collectives, per_device(): totals = lax.all_gather(total, 'ctx', axis_index_groups=outer)  32.7 us
    all_to_all x1, blocking collectives, per_device(): lax.all_to_all(sums.reshape(spread, tokens // spread, columns), 'head', 0...  27 us
    pallas_call x1, Pallas kernels, per_device(): pl.pallas_call(functools.partial(local_kernel, heads), out_shape=(jax.Sha...  16.7 us
    all_to_all x1, blocking collectives, per_device(): states = lax.all_to_all(starts, 'ctx', 0, 0, axis_index_groups=inner)  11 us
    all_to_all x1, waiting for transfers between devices, per_device(): parts = lax.all_to_all(msg, 'ctx', 0, 0, axis_index_groups=inner)  7.66 us
    all_to_all x1, starting transfers between devices, per_device(): parts = lax.all_to_all(msg, 'ctx', 0, 0, axis_index_groups=inner)  6.37 us
    unnamed x15, local copies, waits for them, and re-layouts  2.46 us
  transfers between devices with their start and end apart: 1, of which 1 were waited for; matrix products, arithmetic and copies ran while one was open for 0% of the time, Pallas kernels for 0%

profile of v1, /device:TPU:1, one launch (start us, length us, event | category | flops | bytes accessed | tf_op | source)
XLA Modules:
  0.0 108.4 jit_solution(17660649044947542283)
XLA Ops:
  0.0 0.0 copy-start.4
  0.0 0.0 copy-start.5
  0.0 0.0 copy-start.3
  0.0 0.9 copy.16
  0.9 0.0 copy-done.4
  0.9 0.0 copy-start.2
  0.9 0.1 copy.9.decay_ref
  1.0 0.0 copy-done.5
  1.0 0.2 copy.8
  1.2 0.0 copy-done.3
  1.2 0.6 copy-done.2
  1.9 16.7 %local_chunk.1 = (f32[8,160,128]{2,1,0:T(8,128)}, f32[128,256]{1,0:T(8,128)S(1)}, f32[128,256]{1,0:T(8,128)S(1)}) custom-call(bf16[128,256]{1,0:T(8,128)(2,1)S(1)} %bitcast.22, bf16[256,256]{1,0:T(8,128)(2,1)S(1)} %get-tuple-element.16.k_ref, bf16[256,256]{1,0:T(8,128)(2,1)S(1)} %get-tuple-element.15.v_ref, f32[256,2]{1,0:T(8,128)S(1)} %bitcast.21, ...), custom_call_target="tpu_custom_call" | custom-call | tf_op jit(solution)/shard_map/local_chunk/pallas_call | solution.py:161
  18.6 6.4 %all-to-all-start = ((f32[8,160,128]{2,1,0:T(8,128)}), f32[8,160,128]{2,1,0:T(8,128)S(1)}, u32[]{:S(2)}, u32[]{:S(2)}) async-start(f32[8,160,128]{2,1,0:T(8,128)} %get-tuple-element.12), calls=%async_computation | async-start | bytes 1310720 | tf_op jit(solution)/shard_map/all_to_all | solution.py:178
  24.9 7.7 %all-to-all-done.parts_ref = f32[8,160,128]{2,1,0:T(8,128)S(1)} async-done(((f32[8,160,128]{2,1,0:T(8,128)}), f32[8,160,128]{2,1,0:T(8,128)S(1)}, u32[]{:S(2)}, u32[]{:S(2)}) %all-to-all-start) | async-done | bytes 655392 | tf_op jit(solution)/shard_map/all_to_all | solution.py:178
  32.6 0.9 group_scan.1
  33.5 0.0 copy-start
  33.6 32.7 %all-gather = f32[1280,128]{1,0:T(8,128)S(1)} all-gather(f32[160,128]{1,0:T(8,128)S(1)} %get-tuple-element.13), channel_id=2, replica_groups={{0,64,128,192,256,320,384,448},{8,72,136,200,264,328,392,456},{16,80,14..., dimensions={0}, use_global_device_ids=true | all-gather | bytes 737280 | tf_op jit(solution)/shard_map/all_gather | solution.py:188
  66.3 2.0 %start_states.1 = f32[8,32,128]{2,1,0:T(8,128)S(1)} custom-call(s32[1]{0:T(128)} %bitcast.2.place_ref, f32[8,160,128]{2,1,0:T(8,128)S(1)} %bitcast.19, f32[7,160,128]{2,1,0:T(8,128)S(1)} %get-tuple-element.14.prefix_ref), custom_call_target="tpu_custom_call" | custom-call | tf_op jit(solution)/shard_map/start_states/pallas_call | solution.py:190
  68.2 11.0 %all_to_all.15 = f32[8,32,128]{2,1,0:T(8,128)S(1)} all-to-all(f32[8,32,128]{2,1,0:T(8,128)S(1)} %start_states.1), channel_id=1, replica_groups={{0,8,16,24,32,40,48,56},{64,72,80,88,96,104,112,120},{128,136,144,152,1..., dimensions={0} | all-to-all | bytes 262144 | tf_op jit(solution)/shard_map/all_to_all | solution.py:201
  79.3 0.0 copy-done
  79.3 0.7 copy-done.1
  79.9 0.7 project.1
  80.7 27.0 %all_to_all.16 = f32[8,16,2048]{2,1,0:T(8,128)S(1)} all-to-all(f32[8,16,2048]{2,1,0:T(8,128)S(1)} %bitcast.18), channel_id=1, replica_groups=mesh['ctx'=64,'head'=8] {'head'}, dimensions={0} | all-to-all | bytes 2097152 | tf_op jit(solution)/shard_map/all_to_all | solution.py:208
  107.7 0.7 reduce_sum.9
  (3 shorter events, 0.0 us)
Async XLA Ops:
  0.0 0.9 copy-start.4
  0.0 1.0 copy-start.5
  0.0 1.2 %copy-start.3 = (bf16[128,2,2,128]{3,2,1,0:T(2,128)(2,1)S(1)}, bf16[128,2,2,128]{3,2,1,0:T(2,128)(2,1)}, u32[]{:S(2)}) copy-start(bf16[128,2,2,128]{3,2,1,0:T(2,128)(2,1)} %param.8) | copy-start | bytes 393220
  0.9 0.9 copy-start.2
  18.6 14.0 %all-to-all-start = ((f32[8,160,128]{2,1,0:T(8,128)}), f32[8,160,128]{2,1,0:T(8,128)S(1)}, u32[]{:S(2)}, u32[]{:S(2)}) async-start(f32[8,160,128]{2,1,0:T(8,128)} %get-tuple-element.12), calls=%async_computation | async-start | bytes 1310720 | tf_op jit(solution)/shard_map/all_to_all | solution.py:178
  33.5 45.7 %copy-start = (bf16[256,2048]{1,0:T(8,128)(2,1)S(1)}, bf16[256,2048]{1,0:T(8,128)(2,1)}, u32[]{:S(2)}) copy-start(bf16[256,2048]{1,0:T(8,128)(2,1)} %weight_ref.1) | copy-start | bytes 3145732
  79.3 0.7 copy-start.1

commit v2 on v1

v2 whole, which is shorter than its diff:
```python
import functools

import jax
import jax.numpy as jnp
from jax import lax
from jax.experimental import pallas as pl
from jax.experimental.pallas import tpu as pltpu
from jax.sharding import PartitionSpec as P

F32 = jnp.float32
BF16 = jnp.bfloat16
GROUP = 8


def dims(left_dim, right_dim):
    return (((left_dim,), (right_dim,)), ((), ()))


def halves(value):
    high = value.astype(BF16)
    return high, (value - high.astype(F32)).astype(BF16)


def dot_halves(left, right, left_dim=1, right_dim=0):
    mul = functools.partial(
        lax.dot_general, dimension_numbers=dims(left_dim, right_dim), preferred_element_type=F32
    )
    return mul(left[0], right[0]) + (mul(left[0], right[1]) + mul(left[1], right[0]))


def dot(left, right, left_dim=1, right_dim=0):
    return dot_halves(halves(left), halves(right), left_dim, right_dim)


def unit_rows(rows):
    return rows * lax.rsqrt(jnp.sum(rows * rows, axis=-1, keepdims=True) + 1e-06)


def iota(shape, dim):
    return lax.broadcasted_iota(jnp.int32, shape, dim)


def cumulative(decay_ref, decay_t_ref, rows, tokens):
    up_to = jnp.where(iota((rows, tokens), 0) // 2 >= iota((rows, tokens), 1), 1.0, 0.0).astype(BF16)
    first, rest = halves(decay_ref[...])
    third = (decay_ref[...] - first.astype(F32) - rest.astype(F32)).astype(BF16)
    mul = functools.partial(lax.dot_general, preferred_element_type=F32)
    down = sum(mul(up_to, part, dimension_numbers=dims(1, 0)) for part in (third, rest, first))
    first_t, rest_t = halves(decay_t_ref[...])
    third_t = (decay_t_ref[...] - first_t.astype(F32) - rest_t.astype(F32)).astype(BF16)
    along = sum(mul(part, up_to, dimension_numbers=dims(1, 1)) for part in (third_t, rest_t, first_t))
    return down, along


def stack_rows(part, count):
    return jnp.concatenate([part] * count, axis=0)


def inverse_blocks(lowers, stop):
    size = lowers[0].shape[0]
    width = 8
    lane = iota((width, size), 1)
    row = iota((width, size), 0)
    col = lane % width
    packed = []
    for lower in lowers:
        part = jnp.zeros((width, size), F32)
        for block in range(size // width):
            part = jnp.where(lane // width == block, lower[block * width : (block + 1) * width], part)
        packed.append(part)
    same = iota((size, size), 0) // width == iota((size, size), 1) // width
    eye = jnp.where(row == col, 1.0, 0.0).astype(F32)
    inverses = [eye - jnp.where(row // 2 == col // 2, part, 0.0) for part in packed]
    for step in (2, 4):
        below = (row // (2 * step) == col // (2 * step)) & (row // step != col // step)
        corners = [jnp.where(below, part, 0.0) for part in packed]
        count = size // width
        inner = [dot(c, jnp.where(same, stack_rows(t, count), 0.0)) for c, t in zip(corners, inverses)]
        inverses = [
            t - dot(t, jnp.where(same, stack_rows(y, count), 0.0)) for t, y in zip(inverses, inner)
        ]
    while width < stop:
        count = size // width
        lane = iota((width, size), 1) // width
        even = lane % 2 == 0
        rows = iota((size, size), 0) // width
        cols = iota((size, size), 1) // width
        same = rows == cols
        below = (rows == cols + 1) & (cols % 2 == 0)
        corners = []
        for lower in lowers:
            part = jnp.zeros((width, size), F32)
            for block in range(0, count, 2):
                part = jnp.where(lane == block, lower[(block + 1) * width : (block + 2) * width], part)
            corners.append(part)
        inner = [dot(c, jnp.where(same, stack_rows(t, count), 0.0)) for c, t in zip(corners, inverses)]
        outer = [dot(t, jnp.where(below, stack_rows(y, count), 0.0)) for t, y in zip(inverses, inner)]
        inverses = [
            jnp.concatenate([jnp.where(even, t, 0.0), jnp.where(even, -e, t)], axis=0)
            for t, e in zip(inverses, outer)
        ]
        width *= 2
    return inverses


def local_kernel(heads, k_ref, v_ref, beta_ref, decay_ref, decay_t_ref, msg_ref, solved_ref):
    rows = k_ref.shape[0]
    width = k_ref.shape[1] // heads
    half = rows // 2
    quarter = width * heads // GROUP
    cumul_rows, cumul_line = cumulative(decay_ref, decay_t_ref, rows, rows // 2)
    row_ids = iota((rows, rows), 0)
    col_ids = iota((rows, rows), 1)
    eye_k = jnp.where(iota((width, width), 0) == iota((width, width), 1), 1.0, 0.0).astype(F32)
    keys, lowers = [], []
    for head in range(heads):
        unit = unit_rows(k_ref[:, head * width : (head + 1) * width].astype(F32))
        cumul = cumul_rows[:, head : head + 1]
        line = cumul_line[head : head + 1, :]
        weight = jnp.exp(jnp.where(row_ids > col_ids, cumul - line, -1e30))
        parts = halves(unit)
        lowers.append(beta_ref[:, head : head + 1] * weight * dot_halves(parts, parts, 1, 1))
        keys.append(unit)
    inverses = inverse_blocks(lowers, half)
    rights = []
    for head in range(heads):
        beta = beta_ref[:, head : head + 1]
        value = v_ref[:, head * width : (head + 1) * width].astype(F32)
        pull = beta * jnp.exp(cumul_rows[:, head : head + 1])
        rights.append(jnp.concatenate([beta * value, pull * keys[head]], axis=1))
    uppers = [dot(inverse[:, :half], right[:half]) for inverse, right in zip(inverses, rights)]
    moved = [
        right[half:] - dot(lower[half:, :half], upper)
        for lower, right, upper in zip(lowers, rights, uppers)
    ]
    unders = [dot(inverse[:, half:], rest) for inverse, rest in zip(inverses, moved)]
    for head in range(heads):
        solved = jnp.concatenate([uppers[head], unders[head]], axis=0)
        solved_ref[head] = solved
        cumul = cumul_rows[:, head : head + 1]
        last = cumul[rows - 1 : rows, :]
        tail = jnp.exp(last - cumul) * keys[head]
        pair = dot(solved, tail, 0, 0)
        carry = jnp.exp(last) * eye_k - pair[width:]
        for part in range(GROUP // heads):
            member = head * (GROUP // heads) + part
            msg_ref[member, :width, :] = carry
            msg_ref[member, width:, :] = pair[part * quarter : (part + 1) * quarter]


def own_kernel(heads, q_ref, k_ref, decay_ref, decay_t_ref, solved_ref, own_ref, through_ref):
    tokens = q_ref.shape[0]
    rows = k_ref.shape[0]
    width = k_ref.shape[1] // heads
    cumul_rows, cumul_line = cumulative(decay_ref, decay_t_ref, rows, tokens)
    up_to = jnp.where(iota((tokens, tokens), 0) >= iota((tokens, tokens), 1), 1.0, 0.0).astype(BF16)
    first, rest = halves(decay_ref[...])
    third = (decay_ref[...] - first.astype(F32) - rest.astype(F32)).astype(BF16)
    cumul_toks = sum(jnp.dot(up_to, part, preferred_element_type=F32) for part in (third, rest, first))
    reached = iota((tokens, rows), 0) >= iota((tokens, rows), 1) // 2
    for head in range(heads):
        lanes = slice(head * width, (head + 1) * width)
        keys = unit_rows(k_ref[:, lanes].astype(F32))
        query = unit_rows(q_ref[:, lanes].astype(F32))
        cumul = cumul_toks[:, head : head + 1]
        weight = jnp.exp(jnp.where(reached, cumul - cumul_line[head : head + 1, :], -1e30))
        mixed = dot(dot(query, keys, 1, 1) * weight, solved_ref[head])
        own_ref[:, lanes] = mixed[:, :width]
        through_ref[:, lanes] = jnp.exp(cumul) * query - mixed[:, width:]


def compose(earlier, later, width):
    both = dot(earlier, later[:width])
    return jnp.concatenate([both[:width], both[width:] + later[width:]], axis=0)


def group_kernel(width, parts_ref, prefix_ref, total_ref):
    count = parts_ref.shape[0]
    runs = [parts_ref[i] for i in range(count)]
    step = 1
    while step < count:
        for start in range(step, count, 2 * step):
            for i in range(start, start + step):
                runs[i] = compose(runs[start - 1], runs[i], width)
        step *= 2
    for i in range(count - 1):
        prefix_ref[i] = runs[i]
    total_ref[...] = runs[count - 1]


def pair_kernel(width, pair_ref, total_ref):
    total_ref[...] = compose(pair_ref[0], pair_ref[1], width)


def write_kernel(width, pair_ref, write_ref):
    write_ref[...] = dot(pair_ref[0, width:], pair_ref[1, :width]) + pair_ref[1, width:]


def start_kernel(width, place_ref, pair_ref, quad_ref, far_ref, prefix_ref, state_ref):
    place = place_ref[0]
    state = jnp.where(place >= 4, far_ref[0], 0.0)
    moved = dot(state, quad_ref[0, :width]) + quad_ref[0, width:]
    state = jnp.where((place // 2) % 2 == 1, moved, state)
    moved = dot(state, pair_ref[0, :width]) + pair_ref[0, width:]
    state = jnp.where(place % 2 == 1, moved, state)
    state_ref[0] = state
    parts = halves(state)
    for i in range(prefix_ref.shape[0]):
        state_ref[i + 1] = dot_halves(parts, halves(prefix_ref[i, :width])) + prefix_ref[i, width:]


def output_kernel(heads, spread, core_ref, own_ref, through_ref, state_ref, gain_ref, weight_ref, send_ref, keep_ref):
    width = own_ref.shape[1] // heads
    tokens = own_ref.shape[0]
    hidden = []
    for head in range(heads):
        lanes = slice(head * width, (head + 1) * width)
        outputs = own_ref[:, lanes] + dot(through_ref[:, lanes], state_ref[head], 1, 1)
        scale = lax.rsqrt(jnp.mean(outputs * outputs, axis=-1, keepdims=True) + 1e-05)
        hidden.append(outputs * scale * gain_ref[head : head + 1, :])
    hidden = jnp.concatenate(hidden, axis=1)
    share = tokens // spread
    first = jnp.concatenate([hidden[i * share : (i + 1) * share] for i in range(0, spread, 2)], axis=0)
    second = jnp.concatenate([hidden[i * share : (i + 1) * share] for i in range(1, spread, 2)], axis=0)
    on_first = core_ref[0] == 0
    keep_ref[...] = jnp.where(on_first, first, second).astype(BF16)
    send = jnp.where(on_first, second, first).astype(BF16)
    send_ref[...] = jnp.dot(send, weight_ref[...], preferred_element_type=F32)


def keep_kernel(keep_ref, weight_ref, out_ref):
    out_ref[...] = jnp.dot(keep_ref[...], weight_ref[...], preferred_element_type=F32)


def add_kernel(left_ref, right_ref, out_ref):
    out_ref[...] = left_ref[...] + right_ref[...]


def per_device(queries, key_rows, value_rows, strengths, log_decay, norm_gain, out_weight):
    tokens, heads, width = queries.shape
    rows = 2 * tokens
    columns = out_weight.shape[1]
    ctx = lax.axis_size("ctx")
    spread = lax.axis_size("head")
    part_rows = width + width * heads // GROUP
    params = pltpu.CompilerParams(vmem_limit_bytes=48 * 1024 * 1024)

    def call(body, out_shape, name, flops=0, in_specs=None):
        extra = {} if in_specs is None else dict(in_specs=in_specs)
        return pl.pallas_call(
            body,
            out_shape=out_shape,
            compiler_params=params,
            name=name,
            cost_estimate=pl.CostEstimate(flops=flops, bytes_accessed=1 << 20, transcendentals=0),
            **extra,
        )

    def array(*shape):
        return jax.ShapeDtypeStruct(shape, F32)

    def pairs(flip):
        return [[i, i ^ flip] for i in range(ctx) if i < i ^ flip]

    smem = pl.BlockSpec(memory_space=pltpu.SMEM)
    vmem = pl.BlockSpec(memory_space=pltpu.VMEM)
    inner = [[g * GROUP + j for j in range(GROUP)] for g in range(ctx // GROUP)]

    query = queries.reshape(tokens, heads * width)
    keys = key_rows.reshape(rows, heads * width)
    decay_t = jnp.concatenate([log_decay.T, jnp.zeros((8 - heads, tokens), F32)], axis=0)
    msg, solved = call(
        functools.partial(local_kernel, heads),
        (array(GROUP, part_rows, width), array(heads, rows, 2 * width)),
        "local_chunk",
    )(
        keys,
        value_rows.reshape(rows, heads * width),
        strengths.reshape(rows, heads),
        log_decay,
        decay_t,
    )
    parts = lax.all_to_all(msg, "ctx", 0, 0, axis_index_groups=inner)
    own, through = call(
        functools.partial(own_kernel, heads),
        (array(tokens, heads * width), array(tokens, heads * width)),
        "own_outputs",
        flops=4 * 10**9,
    )(query, keys, log_decay, decay_t, solved)
    prefix, total = call(
        functools.partial(group_kernel, width),
        (array(GROUP - 1, part_rows, width), array(part_rows, width)),
        "group_scan",
    )(parts)
    pair = lax.all_gather(total, "ctx", axis_index_groups=pairs(8))
    total = call(functools.partial(pair_kernel, width), array(part_rows, width), "pair_total")(pair)
    quad = lax.all_gather(total, "ctx", axis_index_groups=pairs(16))
    write = call(
        functools.partial(write_kernel, width), array(part_rows - width, width), "half_write"
    )(quad)
    far = lax.all_gather(write, "ctx", axis_index_groups=pairs(48))
    place = (lax.axis_index("ctx") // GROUP).astype(jnp.int32).reshape(1)
    starts = call(
        functools.partial(start_kernel, width),
        array(GROUP, part_rows - width, width),
        "start_states",
        in_specs=[smem, vmem, vmem, vmem, vmem],
    )(place, pair, quad, far, prefix)
    states = lax.all_to_all(starts, "ctx", 0, 0, axis_index_groups=inner)
    core = (lax.axis_index("head") % 2).astype(jnp.int32).reshape(1)
    send, keep = call(
        functools.partial(output_kernel, heads, spread),
        (array(tokens // 2, columns), jax.ShapeDtypeStruct((tokens // 2, heads * width), BF16)),
        "project_send",
        in_specs=[smem, vmem, vmem, vmem, vmem, vmem],
    )(core, own, through, states.reshape(heads, width, width), norm_gain, out_weight)
    arrived = lax.ppermute(send, "head", [(i, i ^ 1) for i in range(spread)])
    kept = call(keep_kernel, array(tokens // 2, columns), "project_keep", flops=10**8)(keep, out_weight)
    sums = call(add_kernel, array(tokens // 2, columns), "add_cores")(kept, arrived)
    ring = [[i * 2 + c for i in range(spread // 2)] for c in range(2)]
    shares = lax.all_to_all(
        sums.reshape(spread // 2, tokens // spread, columns), "head", 0, 0, axis_index_groups=ring
    )
    return jnp.sum(shares, axis=0).astype(BF16)


def solution(mesh):
    in_specs = (
        P("ctx", "head", None),
        P("ctx", None, "head", None),
        P("ctx", None, "head", None),
        P("ctx", None, "head"),
        P("ctx", "head"),
        P("head", None),
        P("head", None),
    )
    out_specs = P(("ctx", "head"), None)
    return jax.shard_map(
        per_device, mesh=mesh, in_specs=in_specs, out_specs=out_specs, check_vma=False
    )
```

time: 109 us -> 86 us (0.79)
  blocking collectives: 70.8 us -> 37.9 us
  starting transfers between devices: 6.37 us -> 20.9 us
  Pallas kernels: 20.3 us -> 9.14 us
  waiting for transfers between devices: 7.66 us -> 13.6 us
    all_to_all x2 -> x1, blocking collectives: 38 us -> 12.4 us  [per_device(): lax.all_to_all(sums.reshape(spread // 2, tokens // spread, columns), 'hea...]
    pallas_call x4 -> x9, Pallas kernels: 20.3 us -> 9.14 us  [the longest x1 5.29 us: per_device(): call(functools.partial(local_kernel, heads), (array(GROUP, part_rows, wid...]
    ppermute x0 -> x1, starting transfers between devices: none -> 8.25 us  [per_device(): arrived = lax.ppermute(send, 'head', [(i, i ^ 1) for i in range(spread)])]
    all_gather x1 -> x3, blocking collectives: 32.7 us -> 25.4 us  [the longest x1 9.39 us: per_device(): quad = lax.all_gather(total, 'ctx', axis_index_groups=pairs(16))]
    all_to_all x0 -> x1, starting transfers between devices: none -> 6.24 us  [per_device(): states = lax.all_to_all(starts, 'ctx', 0, 0, axis_index_groups=inner)]
    all_to_all x0 -> x1, waiting for transfers between devices: none -> 4.72 us  [per_device(): states = lax.all_to_all(starts, 'ctx', 0, 0, axis_index_groups=inner)]
    ppermute x0 -> x1, waiting for transfers between devices: none -> 1.22 us  [per_device(): arrived = lax.ppermute(send, 'head', [(i, i ^ 1) for i in range(spread)])]
  transfers between devices with their start and end apart: 1 -> 3, of which waited for: 1 -> 3; matrix products, arithmetic and copies ran while one was open for 0% -> 0% of each run, Pallas kernels for 0% -> 1%
where the time goes in v2:
time: 86 us; the launch traced here: 85.5 us
  blocking collectives  37.9 us (44%)
  starting transfers between devices  20.9 us (24%)
  waiting for transfers between devices  13.6 us (16%)
  Pallas kernels  9.14 us (11%)
  local copies, waits for them, and re-layouts  3.3 us (4%)
    all_to_all x1, blocking collectives, per_device(): lax.all_to_all(sums.reshape(spread // 2, tokens // spread, columns), 'hea...  12.4 us
    all_gather x1, blocking collectives, per_device(): quad = lax.all_gather(total, 'ctx', axis_index_groups=pairs(16))  9.39 us
    all_gather x1, blocking collectives, per_device(): far = lax.all_gather(write, 'ctx', axis_index_groups=pairs(48))  9.33 us
    ppermute x1, starting transfers between devices, per_device(): arrived = lax.ppermute(send, 'head', [(i, i ^ 1) for i in range(spread)])  8.25 us
    all_to_all x1, waiting for transfers between devices, per_device(): parts = lax.all_to_all(msg, 'ctx', 0, 0, axis_index_groups=inner)  7.66 us
    all_gather x1, blocking collectives, per_device(): pair = lax.all_gather(total, 'ctx', axis_index_groups=pairs(8))  6.72 us
    all_to_all x1, starting transfers between devices, per_device(): parts = lax.all_to_all(msg, 'ctx', 0, 0, axis_index_groups=inner)  6.38 us
    all_to_all x1, starting transfers between devices, per_device(): states = lax.all_to_all(starts, 'ctx', 0, 0, axis_index_groups=inner)  6.24 us
  transfers between devices with their start and end apart: 3, of which 3 were waited for; matrix products, arithmetic and copies ran while one was open for 0% of the time, Pallas kernels for 1%

profile of v2, /device:TPU:1, one launch (start us, length us, event | category | flops | bytes accessed | tf_op | source)
XLA Modules:
  0.0 85.5 jit_solution(2508630711287986346)
XLA Ops:
  0.0 0.8 copy.10.decay_ref
  0.8 0.2 copy.8
  1.0 0.7 copy-done.4
  1.7 0.9 %copy_bitcast_fusion = (bf16[256,256]{1,0:T(8,128)(2,1)S(1)}, bf16[256,256]{1,0:T(8,128)(2,1)S(1)}) fusion(bf16[32,8,2,128]{3,2,1,0:T(2,128)(2,1)S(1)} %bitcast.30, bf16[32,8,2,128]{3,2,1,0:T(2,128)(2,1)} %bitcast.31), kind=kLoop, calls=%fused_computation | loop fusion | bytes 524288 | tf_op jit(solution)/shard_map/reshape | solution.py:278
  2.6 5.3 %local_chunk.1 = (f32[8,160,128]{2,1,0:T(8,128)}, f32[2,256,256]{2,1,0:T(8,128)S(1)}) custom-call(bf16[256,256]{1,0:T(8,128)(2,1)S(1)} %get-tuple-element.22.k_ref, bf16[256,256]{1,0:T(8,128)(2,1)S(1)} %get-tuple-element.21.v_ref, f32[256,2]{1,0:T(8,128)S(1)} %bitcast.27, f32[128,2]{1,0:T(8,128)S(1)} %copy.10.decay_ref, f32[8,128]{1,0:T(8,128)S(1)} %concatenate.3.decay_t_ref), custom_call_target="tpu_custom_call" | custom-call | bytes 1048576 | tf_op jit(solution)/shard_map/local_chunk/pallas_call | solution.py:272
  7.9 6.4 %all-to-all-start = ((f32[8,160,128]{2,1,0:T(8,128)}), f32[8,160,128]{2,1,0:T(8,128)S(1)}, u32[]{:S(2)}, u32[]{:S(2)}) async-start(f32[8,160,128]{2,1,0:T(8,128)} %get-tuple-element.16), calls=%async_computation | async-start | bytes 1310720 | tf_op jit(solution)/shard_map/all_to_all | solution.py:283
  14.3 7.7 %all-to-all-done.parts_ref = f32[8,160,128]{2,1,0:T(8,128)S(1)} async-done(((f32[8,160,128]{2,1,0:T(8,128)}), f32[8,160,128]{2,1,0:T(8,128)S(1)}, u32[]{:S(2)}, u32[]{:S(2)}) %all-to-all-start) | async-done | bytes 655392 | tf_op jit(solution)/shard_map/all_to_all | solution.py:283
  21.9 0.7 group_scan.1
  22.6 6.7 %all-gather = f32[320,128]{1,0:T(8,128)S(1)} all-gather(f32[160,128]{1,0:T(8,128)S(1)} %get-tuple-element.17), channel_id=2, replica_groups={{0,64},{8,72},{16,80},{24,88},{32,96},{40,104},{48,112},{56,120},{128,1..., dimensions={0}, use_global_device_ids=true | all-gather | bytes 245760 | tf_op jit(solution)/shard_map/all_gather | solution.py:295
  29.3 0.2 pair_total.1
  29.5 9.4 %all-gather.1 = f32[320,128]{1,0:T(8,128)S(1)} all-gather(f32[160,128]{1,0:T(8,128)S(1)} %pair_total.1), channel_id=3, replica_groups={{0,128},{8,136},{16,144},{24,152},{32,160},{40,168},{48,176},{56,184},{..., dimensions={0}, use_global_device_ids=true | all-gather | bytes 245760 | tf_op jit(solution)/shard_map/all_gather | solution.py:297
  38.9 0.1 half_write.1
  39.0 9.3 %all-gather.2 = f32[64,128]{1,0:T(8,128)S(1)} all-gather(f32[32,128]{1,0:T(8,128)S(1)} %half_write.1), channel_id=4, replica_groups={{0,384},{8,392},{16,400},{24,408},{32,416},{40,424},{48,432},{56,440},{..., dimensions={0}, use_global_device_ids=true | all-gather | bytes 49152 | tf_op jit(solution)/shard_map/all_gather | solution.py:301
  48.4 1.3 %start_states.1 = f32[8,32,128]{2,1,0:T(8,128)} custom-call(s32[1]{0:T(128)} %bitcast.3.place_ref, f32[2,160,128]{2,1,0:T(8,128)S(1)} %bitcast.25, f32[2,160,128]{2,1,0:T(8,128)S(1)} %bitcast.23, f32[2,32,128]{2,1,0:T(8,128)S(1)} %bitcast.28, f32[7,160,128]{2,1,0:T(8,128)S(1)} %get-tuple-element.18.prefix_ref), custom_call_target="tpu_custom_call" | custom-call | bytes 1048576 | tf_op jit(solution)/shard_map/start_states/pallas_call | solution.py:303
  49.6 6.2 %all-to-all-start.1 = ((f32[8,32,128]{2,1,0:T(8,128)}), f32[8,32,128]{2,1,0:T(8,128)S(1)}, u32[]{:S(2)}, u32[]{:S(2)}) async-start(f32[8,32,128]{2,1,0:T(8,128)} %start_states.1), calls=%async_computation.1 | async-start | bytes 262144 | tf_op jit(solution)/shard_map/all_to_all | solution.py:309
  55.9 0.7 own_outputs.1
  56.6 4.7 %all-to-all-done.1 = f32[8,32,128]{2,1,0:T(8,128)S(1)} async-done(((f32[8,32,128]{2,1,0:T(8,128)}), f32[8,32,128]{2,1,0:T(8,128)S(1)}, u32[]{:S(2)}, u32[]{:S(2)}) %all-to-all-start.1) | async-done | bytes 131104 | tf_op jit(solution)/shard_map/all_to_all | solution.py:309
  61.3 0.7 copy-done.1
  62.0 0.6 project_send.1
  62.6 8.2 %collective-permute-start = (f32[64,2048]{1,0:T(8,128)S(1)}, f32[64,2048]{1,0:T(8,128)S(1)}, u32[]{:S(2)}, u32[]{:S(2)}) collective-permute-start(f32[64,2048]{1,0:T(8,128)S(1)} %get-tuple-element.20), channel_id=1, source_target_pairs={{0,1},{1,0},{2,3},{3,2},{4,5},{5,4},{6,7},{7,6},{8,9},{9,8},{10,11... | collective-permute-start | bytes 1572872 | tf_op jit(solution)/shard_map/ppermute | solution.py:317
  70.9 0.3 project_keep.1.left_ref
  71.2 1.2 %collective-permute-done.right_ref = f32[64,2048]{1,0:T(8,128)S(1)} collective-permute-done((f32[64,2048]{1,0:T(8,128)S(1)}, f32[64,2048]{1,0:T(8,128)S(1)}, u32[]{:S(2)}, u32[]{:S(2)}) %collective-permute-start) | collective-permute-done | bytes 524320 | tf_op jit(solution)/shard_map/ppermute | solution.py:317
  72.4 12.4 %all_to_all.15 = f32[4,16,2048]{2,1,0:T(8,128)S(1)} all-to-all(f32[4,16,2048]{2,1,0:T(8,128)S(1)} %bitcast.21), channel_id=1, replica_groups={{0,2,4,6},{1,3,5,7},{8,10,12,14},{9,11,13,15},{16,18,20,22},{17,19,21,2..., dimensions={0} | all-to-all | bytes 1048576 | tf_op jit(solution)/shard_map/all_to_all | solution.py:321
  84.9 0.7 reduce_sum.9
  (13 shorter events, 0.1 us)
Async XLA Ops:
  0.0 0.8 copy-start.5
  0.0 1.7 %copy-start.2 = (bf16[128,2,2,128]{3,2,1,0:T(2,128)(2,1)S(1)}, bf16[128,2,2,128]{3,2,1,0:T(2,128)(2,1)}, u32[]{:S(2)}) copy-start(bf16[128,2,2,128]{3,2,1,0:T(2,128)(2,1)} %param.9) | copy-start | bytes 393220
  1.0 0.7 copy-start.4
  7.9 14.0 %all-to-all-start = ((f32[8,160,128]{2,1,0:T(8,128)}), f32[8,160,128]{2,1,0:T(8,128)S(1)}, u32[]{:S(2)}, u32[]{:S(2)}) async-start(f32[8,160,128]{2,1,0:T(8,128)} %get-tuple-element.16), calls=%async_computation | async-start | bytes 1310720 | tf_op jit(solution)/shard_map/all_to_all | solution.py:283
  49.6 6.2 %copy-start.3 = (bf16[128,2,128]{2,1,0:T(2,128)(2,1)S(1)}, bf16[128,2,128]{2,1,0:T(2,128)(2,1)}, u32[]{:S(2)}) copy-start(bf16[128,2,128]{2,1,0:T(2,128)(2,1)} %param.7) | copy-start | bytes 196612
  49.6 11.7 %all-to-all-start.1 = ((f32[8,32,128]{2,1,0:T(8,128)}), f32[8,32,128]{2,1,0:T(8,128)S(1)}, u32[]{:S(2)}, u32[]{:S(2)}) async-start(f32[8,32,128]{2,1,0:T(8,128)} %start_states.1), calls=%async_computation.1 | async-start | bytes 262144 | tf_op jit(solution)/shard_map/all_to_all | solution.py:309
  55.9 5.4 %copy-start = (bf16[256,2048]{1,0:T(8,128)(2,1)S(1)}, bf16[256,2048]{1,0:T(8,128)(2,1)}, u32[]{:S(2)}) copy-start(bf16[256,2048]{1,0:T(8,128)(2,1)} %weight_ref.3) | copy-start | bytes 3145732
  61.3 0.7 copy-start.1
  62.6 9.8 %collective-permute-start = (f32[64,2048]{1,0:T(8,128)S(1)}, f32[64,2048]{1,0:T(8,128)S(1)}, u32[]{:S(2)}, u32[]{:S(2)}) collective-permute-start(f32[64,2048]{1,0:T(8,128)S(1)} %get-tuple-element.20), channel_id=1, source_target_pairs={{0,1},{1,0},{2,3},{3,2},{4,5},{5,4},{6,7},{7,6},{8,9},{9,8},{10,11... | collective-permute-start | bytes 1572872 | tf_op jit(solution)/shard_map/ppermute | solution.py:317

commit v3 on v2

--- a/solution.py
+++ b/solution.py
@@ -40,16 +40,24 @@
     return lax.broadcasted_iota(jnp.int32, shape, dim)
 
 
-def cumulative(decay_ref, decay_t_ref, rows, tokens):
-    up_to = jnp.where(iota((rows, tokens), 0) // 2 >= iota((rows, tokens), 1), 1.0, 0.0).astype(BF16)
-    first, rest = halves(decay_ref[...])
-    third = (decay_ref[...] - first.astype(F32) - rest.astype(F32)).astype(BF16)
-    mul = functools.partial(lax.dot_general, preferred_element_type=F32)
-    down = sum(mul(up_to, part, dimension_numbers=dims(1, 0)) for part in (third, rest, first))
-    first_t, rest_t = halves(decay_t_ref[...])
-    third_t = (decay_t_ref[...] - first_t.astype(F32) - rest_t.astype(F32)).astype(BF16)
-    along = sum(mul(part, up_to, dimension_numbers=dims(1, 1)) for part in (third_t, rest_t, first_t))
-    return down, along
+def thirds(value):
+    high, rest = halves(value)
+    last = (value - high.astype(F32) - rest.astype(F32)).astype(BF16)
+    return jnp.concatenate([last.astype(F32), rest.astype(F32), high.astype(F32)], axis=0).astype(BF16)
+
+
+def picked(mask, small):
+    wide = lax.dot_general(
+        jnp.where(mask, 1.0, 0.0).astype(BF16), small, dims(1, 1), preferred_element_type=F32
+    )
+    return wide[:, :8] + wide[:, 8:16] + wide[:, 16:24]
+
+
+def picked_line(small, mask):
+    wide = lax.dot_general(
+        small, jnp.where(mask, 1.0, 0.0).astype(BF16), dims(1, 1), preferred_element_type=F32
+    )
+    return wide[:8] + wide[8:16] + wide[16:24]
 
 
 def stack_rows(part, count):
@@ -103,31 +111,44 @@
     return inverses
 
 
-def local_kernel(heads, k_ref, v_ref, beta_ref, decay_ref, decay_t_ref, msg_ref, solved_ref):
-    rows = k_ref.shape[0]
-    width = k_ref.shape[1] // heads
+def local_kernel(heads, k_ref, v_ref, small_ref, msg_ref, solved_ref, keys_ref, spread_k, spread_v):
+    rows = k_ref.shape[0] // heads
+    tokens = rows // 2
+    width = k_ref.shape[1]
     half = rows // 2
     quarter = width * heads // GROUP
-    cumul_rows, cumul_line = cumulative(decay_ref, decay_t_ref, rows, rows // 2)
+    spread_k[...] = unit_rows(k_ref[...].astype(F32))
+    spread_v[...] = v_ref[...].astype(F32)
+    small = thirds(small_ref[...])
+    row_tok = iota((rows, tokens), 0) // 2
+    tok = iota((rows, tokens), 1)
+    cumul_rows = picked(row_tok >= tok, small)
+    cumul_line = picked_line(small, row_tok >= tok)
+    betas = picked(row_tok == tok, small)
+    first = iota((rows, 1), 0) % 2 == 0
     row_ids = iota((rows, rows), 0)
     col_ids = iota((rows, rows), 1)
     eye_k = jnp.where(iota((width, width), 0) == iota((width, width), 1), 1.0, 0.0).astype(F32)
-    keys, lowers = [], []
+    keys, lowers, strength, values = [], [], [], []
     for head in range(heads):
-        unit = unit_rows(k_ref[:, head * width : (head + 1) * width].astype(F32))
+        unit = spread_k[pl.ds(head, rows, stride=heads), :]
+        values.append(spread_v[pl.ds(head, rows, stride=heads), :])
+        beta = jnp.where(
+            first, betas[:, heads + head : heads + head + 1], betas[:, 2 * heads + head : 2 * heads + head + 1]
+        )
         cumul = cumul_rows[:, head : head + 1]
         line = cumul_line[head : head + 1, :]
         weight = jnp.exp(jnp.where(row_ids > col_ids, cumul - line, -1e30))
         parts = halves(unit)
-        lowers.append(beta_ref[:, head : head + 1] * weight * dot_halves(parts, parts, 1, 1))
+        lowers.append(beta * weight * dot_halves(parts, parts, 1, 1))
         keys.append(unit)
+        strength.append(beta)
+        keys_ref[head] = unit
     inverses = inverse_blocks(lowers, half)
-    rights = []
-    for head in range(heads):
-        beta = beta_ref[:, head : head + 1]
-        value = v_ref[:, head * width : (head + 1) * width].astype(F32)
-        pull = beta * jnp.exp(cumul_rows[:, head : head + 1])
-        rights.append(jnp.concatenate([beta * value, pull * keys[head]], axis=1))
+    rights = [
+        jnp.concatenate([beta * value, (beta * jnp.exp(cumul_rows[:, head : head + 1])) * unit], axis=1)
+        for head, (beta, value, unit) in enumerate(zip(strength, values, keys))
+    ]
     uppers = [dot(inverse[:, :half], right[:half]) for inverse, right in zip(inverses, rights)]
     moved = [
         right[half:] - dot(lower[half:, :half], upper)
@@ -148,25 +169,44 @@
             msg_ref[member, width:, :] = pair[part * quarter : (part + 1) * quarter]
 
 
-def own_kernel(heads, q_ref, k_ref, decay_ref, decay_t_ref, solved_ref, own_ref, through_ref):
-    tokens = q_ref.shape[0]
-    rows = k_ref.shape[0]
-    width = k_ref.shape[1] // heads
-    cumul_rows, cumul_line = cumulative(decay_ref, decay_t_ref, rows, tokens)
-    up_to = jnp.where(iota((tokens, tokens), 0) >= iota((tokens, tokens), 1), 1.0, 0.0).astype(BF16)
-    first, rest = halves(decay_ref[...])
-    third = (decay_ref[...] - first.astype(F32) - rest.astype(F32)).astype(BF16)
-    cumul_toks = sum(jnp.dot(up_to, part, preferred_element_type=F32) for part in (third, rest, first))
+def own_kernel(heads, q_ref, keys_ref, small_ref, solved_ref, own_ref, through_ref, spread_q):
+    tokens = q_ref.shape[0] // heads
+    rows = keys_ref.shape[1]
+    spread_q[...] = unit_rows(q_ref[...].astype(F32))
+    small = thirds(small_ref[...])
+    reached = iota((rows, tokens), 0) // 2 >= iota((rows, tokens), 1)
+    cumul_line = picked_line(small, reached)
+    cumul_toks = picked(iota((tokens, tokens), 0) >= iota((tokens, tokens), 1), small)
     reached = iota((tokens, rows), 0) >= iota((tokens, rows), 1) // 2
+    width = keys_ref.shape[2]
     for head in range(heads):
         lanes = slice(head * width, (head + 1) * width)
-        keys = unit_rows(k_ref[:, lanes].astype(F32))
-        query = unit_rows(q_ref[:, lanes].astype(F32))
+        query = spread_q[pl.ds(head, tokens, stride=heads), :]
         cumul = cumul_toks[:, head : head + 1]
         weight = jnp.exp(jnp.where(reached, cumul - cumul_line[head : head + 1, :], -1e30))
-        mixed = dot(dot(query, keys, 1, 1) * weight, solved_ref[head])
+        mixed = dot(dot(query, keys_ref[head], 1, 1) * weight, solved_ref[head])
         own_ref[:, lanes] = mixed[:, :width]
         through_ref[:, lanes] = jnp.exp(cumul) * query - mixed[:, width:]
+
+
+def widen_kernel(in_ref, out_ref):
+    out_ref[...] = in_ref[...].astype(F32)
+
+
+def weight_kernel(core_ref, own_ref, other_ref, both_ref):
+    rows = own_ref.shape[0]
+    other = other_ref[...].astype(BF16)
+    on_first = core_ref[0] == 0
+
+    @pl.when(on_first)
+    def _():
+        both_ref[:rows] = own_ref[...]
+        both_ref[rows:] = other
+
+    @pl.when(jnp.logical_not(on_first))
+    def _():
+        both_ref[:rows] = other
+        both_ref[rows:] = own_ref[...]
 
 
 def compose(earlier, later, width):
@@ -209,31 +249,25 @@
         state_ref[i + 1] = dot_halves(parts, halves(prefix_ref[i, :width])) + prefix_ref[i, width:]
 
 
-def output_kernel(heads, spread, core_ref, own_ref, through_ref, state_ref, gain_ref, weight_ref, send_ref, keep_ref):
+def hidden_kernel(heads, own_ref, through_ref, state_ref, gain_ref, hidden_ref):
     width = own_ref.shape[1] // heads
-    tokens = own_ref.shape[0]
-    hidden = []
     for head in range(heads):
         lanes = slice(head * width, (head + 1) * width)
         outputs = own_ref[:, lanes] + dot(through_ref[:, lanes], state_ref[head], 1, 1)
         scale = lax.rsqrt(jnp.mean(outputs * outputs, axis=-1, keepdims=True) + 1e-05)
-        hidden.append(outputs * scale * gain_ref[head : head + 1, :])
-    hidden = jnp.concatenate(hidden, axis=1)
-    share = tokens // spread
-    first = jnp.concatenate([hidden[i * share : (i + 1) * share] for i in range(0, spread, 2)], axis=0)
-    second = jnp.concatenate([hidden[i * share : (i + 1) * share] for i in range(1, spread, 2)], axis=0)
-    on_first = core_ref[0] == 0
-    keep_ref[...] = jnp.where(on_first, first, second).astype(BF16)
-    send = jnp.where(on_first, second, first).astype(BF16)
-    send_ref[...] = jnp.dot(send, weight_ref[...], preferred_element_type=F32)
-
-
-def keep_kernel(keep_ref, weight_ref, out_ref):
-    out_ref[...] = jnp.dot(keep_ref[...], weight_ref[...], preferred_element_type=F32)
-
-
-def add_kernel(left_ref, right_ref, out_ref):
-    out_ref[...] = left_ref[...] + right_ref[...]
+        scaled = outputs * scale * gain_ref[head : head + 1, :]
+        hidden_ref[:, lanes] = scaled.astype(BF16).astype(F32)
+
+
+def project_kernel(spread, core_ref, hidden_ref, weight_ref, out_ref):
+    share = hidden_ref.shape[1] // spread
+    kept = []
+    for i in range(0, spread, 2):
+        even = jnp.concatenate([hidden_ref[c, i * share : (i + 1) * share] for c in range(2)], axis=1)
+        odd = jnp.concatenate([hidden_ref[c, (i + 1) * share : (i + 2) * share] for c in range(2)], axis=1)
+        kept.append(jnp.where(core_ref[0] == 0, even, odd))
+    kept = jnp.concatenate(kept, axis=0).astype(BF16)
+    out_ref[...] = jnp.dot(kept, weight_ref[...], preferred_element_type=F32)
 
 
 def per_device(queries, key_rows, value_rows, strengths, log_decay, norm_gain, out_weight):
@@ -245,7 +279,7 @@
     part_rows = width + width * heads // GROUP
     params = pltpu.CompilerParams(vmem_limit_bytes=48 * 1024 * 1024)
 
-    def call(body, out_shape, name, flops=0, in_specs=None):
+    def call(body, out_shape, name, flops=0, in_specs=None, scratch=()):
         extra = {} if in_specs is None else dict(in_specs=in_specs)
         return pl.pallas_call(
             body,
@@ -253,11 +287,12 @@
             compiler_params=params,
             name=name,
             cost_estimate=pl.CostEstimate(flops=flops, bytes_accessed=1 << 20, transcendentals=0),
+            scratch_shapes=scratch,
             **extra,
         )
 
-    def array(*shape):
-        return jax.ShapeDtypeStruct(shape, F32)
+    def array(*shape, dtype=F32):
+        return jax.ShapeDtypeStruct(shape, dtype)
 
     def pairs(flip):
         return [[i, i ^ flip] for i in range(ctx) if i < i ^ flip]
@@ -265,28 +300,41 @@
     smem = pl.BlockSpec(memory_space=pltpu.SMEM)
     vmem = pl.BlockSpec(memory_space=pltpu.VMEM)
     inner = [[g * GROUP + j for j in range(GROUP)] for g in range(ctx // GROUP)]
-
-    query = queries.reshape(tokens, heads * width)
-    keys = key_rows.reshape(rows, heads * width)
-    decay_t = jnp.concatenate([log_decay.T, jnp.zeros((8 - heads, tokens), F32)], axis=0)
-    msg, solved = call(
+    cores = [[i, i + 1] for i in range(0, spread, 2)]
+    core = (lax.axis_index("head") % 2).astype(jnp.int32).reshape(1)
+
+    small = jnp.concatenate(
+        [
+            log_decay.T,
+            strengths.transpose(1, 2, 0).reshape(2 * heads, tokens),
+            jnp.zeros((8 - 3 * heads, tokens), F32),
+        ],
+        axis=0,
+    )
+    msg, solved, keys = call(
         functools.partial(local_kernel, heads),
-        (array(GROUP, part_rows, width), array(heads, rows, 2 * width)),
+        (array(GROUP, part_rows, width), array(heads, rows, 2 * width), array(heads, rows, width)),
         "local_chunk",
-    )(
-        keys,
-        value_rows.reshape(rows, heads * width),
-        strengths.reshape(rows, heads),
-        log_decay,
-        decay_t,
-    )
+        scratch=[pltpu.VMEM((heads * rows, width), F32)] * 2,
+    )(key_rows.reshape(heads * rows, width), value_rows.reshape(heads * rows, width), small)
     parts = lax.all_to_all(msg, "ctx", 0, 0, axis_index_groups=inner)
+    late_weight, _ = lax.optimization_barrier((out_weight, solved))
+    wide = call(widen_kernel, array(*out_weight.shape), "widen", flops=10**9)(late_weight)
+    other = lax.ppermute(wide, "head", [(i, i ^ 1) for i in range(spread)])
+    both = call(
+        weight_kernel,
+        array(2 * out_weight.shape[0], columns, dtype=BF16),
+        "chip_weight",
+        flops=10**9,
+        in_specs=[smem, vmem, vmem],
+    )(core, late_weight, other)
     own, through = call(
         functools.partial(own_kernel, heads),
         (array(tokens, heads * width), array(tokens, heads * width)),
         "own_outputs",
         flops=4 * 10**9,
-    )(query, keys, log_decay, decay_t, solved)
+        scratch=[pltpu.VMEM((heads * tokens, width), F32)],
+    )(queries.reshape(heads * tokens, width), keys, small, solved)
     prefix, total = call(
         functools.partial(group_kernel, width),
         (array(GROUP - 1, part_rows, width), array(part_rows, width)),
@@ -307,16 +355,16 @@
         in_specs=[smem, vmem, vmem, vmem, vmem],
     )(place, pair, quad, far, prefix)
     states = lax.all_to_all(starts, "ctx", 0, 0, axis_index_groups=inner)
-    core = (lax.axis_index("head") % 2).astype(jnp.int32).reshape(1)
-    send, keep = call(
-        functools.partial(output_kernel, heads, spread),
-        (array(tokens // 2, columns), jax.ShapeDtypeStruct((tokens // 2, heads * width), BF16)),
-        "project_send",
-        in_specs=[smem, vmem, vmem, vmem, vmem, vmem],
-    )(core, own, through, states.reshape(heads, width, width), norm_gain, out_weight)
-    arrived = lax.ppermute(send, "head", [(i, i ^ 1) for i in range(spread)])
-    kept = call(keep_kernel, array(tokens // 2, columns), "project_keep", flops=10**8)(keep, out_weight)
-    sums = call(add_kernel, array(tokens // 2, columns), "add_cores")(kept, arrived)
+    hidden = call(
+        functools.partial(hidden_kernel, heads), array(tokens, heads * width), "hidden"
+    )(own, through, states.reshape(heads, width, width), norm_gain)
+    hidden = lax.all_gather(hidden, "head", axis_index_groups=cores)
+    sums = call(
+        functools.partial(project_kernel, spread),
+        array(tokens // 2, columns),
+        "project",
+        in_specs=[smem, vmem, vmem],
+    )(core, hidden, both)
     ring = [[i * 2 + c for i in range(spread // 2)] for c in range(2)]
     shares = lax.all_to_all(
         sums.reshape(spread // 2, tokens // spread, columns), "head", 0, 0, axis_index_groups=ring

time: 86 us -> 84.4 us (0.981)
  waiting for transfers between devices: 13.6 us -> 0.52 us
  blocking collectives: 37.9 us -> 44.7 us
  local copies, waits for them, and re-layouts: 3.3 us -> 7.86 us
  starting transfers between devices: 20.9 us -> 18.6 us
  Pallas kernels: 9.14 us -> 10.7 us
    all_gather x0 -> x1, blocking collectives: none -> 7.97 us  [per_device(): hidden = lax.all_gather(hidden, 'head', axis_index_groups=cores)]
    all_to_all x1, waiting for transfers between devices: 7.66 us -> 0.01 us  [per_device(): parts = lax.all_to_all(msg, 'ctx', 0, 0, axis_index_groups=inner)]
    unnamed x15 -> x20, local copies, waits for them, and re-layouts: 2.36 us -> 7.78 us
    all_to_all x1, waiting for transfers between devices: 4.72 us -> 0.52 us  [per_device(): states = lax.all_to_all(starts, 'ctx', 0, 0, axis_index_groups=inner)]
    ppermute x1, starting transfers between devices: 8.25 us -> 6.08 us  [per_device(): other = lax.ppermute(wide, 'head', [(i, i ^ 1) for i in range(spread)])]
    pallas_call x3 -> x4, Pallas kernels: 0.95 us -> 2.62 us  [the longest x1 1.47 us: per_device(): call(widen_kernel, array(*out_weight.shape), 'widen', flops=10 ** 9)]
    ppermute x1, waiting for transfers between devices: 1.22 us -> 0.01 us  [per_device(): other = lax.ppermute(wide, 'head', [(i, i ^ 1) for i in range(spread)])]
    all_gather x1, blocking collectives: 6.72 us -> 5.57 us  [per_device(): pair = lax.all_gather(total, 'ctx', axis_index_groups=pairs(8))]
  transfers between devices with their start and end apart: 3 -> 3, of which waited for: 3 -> 1; matrix products, arithmetic and copies ran while one was open for 0% -> 0% of each run, Pallas kernels for 1% -> 6%
where the time goes in v3:
time: 84.4 us; the launch traced here: 83.9 us
  blocking collectives  44.7 us (53%)
  starting transfers between devices  18.6 us (22%)
  Pallas kernels  10.7 us (13%)
  local copies, waits for them, and re-layouts  7.86 us (9%)
  other arithmetic  1.42 us (2%)
    all_to_all x1, blocking collectives, per_device(): lax.all_to_all(sums.reshape(spread // 2, tokens // spread, columns), 'hea...  12.4 us
    all_gather x1, blocking collectives, per_device(): quad = lax.all_gather(total, 'ctx', axis_index_groups=pairs(16))  9.39 us
    all_gather x1, blocking collectives, per_device(): far = lax.all_gather(write, 'ctx', axis_index_groups=pairs(48))  9.33 us
    all_gather x1, blocking collectives, per_device(): hidden = lax.all_gather(hidden, 'head', axis_index_groups=cores)  7.97 us
    unnamed x20, local copies, waits for them, and re-layouts  7.78 us
    all_to_all x1, starting transfers between devices, per_device(): parts = lax.all_to_all(msg, 'ctx', 0, 0, axis_index_groups=inner)  6.37 us
    all_to_all x1, starting transfers between devices, per_device(): states = lax.all_to_all(starts, 'ctx', 0, 0, axis_index_groups=inner)  6.11 us
    ppermute x1, starting transfers between devices, per_device(): other = lax.ppermute(wide, 'head', [(i, i ^ 1) for i in range(spread)])  6.08 us
  transfers between devices with their start and end apart: 3, of which 1 were waited for; matrix products, arithmetic and copies ran while one was open for 0% of the time, Pallas kernels for 6%

profile of v3, /device:TPU:1, one launch (start us, length us, event | category | flops | bytes accessed | tf_op | source)
XLA Modules:
  0.0 83.9 jit_solution(8257393425179923541)
XLA Ops:
  0.1 0.8 maximum_maximum_fusion.small_ref
  0.8 0.9 %copy-done.4 = bf16[128,2,2,128]{3,2,1,0:T(2,128)(2,1)S(1)} copy-done((bf16[128,2,2,128]{3,2,1,0:T(2,128)(2,1)S(1)}, bf16[128,2,2,128]{3,2,1,0:T(2,128)(2,1)}, u32[]{:S(2)}) %copy-start.4) | copy-done | bytes 131096
  1.8 0.9 %copy-done.5 = bf16[128,2,2,128]{3,2,1,0:T(2,128)(2,1)S(1)} copy-done((bf16[128,2,2,128]{3,2,1,0:T(2,128)(2,1)S(1)}, bf16[128,2,2,128]{3,2,1,0:T(2,128)(2,1)}, u32[]{:S(2)}) %copy-start.5) | copy-done | bytes 131096
  2.7 5.2 %local_chunk.1 = (f32[8,160,128]{2,1,0:T(8,128)}, f32[2,256,256]{2,1,0:T(8,128)S(1)}, f32[2,256,128]{2,1,0:T(8,128)S(1)}) custom-call(bf16[512,128]{1,0:T(8,128)(2,1)S(1)} %bitcast.22, bf16[512,128]{1,0:T(8,128)(2,1)S(1)} %bitcast.23, f32[8,128]{1,0:T(8,128)S(1)} %maximum_maximum_fusion.small_ref), custom_call_target="tpu_custom_call" | custom-call | bytes 1048576 | tf_op jit(solution)/shard_map/local_chunk/pallas_call | solution.py:314
  7.9 0.8 copy-done.7
  8.7 6.4 %all-to-all-start = ((f32[8,160,128]{2,1,0:T(8,128)}), f32[8,160,128]{2,1,0:T(8,128)S(1)}, u32[]{:S(2)}, u32[]{:S(2)}) async-start(f32[8,160,128]{2,1,0:T(8,128)} %get-tuple-element.17), calls=%async_computation | async-start | bytes 1310720 | tf_op jit(solution)/shard_map/all_to_all | solution.py:320
  15.1 1.2 %copy-done.2 = bf16[256,2048]{1,0:T(8,128)(2,1)S(1)} copy-done((bf16[256,2048]{1,0:T(8,128)(2,1)S(1)}, bf16[256,2048]{1,0:T(8,128)(2,1)}, u32[]{:S(2)}) %copy-start.2) | copy-done | bytes 1048600
  16.3 1.5 %widen.1 = f32[256,2048]{1,0:T(8,128)} custom-call(bf16[256,2048]{1,0:T(8,128)(2,1)S(1)} %copy-done.2), custom_call_target="tpu_custom_call" | custom-call | flops 1000000000 | bytes 1048576 | tf_op jit(solution)/shard_map/widen/pallas_call | solution.py:322
  17.7 6.1 %collective-permute-start = (f32[256,2048]{1,0:T(8,128)}, f32[256,2048]{1,0:T(8,128)S(1)}, u32[]{:S(2)}, u32[]{:S(2)}) collective-permute-start(f32[256,2048]{1,0:T(8,128)} %widen.1), channel_id=1, source_target_pairs={{0,1},{1,0},{2,3},{3,2},{4,5},{5,4},{6,7},{7,6},{8,9},{9,8},{10,11... | collective-permute-start | bytes 6291464 | tf_op jit(solution)/shard_map/ppermute | solution.py:323
  23.9 0.7 group_scan.1
  24.5 5.6 %all-gather = f32[320,128]{1,0:T(8,128)S(1)} all-gather(f32[160,128]{1,0:T(8,128)S(1)} %get-tuple-element.18), channel_id=2, replica_groups={{0,64},{8,72},{16,80},{24,88},{32,96},{40,104},{48,112},{56,120},{128,1..., dimensions={0}, use_global_device_ids=true | all-gather | bytes 245760 | tf_op jit(solution)/shard_map/all_gather | solution.py:343
  30.3 9.4 %all-gather.1 = f32[320,128]{1,0:T(8,128)S(1)} all-gather(f32[160,128]{1,0:T(8,128)S(1)} %pair_total.1), channel_id=3, replica_groups={{0,128},{8,136},{16,144},{24,152},{32,160},{40,168},{48,176},{56,184},{..., dimensions={0}, use_global_device_ids=true | all-gather | bytes 245760 | tf_op jit(solution)/shard_map/all_gather | solution.py:345
  39.8 9.3 %all-gather.2 = f32[64,128]{1,0:T(8,128)S(1)} all-gather(f32[32,128]{1,0:T(8,128)S(1)} %half_write.1), channel_id=4, replica_groups={{0,384},{8,392},{16,400},{24,408},{32,416},{40,424},{48,432},{56,440},{..., dimensions={0}, use_global_device_ids=true | all-gather | bytes 49152 | tf_op jit(solution)/shard_map/all_gather | solution.py:349
  49.1 1.3 %start_states.1 = f32[8,32,128]{2,1,0:T(8,128)} custom-call(s32[1]{0:T(128)} %bitcast.7.place_ref, f32[2,160,128]{2,1,0:T(8,128)S(1)} %bitcast.19, f32[2,160,128]{2,1,0:T(8,128)S(1)} %bitcast.17, f32[2,32,128]{2,1,0:T(8,128)S(1)} %bitcast.24, f32[7,160,128]{2,1,0:T(8,128)S(1)} %get-tuple-element.19.prefix_ref), custom_call_target="tpu_custom_call" | custom-call | bytes 1048576 | tf_op jit(solution)/shard_map/start_states/pallas_call | solution.py:351
  50.4 6.1 %all-to-all-start.1 = ((f32[8,32,128]{2,1,0:T(8,128)}), f32[8,32,128]{2,1,0:T(8,128)S(1)}, u32[]{:S(2)}, u32[]{:S(2)}) async-start(f32[8,32,128]{2,1,0:T(8,128)} %start_states.1), calls=%async_computation.1 | async-start | bytes 262144 | tf_op jit(solution)/shard_map/all_to_all | solution.py:357
  56.5 1.0 %copy-done.8 = f32[2,256,256]{2,1,0:T(8,128)S(1)} copy-done((f32[2,256,256]{2,1,0:T(8,128)S(1)}, f32[2,256,256]{2,1,0:T(8,128)}, u32[]{:S(2)}) %copy-start.8) | copy-done | bytes 524312
  57.6 0.6 own_outputs.1
  58.2 1.3 %copy-done = f32[256,2048]{1,0:T(8,128)} copy-done((f32[256,2048]{1,0:T(8,128)}, f32[256,2048]{1,0:T(8,128)S(1)}, u32[]{:S(2)}) %copy-start) | copy-done | bytes 2097176
  59.5 1.6 %copy-done.1 = f32[256,2048]{1,0:T(8,128)S(1)} copy-done((f32[256,2048]{1,0:T(8,128)S(1)}, f32[256,2048]{1,0:T(8,128)}, u32[]{:S(2)}) %copy-start.1) | copy-done | bytes 2097176
  61.4 0.5 all-to-all-done.1
  62.3 8.0 %all-gather.3 = f32[256,256]{1,0:T(8,128)S(1)} all-gather(f32[128,256]{1,0:T(8,128)S(1)} %hidden.1), channel_id=5, replica_groups={{0,1},{2,3},{4,5},{6,7},{8,9},{10,11},{12,13},{14,15},{16,17},{18,19},{..., dimensions={0}, use_global_device_ids=true | all-gather | bytes 393216 | tf_op jit(solution)/shard_map/all_gather | solution.py:361
  70.3 0.5 project.1
  70.8 12.4 %all_to_all.15 = f32[4,16,2048]{2,1,0:T(8,128)S(1)} all-to-all(f32[4,16,2048]{2,1,0:T(8,128)S(1)} %bitcast.15), channel_id=1, replica_groups={{0,2,4,6},{1,3,5,7},{8,10,12,14},{9,11,13,15},{16,18,20,22},{17,19,21,2..., dimensions={0} | all-to-all | bytes 1048576 | tf_op jit(solution)/shard_map/all_to_all | solution.py:369
  83.2 0.7 reduce_sum.9
  (21 shorter events, 1.1 us)
Async XLA Ops:
  0.8 0.9 %copy-start.4 = (bf16[128,2,2,128]{3,2,1,0:T(2,128)(2,1)S(1)}, bf16[128,2,2,128]{3,2,1,0:T(2,128)(2,1)}, u32[]{:S(2)}) copy-start(bf16[128,2,2,128]{3,2,1,0:T(2,128)(2,1)} %param.8) | copy-start | bytes 393220
  1.8 0.9 %copy-start.5 = (bf16[128,2,2,128]{3,2,1,0:T(2,128)(2,1)S(1)}, bf16[128,2,2,128]{3,2,1,0:T(2,128)(2,1)}, u32[]{:S(2)}) copy-start(bf16[128,2,2,128]{3,2,1,0:T(2,128)(2,1)} %param.9) | copy-start | bytes 393220
  7.9 0.8 copy-start.7
  8.7 15.2 %all-to-all-start = ((f32[8,160,128]{2,1,0:T(8,128)}), f32[8,160,128]{2,1,0:T(8,128)S(1)}, u32[]{:S(2)}, u32[]{:S(2)}) async-start(f32[8,160,128]{2,1,0:T(8,128)} %get-tuple-element.17), calls=%async_computation | async-start | bytes 1310720 | tf_op jit(solution)/shard_map/all_to_all | solution.py:320
  15.0 1.2 %copy-start.2 = (bf16[256,2048]{1,0:T(8,128)(2,1)S(1)}, bf16[256,2048]{1,0:T(8,128)(2,1)}, u32[]{:S(2)}) copy-start(bf16[256,2048]{1,0:T(8,128)(2,1)} %own_ref) | copy-start | bytes 3145732
  17.7 38.8 %copy-start.9 = (bf16[128,2,128]{2,1,0:T(2,128)(2,1)S(1)}, bf16[128,2,128]{2,1,0:T(2,128)(2,1)}, u32[]{:S(2)}) copy-start(bf16[128,2,128]{2,1,0:T(2,128)(2,1)} %param.7) | copy-start | bytes 196612
  17.7 40.4 %collective-permute-start = (f32[256,2048]{1,0:T(8,128)}, f32[256,2048]{1,0:T(8,128)S(1)}, u32[]{:S(2)}, u32[]{:S(2)}) collective-permute-start(f32[256,2048]{1,0:T(8,128)} %widen.1), channel_id=1, source_target_pairs={{0,1},{1,0},{2,3},{3,2},{4,5},{5,4},{6,7},{7,6},{8,9},{9,8},{10,11... | collective-permute-start | bytes 6291464 | tf_op jit(solution)/shard_map/ppermute | solution.py:323
  50.4 11.5 %all-to-all-start.1 = ((f32[8,32,128]{2,1,0:T(8,128)}), f32[8,32,128]{2,1,0:T(8,128)S(1)}, u32[]{:S(2)}, u32[]{:S(2)}) async-start(f32[8,32,128]{2,1,0:T(8,128)} %start_states.1), calls=%async_computation.1 | async-start | bytes 262144 | tf_op jit(solution)/shard_map/all_to_all | solution.py:357
  56.5 1.0 %copy-start.8 = (f32[2,256,256]{2,1,0:T(8,128)S(1)}, f32[2,256,256]{2,1,0:T(8,128)}, u32[]{:S(2)}) copy-start(f32[2,256,256]{2,1,0:T(8,128)} %copy-done.7) | copy-start | bytes 1572868
  57.6 2.0 %copy-start.3 = (bf16[256,2048]{1,0:T(8,128)(2,1)S(1)}, bf16[256,2048]{1,0:T(8,128)(2,1)}, u32[]{:S(2)}) copy-start(bf16[256,2048]{1,0:T(8,128)(2,1)} %own_ref) | copy-start | bytes 3145732
  58.2 1.3 %copy-start = (f32[256,2048]{1,0:T(8,128)}, f32[256,2048]{1,0:T(8,128)S(1)}, u32[]{:S(2)}) copy-start(f32[256,2048]{1,0:T(8,128)S(1)} %collective-permute-done.other_ref) | copy-start | bytes 6291460
  59.5 1.6 %copy-start.1 = (f32[256,2048]{1,0:T(8,128)S(1)}, f32[256,2048]{1,0:T(8,128)}, u32[]{:S(2)}) copy-start(f32[256,2048]{1,0:T(8,128)} %copy-done) | copy-start | bytes 6291460
  61.1 0.8 copy-start.6

commit v4 on v3

--- a/solution.py
+++ b/solution.py
@@ -25,7 +25,11 @@
     mul = functools.partial(
         lax.dot_general, dimension_numbers=dims(left_dim, right_dim), preferred_element_type=F32
     )
-    return mul(left[0], right[0]) + (mul(left[0], right[1]) + mul(left[1], right[0]))
+    if left_dim == 0:
+        return mul(left[0], right[0]) + (mul(left[0], right[1]) + mul(left[1], right[0]))
+    count = left[0].shape[0]
+    both = mul(jnp.concatenate(left, axis=0), right[0])
+    return both[:count] + (both[count:] + mul(left[0], right[1]))
 
 
 def dot(left, right, left_dim=1, right_dim=0):
@@ -60,8 +64,10 @@
     return wide[:8] + wide[8:16] + wide[16:24]
 
 
-def stack_rows(part, count):
-    return jnp.concatenate([part] * count, axis=0)
+def blocks_of(part, count, mask):
+    if part.shape[0] % 16:
+        part, count = jnp.concatenate([part, part], axis=0), count // 2
+    return tuple(jnp.concatenate([piece] * count, axis=0) * mask for piece in halves(part))
 
 
 def inverse_blocks(lowers, stop):
@@ -70,39 +76,39 @@
     lane = iota((width, size), 1)
     row = iota((width, size), 0)
     col = lane % width
+    rows = iota((size, size), 0)
+    cols = iota((size, size), 1)
     packed = []
     for lower in lowers:
         part = jnp.zeros((width, size), F32)
         for block in range(size // width):
             part = jnp.where(lane // width == block, lower[block * width : (block + 1) * width], part)
         packed.append(part)
-    same = iota((size, size), 0) // width == iota((size, size), 1) // width
+    same = jnp.where(rows // width == cols // width, 1.0, 0.0).astype(BF16)
     eye = jnp.where(row == col, 1.0, 0.0).astype(F32)
     inverses = [eye - jnp.where(row // 2 == col // 2, part, 0.0) for part in packed]
+    count = size // width
     for step in (2, 4):
         below = (row // (2 * step) == col // (2 * step)) & (row // step != col // step)
-        corners = [jnp.where(below, part, 0.0) for part in packed]
-        count = size // width
-        inner = [dot(c, jnp.where(same, stack_rows(t, count), 0.0)) for c, t in zip(corners, inverses)]
+        corners = [halves(jnp.where(below, part, 0.0)) for part in packed]
+        inner = [dot_halves(c, blocks_of(t, count, same)) for c, t in zip(corners, inverses)]
         inverses = [
-            t - dot(t, jnp.where(same, stack_rows(y, count), 0.0)) for t, y in zip(inverses, inner)
+            t - dot_halves(halves(t), blocks_of(y, count, same)) for t, y in zip(inverses, inner)
         ]
     while width < stop:
         count = size // width
         lane = iota((width, size), 1) // width
         even = lane % 2 == 0
-        rows = iota((size, size), 0) // width
-        cols = iota((size, size), 1) // width
-        same = rows == cols
-        below = (rows == cols + 1) & (cols % 2 == 0)
+        same = jnp.where(rows // width == cols // width, 1.0, 0.0).astype(BF16)
+        below = jnp.where((rows // width == cols // width + 1) & ((cols // width) % 2 == 0), 1.0, 0.0).astype(BF16)
         corners = []
         for lower in lowers:
             part = jnp.zeros((width, size), F32)
             for block in range(0, count, 2):
                 part = jnp.where(lane == block, lower[(block + 1) * width : (block + 2) * width], part)
-            corners.append(part)
-        inner = [dot(c, jnp.where(same, stack_rows(t, count), 0.0)) for c, t in zip(corners, inverses)]
-        outer = [dot(t, jnp.where(below, stack_rows(y, count), 0.0)) for t, y in zip(inverses, inner)]
+            corners.append(halves(part))
+        inner = [dot_halves(c, blocks_of(t, count, same)) for c, t in zip(corners, inverses)]
+        outer = [dot_halves(halves(t), blocks_of(y, count, below)) for t, y in zip(inverses, inner)]
         inverses = [
             jnp.concatenate([jnp.where(even, t, 0.0), jnp.where(even, -e, t)], axis=0)
             for t, e in zip(inverses, outer)
@@ -111,28 +117,51 @@
     return inverses
 
 
-def local_kernel(heads, k_ref, v_ref, small_ref, msg_ref, solved_ref, keys_ref, spread_k, spread_v):
+def local_kernel(
+    heads, k_hbm, v_hbm, decay_hbm, beta_hbm, msg_hbm, solved_hbm, keys_hbm,
+    k_ref, v_ref, small_ref, spread_k, spread_v, keys_ref, solved_ref, carry_ref, write_ref, in_sems, out_sems,
+):
     rows = k_ref.shape[0] // heads
     tokens = rows // 2
     width = k_ref.shape[1]
     half = rows // 2
     quarter = width * heads // GROUP
-    spread_k[...] = unit_rows(k_ref[...].astype(F32))
-    spread_v[...] = v_ref[...].astype(F32)
-    small = thirds(small_ref[...])
+    sends = []
+
+    def send(source, target):
+        sends.append(pltpu.make_async_copy(source, target, out_sems.at[len(sends)]))
+        sends[-1].start()
+
+    small_ref[3 * heads :] = jnp.zeros((8 - 3 * heads, tokens), F32)
+    fetches = [
+        pltpu.make_async_copy(source, target, in_sems.at[i])
+        for i, (source, target) in enumerate(
+            (
+                (k_hbm, k_ref),
+                (decay_hbm, small_ref.at[:heads]),
+                (beta_hbm, small_ref.at[heads : 3 * heads]),
+                (v_hbm, v_ref),
+            )
+        )
+    ]
+    for fetch in fetches:
+        fetch.start()
     row_tok = iota((rows, tokens), 0) // 2
     tok = iota((rows, tokens), 1)
-    cumul_rows = picked(row_tok >= tok, small)
-    cumul_line = picked_line(small, row_tok >= tok)
-    betas = picked(row_tok == tok, small)
     first = iota((rows, 1), 0) % 2 == 0
     row_ids = iota((rows, rows), 0)
     col_ids = iota((rows, rows), 1)
     eye_k = jnp.where(iota((width, width), 0) == iota((width, width), 1), 1.0, 0.0).astype(F32)
-    keys, lowers, strength, values = [], [], [], []
+    for fetch in fetches[:3]:
+        fetch.wait()
+    small = thirds(small_ref[...])
+    cumul_rows = picked(row_tok >= tok, small)
+    cumul_line = picked_line(small, row_tok >= tok)
+    betas = picked(row_tok == tok, small)
+    spread_k[...] = unit_rows(k_ref[...].astype(F32))
+    keys, lowers, strength = [], [], []
     for head in range(heads):
         unit = spread_k[pl.ds(head, rows, stride=heads), :]
-        values.append(spread_v[pl.ds(head, rows, stride=heads), :])
         beta = jnp.where(
             first, betas[:, heads + head : heads + head + 1], betas[:, 2 * heads + head : 2 * heads + head + 1]
         )
@@ -144,10 +173,19 @@
         keys.append(unit)
         strength.append(beta)
         keys_ref[head] = unit
+        send(keys_ref.at[head], keys_hbm.at[head])
     inverses = inverse_blocks(lowers, half)
+    fetches[3].wait()
+    spread_v[...] = v_ref[...].astype(F32)
     rights = [
-        jnp.concatenate([beta * value, (beta * jnp.exp(cumul_rows[:, head : head + 1])) * unit], axis=1)
-        for head, (beta, value, unit) in enumerate(zip(strength, values, keys))
+        jnp.concatenate(
+            [
+                strength[head] * spread_v[pl.ds(head, rows, stride=heads), :],
+                (strength[head] * jnp.exp(cumul_rows[:, head : head + 1])) * keys[head],
+            ],
+            axis=1,
+        )
+        for head in range(heads)
     ]
     uppers = [dot(inverse[:, :half], right[:half]) for inverse, right in zip(inverses, rights)]
     moved = [
@@ -158,22 +196,57 @@
     for head in range(heads):
         solved = jnp.concatenate([uppers[head], unders[head]], axis=0)
         solved_ref[head] = solved
+        send(solved_ref.at[head], solved_hbm.at[head])
         cumul = cumul_rows[:, head : head + 1]
         last = cumul[rows - 1 : rows, :]
         tail = jnp.exp(last - cumul) * keys[head]
         pair = dot(solved, tail, 0, 0)
-        carry = jnp.exp(last) * eye_k - pair[width:]
+        write_ref[head] = pair[:width]
+        carry_ref[head] = jnp.exp(last) * eye_k - pair[width:]
         for part in range(GROUP // heads):
             member = head * (GROUP // heads) + part
-            msg_ref[member, :width, :] = carry
-            msg_ref[member, width:, :] = pair[part * quarter : (part + 1) * quarter]
-
-
-def own_kernel(heads, q_ref, keys_ref, small_ref, solved_ref, own_ref, through_ref, spread_q):
+            send(carry_ref.at[head], msg_hbm.at[member, :width])
+            send(write_ref.at[head, part * quarter : (part + 1) * quarter], msg_hbm.at[member, width:])
+    for copy in sends:
+        copy.wait()
+
+
+def local_call(keys, values, decay, beta):
+    heads, tokens = decay.shape
+    rows, width = keys.shape[0] // heads, keys.shape[1]
+    any_space = pl.BlockSpec(memory_space=pl.ANY)
+    return pl.pallas_call(
+        functools.partial(local_kernel, heads),
+        out_shape=(
+            jax.ShapeDtypeStruct((GROUP, width + width * heads // GROUP, width), F32),
+            jax.ShapeDtypeStruct((heads, rows, 2 * width), F32),
+            jax.ShapeDtypeStruct((heads, rows, width), F32),
+        ),
+        in_specs=[any_space] * 4,
+        out_specs=(any_space,) * 3,
+        scratch_shapes=[
+            pltpu.VMEM(keys.shape, BF16),
+            pltpu.VMEM(values.shape, BF16),
+            pltpu.VMEM((8, tokens), F32),
+            pltpu.VMEM(keys.shape, F32),
+            pltpu.VMEM(values.shape, F32),
+            pltpu.VMEM((heads, rows, width), F32),
+            pltpu.VMEM((heads, rows, 2 * width), F32),
+            pltpu.VMEM((heads, width, width), F32),
+            pltpu.VMEM((heads, width, width), F32),
+            pltpu.SemaphoreType.DMA((4,)),
+            pltpu.SemaphoreType.DMA((2 * heads + 2 * GROUP,)),
+        ],
+        compiler_params=pltpu.CompilerParams(vmem_limit_bytes=60 * 1024 * 1024),
+        name="local_chunk",
+    )(keys, values, decay, beta)
+
+
+def own_kernel(heads, q_ref, keys_ref, decay_ref, solved_ref, own_ref, through_ref, spread_q):
     tokens = q_ref.shape[0] // heads
     rows = keys_ref.shape[1]
     spread_q[...] = unit_rows(q_ref[...].astype(F32))
-    small = thirds(small_ref[...])
+    small = thirds(jnp.concatenate([decay_ref[...], jnp.zeros((8 - heads, tokens), F32)], axis=0))
     reached = iota((rows, tokens), 0) // 2 >= iota((rows, tokens), 1)
     cumul_line = picked_line(small, reached)
     cumul_toks = picked(iota((tokens, tokens), 0) >= iota((tokens, tokens), 1), small)
@@ -303,20 +376,12 @@
     cores = [[i, i + 1] for i in range(0, spread, 2)]
     core = (lax.axis_index("head") % 2).astype(jnp.int32).reshape(1)
 
-    small = jnp.concatenate(
-        [
-            log_decay.T,
-            strengths.transpose(1, 2, 0).reshape(2 * heads, tokens),
-            jnp.zeros((8 - 3 * heads, tokens), F32),
-        ],
-        axis=0,
-    )
-    msg, solved, keys = call(
-        functools.partial(local_kernel, heads),
-        (array(GROUP, part_rows, width), array(heads, rows, 2 * width), array(heads, rows, width)),
-        "local_chunk",
-        scratch=[pltpu.VMEM((heads * rows, width), F32)] * 2,
-    )(key_rows.reshape(heads * rows, width), value_rows.reshape(heads * rows, width), small)
+    msg, solved, keys = local_call(
+        key_rows.reshape(heads * rows, width),
+        value_rows.reshape(heads * rows, width),
+        log_decay.T,
+        strengths.transpose(1, 2, 0).reshape(2 * heads, tokens),
+    )
     parts = lax.all_to_all(msg, "ctx", 0, 0, axis_index_groups=inner)
     late_weight, _ = lax.optimization_barrier((out_weight, solved))
     wide = call(widen_kernel, array(*out_weight.shape), "widen", flops=10**9)(late_weight)
@@ -334,7 +399,8 @@
         "own_outputs",
         flops=4 * 10**9,
         scratch=[pltpu.VMEM((heads * tokens, width), F32)],
-    )(queries.reshape(heads * tokens, width), keys, small, solved)
+    )(queries.reshape(heads * tokens, width), keys, log_decay.T, solved)
+    parts, own, through = lax.optimization_barrier((parts, own, through))
     prefix, total = call(
         functools.partial(group_kernel, width),
         (array(GROUP - 1, part_rows, width), array(part_rows, width)),

time: 84.4 us -> 81.5 us (0.966)
  blocking collectives: 44.7 us -> 43.1 us
  local copies, waits for them, and re-layouts: 7.86 us -> 6.42 us
    unnamed x20 -> x18, local copies, waits for them, and re-layouts: 7.78 us -> 6.42 us
where the time goes in v4:
time: 81.5 us; the launch traced here: 81 us
  blocking collectives  43.1 us (53%)
  starting transfers between devices  18.5 us (23%)
  Pallas kernels  11.2 us (14%)
  local copies, waits for them, and re-layouts  6.42 us (8%)
  waiting for transfers between devices  0.97 us (1%)
    all_to_all x1, blocking collectives, per_device(): lax.all_to_all(sums.reshape(spread // 2, tokens // spread, columns), 'hea...  12.4 us
    all_gather x1, blocking collectives, per_device(): far = lax.all_gather(write, 'ctx', axis_index_groups=pairs(48))  9.24 us
    all_gather x1, blocking collectives, per_device(): quad = lax.all_gather(total, 'ctx', axis_index_groups=pairs(16))  8.58 us
    all_gather x1, blocking collectives, per_device(): hidden = lax.all_gather(hidden, 'head', axis_index_groups=cores)  7.97 us
    unnamed x18, local copies, waits for them, and re-layouts  6.42 us
    all_to_all x1, starting transfers between devices, per_device(): parts = lax.all_to_all(msg, 'ctx', 0, 0, axis_index_groups=inner)  6.4 us
    all_to_all x1, starting transfers between devices, per_device(): states = lax.all_to_all(starts, 'ctx', 0, 0, axis_index_groups=inner)  6.12 us
    pallas_call x1, Pallas kernels, local_call(): pl.pallas_call(functools.partial(local_kernel, heads), out_shape=(jax.Sha...  5.94 us
  transfers between devices with their start and end apart: 3, of which 1 were waited for; matrix products, arithmetic and copies ran while one was open for 0% of the time, Pallas kernels for 6%

profile of v4, /device:TPU:1, one launch (start us, length us, event | category | flops | bytes accessed | tf_op | source)
XLA Modules:
  0.0 81.0 jit_solution(12020079510260243154)
XLA Ops:
  0.0 5.9 %local_chunk.1 = (f32[8,160,128]{2,1,0:T(8,128)}, f32[2,256,256]{2,1,0:T(8,128)}, f32[2,256,128]{2,1,0:T(8,128)}) custom-call(bf16[512,128]{1,0:T(8,128)(2,1)} %bitcast.26, bf16[512,128]{1,0:T(8,128)(2,1)} %bitcast.27, f32[2,128]{1,0:T(2,128)} %bitcast.23, f32[4,128]{1,0:T(4,128)} %bitcast.28), custom_call_target="tpu_custom_call" | custom-call | tf_op jit(solution)/shard_map/local_chunk/pallas_call | solution.py:218
  6.0 6.4 %all-to-all-start = ((f32[8,160,128]{2,1,0:T(8,128)}), f32[8,160,128]{2,1,0:T(8,128)S(1)}, u32[]{:S(2)}, u32[]{:S(2)}) async-start(f32[8,160,128]{2,1,0:T(8,128)} %get-tuple-element.16), calls=%async_computation | async-start | bytes 1310720 | tf_op jit(solution)/shard_map/all_to_all | solution.py:385
  12.4 1.2 %copy-done.2 = bf16[256,2048]{1,0:T(8,128)(2,1)S(1)} copy-done((bf16[256,2048]{1,0:T(8,128)(2,1)S(1)}, bf16[256,2048]{1,0:T(8,128)(2,1)}, u32[]{:S(2)}) %copy-start.2) | copy-done | bytes 1048600
  13.6 1.5 %widen.1 = f32[256,2048]{1,0:T(8,128)} custom-call(bf16[256,2048]{1,0:T(8,128)(2,1)S(1)} %copy-done.2), custom_call_target="tpu_custom_call" | custom-call | flops 1000000000 | bytes 1048576 | tf_op jit(solution)/shard_map/widen/pallas_call | solution.py:387
  15.1 5.9 %collective-permute-start = (f32[256,2048]{1,0:T(8,128)}, f32[256,2048]{1,0:T(8,128)S(1)}, u32[]{:S(2)}, u32[]{:S(2)}) collective-permute-start(f32[256,2048]{1,0:T(8,128)} %widen.1), channel_id=1, source_target_pairs={{0,1},{1,0},{2,3},{3,2},{4,5},{5,4},{6,7},{7,6},{8,9},{9,8},{10,11... | collective-permute-start | bytes 6291464 | tf_op jit(solution)/shard_map/ppermute | solution.py:388
  21.1 1.0 %copy-done.6 = f32[2,256,256]{2,1,0:T(8,128)S(1)} copy-done((f32[2,256,256]{2,1,0:T(8,128)S(1)}, f32[2,256,256]{2,1,0:T(8,128)}, u32[]{:S(2)}) %copy-start.6) | copy-done | bytes 524312
  22.1 0.6 own_outputs.1
  22.7 0.6 group_scan.1
  23.4 4.9 %all-gather = f32[320,128]{1,0:T(8,128)S(1)} all-gather(f32[160,128]{1,0:T(8,128)S(1)} %get-tuple-element.24), channel_id=2, replica_groups={{0,64},{8,72},{16,80},{24,88},{32,96},{40,104},{48,112},{56,120},{128,1..., dimensions={0}, use_global_device_ids=true | all-gather | bytes 245760 | tf_op jit(solution)/shard_map/all_gather | solution.py:409
  28.3 0.2 pair_total.1
  28.4 8.6 %all-gather.1 = f32[320,128]{1,0:T(8,128)S(1)} all-gather(f32[160,128]{1,0:T(8,128)S(1)} %pair_total.1), channel_id=3, replica_groups={{0,128},{8,136},{16,144},{24,152},{32,160},{40,168},{48,176},{56,184},{..., dimensions={0}, use_global_device_ids=true | all-gather | bytes 245760 | tf_op jit(solution)/shard_map/all_gather | solution.py:411
  37.1 9.2 %all-gather.2 = f32[64,128]{1,0:T(8,128)S(1)} all-gather(f32[32,128]{1,0:T(8,128)S(1)} %half_write.1), channel_id=4, replica_groups={{0,384},{8,392},{16,400},{24,408},{32,416},{40,424},{48,432},{56,440},{..., dimensions={0}, use_global_device_ids=true | all-gather | bytes 49152 | tf_op jit(solution)/shard_map/all_gather | solution.py:415
  46.4 1.2 %start_states.1 = f32[8,32,128]{2,1,0:T(8,128)} custom-call(s32[1]{0:T(128)} %bitcast.7.place_ref, f32[2,160,128]{2,1,0:T(8,128)S(1)} %bitcast.19, f32[2,160,128]{2,1,0:T(8,128)S(1)} %bitcast.17, f32[2,32,128]{2,1,0:T(8,128)S(1)} %bitcast.22, f32[7,160,128]{2,1,0:T(8,128)S(1)} %get-tuple-element.25.prefix_ref), custom_call_target="tpu_custom_call" | custom-call | bytes 1048576 | tf_op jit(solution)/shard_map/start_states/pallas_call | solution.py:417
  47.6 6.1 %all-to-all-start.1 = ((f32[8,32,128]{2,1,0:T(8,128)}), f32[8,32,128]{2,1,0:T(8,128)S(1)}, u32[]{:S(2)}, u32[]{:S(2)}) async-start(f32[8,32,128]{2,1,0:T(8,128)} %start_states.1), calls=%async_computation.1 | async-start | bytes 262144 | tf_op jit(solution)/shard_map/all_to_all | solution.py:423
  53.7 1.3 %copy-done = f32[256,2048]{1,0:T(8,128)} copy-done((f32[256,2048]{1,0:T(8,128)}, f32[256,2048]{1,0:T(8,128)S(1)}, u32[]{:S(2)}) %copy-start) | copy-done | bytes 2097176
  55.0 1.6 %copy-done.1 = f32[256,2048]{1,0:T(8,128)S(1)} copy-done((f32[256,2048]{1,0:T(8,128)S(1)}, f32[256,2048]{1,0:T(8,128)}, u32[]{:S(2)}) %copy-start.1) | copy-done | bytes 2097176
  56.6 1.2 %copy-done.3 = bf16[256,2048]{1,0:T(8,128)(2,1)S(1)} copy-done((bf16[256,2048]{1,0:T(8,128)(2,1)S(1)}, bf16[256,2048]{1,0:T(8,128)(2,1)}, u32[]{:S(2)}) %copy-start.3) | copy-done | bytes 1048600
  57.8 0.3 chip_weight.1.weight_ref
  58.1 1.0 %all-to-all-done.1 = f32[8,32,128]{2,1,0:T(8,128)S(1)} async-done(((f32[8,32,128]{2,1,0:T(8,128)}), f32[8,32,128]{2,1,0:T(8,128)S(1)}, u32[]{:S(2)}, u32[]{:S(2)}) %all-to-all-start.1) | async-done | bytes 131104 | tf_op jit(solution)/shard_map/all_to_all | solution.py:423
  59.1 0.3 hidden.1
  59.4 8.0 %all-gather.3 = f32[256,256]{1,0:T(8,128)S(1)} all-gather(f32[128,256]{1,0:T(8,128)S(1)} %hidden.1), channel_id=5, replica_groups={{0,1},{2,3},{4,5},{6,7},{8,9},{10,11},{12,13},{14,15},{16,17},{18,19},{..., dimensions={0}, use_global_device_ids=true | all-gather | bytes 393216 | tf_op jit(solution)/shard_map/all_gather | solution.py:427
  67.4 0.5 project.1
  67.9 12.4 %all_to_all.15 = f32[4,16,2048]{2,1,0:T(8,128)S(1)} all-to-all(f32[4,16,2048]{2,1,0:T(8,128)S(1)} %bitcast.15), channel_id=1, replica_groups={{0,2,4,6},{1,3,5,7},{8,10,12,14},{9,11,13,15},{16,18,20,22},{17,19,21,2..., dimensions={0} | all-to-all | bytes 1048576 | tf_op jit(solution)/shard_map/all_to_all | solution.py:435
  80.3 0.7 reduce_sum.9
  (16 shorter events, 0.2 us)
Async XLA Ops:
  6.0 16.8 %all-to-all-start = ((f32[8,160,128]{2,1,0:T(8,128)}), f32[8,160,128]{2,1,0:T(8,128)S(1)}, u32[]{:S(2)}, u32[]{:S(2)}) async-start(f32[8,160,128]{2,1,0:T(8,128)} %get-tuple-element.16), calls=%async_computation | async-start | bytes 1310720 | tf_op jit(solution)/shard_map/all_to_all | solution.py:385
  12.4 8.7 %copy-start.4 = (f32[128,2]{0,1:T(2,128)S(1)}, f32[128,2]{0,1:T(2,128)}, u32[]{:S(2)}) copy-start(f32[128,2]{0,1:T(2,128)} %param.11) | copy-start | bytes 3076
  12.4 1.2 %copy-start.2 = (bf16[256,2048]{1,0:T(8,128)(2,1)S(1)}, bf16[256,2048]{1,0:T(8,128)(2,1)}, u32[]{:S(2)}) copy-start(bf16[256,2048]{1,0:T(8,128)(2,1)} %own_ref) | copy-start | bytes 3145732
  13.6 7.5 %copy-start.7 = (f32[2,256,128]{2,1,0:T(8,128)S(1)}, f32[2,256,128]{2,1,0:T(8,128)}, u32[]{:S(2)}) copy-start(f32[2,256,128]{2,1,0:T(8,128)} %get-tuple-element.17.keys_ref) | copy-start | bytes 786436
  13.6 7.5 %copy-start.8 = (bf16[128,2,128]{2,1,0:T(2,128)(2,1)S(1)}, bf16[128,2,128]{2,1,0:T(2,128)(2,1)}, u32[]{:S(2)}) copy-start(bf16[128,2,128]{2,1,0:T(2,128)(2,1)} %param.7) | copy-start | bytes 196612
  15.1 38.6 %collective-permute-start = (f32[256,2048]{1,0:T(8,128)}, f32[256,2048]{1,0:T(8,128)S(1)}, u32[]{:S(2)}, u32[]{:S(2)}) collective-permute-start(f32[256,2048]{1,0:T(8,128)} %widen.1), channel_id=1, source_target_pairs={{0,1},{1,0},{2,3},{3,2},{4,5},{5,4},{6,7},{7,6},{8,9},{9,8},{10,11... | collective-permute-start | bytes 6291464 | tf_op jit(solution)/shard_map/ppermute | solution.py:388
  21.1 1.0 %copy-start.6 = (f32[2,256,256]{2,1,0:T(8,128)S(1)}, f32[2,256,256]{2,1,0:T(8,128)}, u32[]{:S(2)}) copy-start(f32[2,256,256]{2,1,0:T(8,128)} %get-tuple-element.18.solved_ref) | copy-start | bytes 1572868
  47.6 11.6 %all-to-all-start.1 = ((f32[8,32,128]{2,1,0:T(8,128)}), f32[8,32,128]{2,1,0:T(8,128)S(1)}, u32[]{:S(2)}, u32[]{:S(2)}) async-start(f32[8,32,128]{2,1,0:T(8,128)} %start_states.1), calls=%async_computation.1 | async-start | bytes 262144 | tf_op jit(solution)/shard_map/all_to_all | solution.py:423
  53.7 1.3 %copy-start = (f32[256,2048]{1,0:T(8,128)}, f32[256,2048]{1,0:T(8,128)S(1)}, u32[]{:S(2)}) copy-start(f32[256,2048]{1,0:T(8,128)S(1)} %collective-permute-done.other_ref) | copy-start | bytes 6291460
  55.0 1.6 %copy-start.1 = (f32[256,2048]{1,0:T(8,128)S(1)}, f32[256,2048]{1,0:T(8,128)}, u32[]{:S(2)}) copy-start(f32[256,2048]{1,0:T(8,128)} %copy-done) | copy-start | bytes 6291460
  56.6 1.2 %copy-start.3 = (bf16[256,2048]{1,0:T(8,128)(2,1)S(1)}, bf16[256,2048]{1,0:T(8,128)(2,1)}, u32[]{:S(2)}) copy-start(bf16[256,2048]{1,0:T(8,128)(2,1)} %own_ref) | copy-start | bytes 3145732
  57.8 1.3 %copy-start.5 = (f32[2,128]{1,0:T(2,128)S(1)}, f32[2,128]{1,0:T(2,128)}, u32[]{:S(2)}) copy-start(f32[2,128]{1,0:T(2,128)} %gain_ref.1) | copy-start | bytes 3076

commit v5 on v4

--- a/solution.py
+++ b/solution.py
@@ -301,25 +301,39 @@
     total_ref[...] = runs[count - 1]
 
 
-def pair_kernel(width, pair_ref, total_ref):
-    total_ref[...] = compose(pair_ref[0], pair_ref[1], width)
-
-
-def write_kernel(width, pair_ref, write_ref):
-    write_ref[...] = dot(pair_ref[0, width:], pair_ref[1, :width]) + pair_ref[1, width:]
-
-
-def start_kernel(width, place_ref, pair_ref, quad_ref, far_ref, prefix_ref, state_ref):
+def in_order(place, own, arrived):
+    is_first = place % 2 == 0
+    return jnp.where(is_first, own, arrived), jnp.where(is_first, arrived, own)
+
+
+def first_kernel(width, place_ref, own_ref, arrived_ref, write_ref):
+    earlier, later = in_order(place_ref[0], own_ref[...], arrived_ref[...])
+    write_ref[...] = dot(earlier[width:], later[:width]) + later[width:]
+
+
+def write_kernel(width, place_ref, state_ref, own_ref, arrived_ref, write_ref):
+    earlier, later = in_order(place_ref[0], own_ref[...], arrived_ref[...])
+    middle = dot(state_ref[...], earlier[:width]) + earlier[width:]
+    write_ref[...] = dot(middle, later[:width]) + later[width:]
+
+
+def start_kernel(width, place_ref, own_ref, *refs):
+    swap_refs, state_refs, prefix_ref, out_ref = refs[:4], refs[4:7], refs[7], refs[8]
     place = place_ref[0]
-    state = jnp.where(place >= 4, far_ref[0], 0.0)
-    moved = dot(state, quad_ref[0, :width]) + quad_ref[0, width:]
-    state = jnp.where((place // 2) % 2 == 1, moved, state)
-    moved = dot(state, pair_ref[0, :width]) + pair_ref[0, width:]
+    arrived = swap_refs[0][...]
+    for ref in swap_refs[1:]:
+        arrived = arrived + ref[...]
+    state = state_refs[0][...] + state_refs[1][...] + state_refs[2][...]
+    moved = dot(state, arrived[:width]) + arrived[width:]
     state = jnp.where(place % 2 == 1, moved, state)
-    state_ref[0] = state
+    out_ref[0] = state
     parts = halves(state)
     for i in range(prefix_ref.shape[0]):
-        state_ref[i + 1] = dot_halves(parts, halves(prefix_ref[i, :width])) + prefix_ref[i, width:]
+        out_ref[i + 1] = dot_halves(parts, halves(prefix_ref[i, :width])) + prefix_ref[i, width:]
+
+
+def copy_kernel(in_ref, _, out_ref):
+    out_ref[...] = in_ref[...]
 
 
 def hidden_kernel(heads, own_ref, through_ref, state_ref, gain_ref, hidden_ref):
@@ -406,20 +420,35 @@
         (array(GROUP - 1, part_rows, width), array(part_rows, width)),
         "group_scan",
     )(parts)
-    pair = lax.all_gather(total, "ctx", axis_index_groups=pairs(8))
-    total = call(functools.partial(pair_kernel, width), array(part_rows, width), "pair_total")(pair)
-    quad = lax.all_gather(total, "ctx", axis_index_groups=pairs(16))
-    write = call(
-        functools.partial(write_kernel, width), array(part_rows - width, width), "half_write"
-    )(quad)
-    far = lax.all_gather(write, "ctx", axis_index_groups=pairs(48))
+    quarter = ctx // 4
+    group = [[g * quarter + i for i in range(quarter)] for g in range(4)]
+
     place = (lax.axis_index("ctx") // GROUP).astype(jnp.int32).reshape(1)
+    state_shape = array(part_rows - width, width)
+    swapped, arrived, offered = [], [], total
+    for g in range(4):
+        swapped.append(lax.ppermute(offered, "ctx", [(i, i ^ GROUP) for i in group[g]]))
+        if g == 0:
+            write = call(
+                functools.partial(first_kernel, width), state_shape, "first_write", in_specs=[smem, vmem, vmem]
+            )(place, total, swapped[0])
+        elif g < 3:
+            write = call(
+                functools.partial(write_kernel, width),
+                state_shape,
+                "next_write",
+                in_specs=[smem, vmem, vmem, vmem],
+            )(place, arrived[-1], total, swapped[g])
+        if g < 3:
+            came = lax.ppermute(write, "ctx", list(zip(group[g], group[g + 1])))
+            arrived.append(call(copy_kernel, state_shape, "state", flops=10**9)(came, came))
+            offered = call(copy_kernel, array(part_rows, width), "offer")(total, write)
     starts = call(
         functools.partial(start_kernel, width),
         array(GROUP, part_rows - width, width),
         "start_states",
-        in_specs=[smem, vmem, vmem, vmem, vmem],
-    )(place, pair, quad, far, prefix)
+        in_specs=[smem] + [vmem] * 9,
+    )(place, total, *swapped, *arrived, prefix)
     states = lax.all_to_all(starts, "ctx", 0, 0, axis_index_groups=inner)
     hidden = call(
         functools.partial(hidden_kernel, heads), array(tokens, heads * width), "hidden"

time: 81.5 us -> 74 us (0.908)
  the two profiles are of different devices: /device:TPU:1 before, /device:TPU:448 now
where the time goes in v5:
time: 74 us; the launch traced here: 73.4 us
  waiting for transfers between devices  20.1 us (27%)
  starting transfers between devices  18.9 us (26%)
  blocking collectives  15.9 us (21%)
  Pallas kernels  11.6 us (16%)
  local copies, waits for them, and re-layouts  6.02 us (8%)
    all_to_all x1, blocking collectives, per_device(): lax.all_to_all(sums.reshape(spread // 2, tokens // spread, columns), 'hea...  13.9 us
    ppermute x3, waiting for transfers between devices, per_device(): came = lax.ppermute(write, 'ctx', list(zip(group[g], group[g + 1])))  13.2 us
    unnamed x22, local copies, waits for them, and re-layouts  6.02 us
    pallas_call x1, Pallas kernels, local_call(): pl.pallas_call(functools.partial(local_kernel, heads), out_shape=(jax.Sha...  5.97 us
    ppermute x4, starting transfers between devices, per_device(): lax.ppermute(offered, 'ctx', [(i, i ^ GROUP) for i in group[g]])  5.35 us
    all_to_all x1, starting transfers between devices, per_device(): parts = lax.all_to_all(msg, 'ctx', 0, 0, axis_index_groups=inner)  4.94 us
    all_to_all x1, waiting for transfers between devices, per_device(): parts = lax.all_to_all(msg, 'ctx', 0, 0, axis_index_groups=inner)  4.72 us
    all_to_all x1, starting transfers between devices, per_device(): states = lax.all_to_all(starts, 'ctx', 0, 0, axis_index_groups=inner)  4.07 us
  transfers between devices with their start and end apart: 10, of which 3 were waited for; matrix products, arithmetic and copies ran while one was open for 0% of the time, Pallas kernels for 7%

profile of v5, /device:TPU:448, one launch (start us, length us, event | category | flops | bytes accessed | tf_op | source)
XLA Modules:
  0.0 73.4 jit_solution(7455841853528789632)
XLA Ops:
  0.0 6.0 %local_chunk.1 = (f32[8,160,128]{2,1,0:T(8,128)}, f32[2,256,256]{2,1,0:T(8,128)}, f32[2,256,128]{2,1,0:T(8,128)}) custom-call(bf16[512,128]{1,0:T(8,128)(2,1)} %bitcast.18, bf16[512,128]{1,0:T(8,128)(2,1)} %bitcast.19, f32[2,128]{1,0:T(2,128)} %bitcast.15, f32[4,128]{1,0:T(4,128)} %bitcast.20), custom_call_target="tpu_custom_call" | custom-call | tf_op jit(solution)/shard_map/local_chunk/pallas_call | solution.py:218
  6.0 4.9 %all-to-all-start = ((f32[8,160,128]{2,1,0:T(8,128)}), f32[8,160,128]{2,1,0:T(8,128)S(1)}, u32[]{:S(2)}, u32[]{:S(2)}) async-start(f32[8,160,128]{2,1,0:T(8,128)} %get-tuple-element.16), calls=%async_computation | async-start | bytes 1310720 | tf_op jit(solution)/shard_map/all_to_all | solution.py:399
  10.9 1.2 %copy-done.2 = bf16[256,2048]{1,0:T(8,128)(2,1)S(1)} copy-done((bf16[256,2048]{1,0:T(8,128)(2,1)S(1)}, bf16[256,2048]{1,0:T(8,128)(2,1)}, u32[]{:S(2)}) %copy-start.2) | copy-done | bytes 1048600
  12.2 1.5 %widen.1 = f32[256,2048]{1,0:T(8,128)} custom-call(bf16[256,2048]{1,0:T(8,128)(2,1)S(1)} %copy-done.2), custom_call_target="tpu_custom_call" | custom-call | flops 1000000000 | bytes 1048576 | tf_op jit(solution)/shard_map/widen/pallas_call | solution.py:401
  13.6 1.9 %collective-permute-start.7 = (f32[256,2048]{1,0:T(8,128)}, f32[256,2048]{1,0:T(8,128)S(1)}, u32[]{:S(2)}, u32[]{:S(2)}) collective-permute-start(f32[256,2048]{1,0:T(8,128)} %widen.1), channel_id=1, source_target_pairs={{0,1},{1,0},{2,3},{3,2},{4,5},{5,4},{6,7},{7,6},{8,9},{9,8},{10,11... | collective-permute-start | bytes 6291464 | tf_op jit(solution)/shard_map/ppermute | solution.py:402
  16.9 4.7 %all-to-all-done.parts_ref = f32[8,160,128]{2,1,0:T(8,128)S(1)} async-done(((f32[8,160,128]{2,1,0:T(8,128)}), f32[8,160,128]{2,1,0:T(8,128)S(1)}, u32[]{:S(2)}, u32[]{:S(2)}) %all-to-all-start) | async-done | bytes 655392 | tf_op jit(solution)/shard_map/all_to_all | solution.py:399
  21.6 0.7 group_scan.1
  22.2 0.7 collective-permute-start
  23.1 0.7 collective-permute-start.2
  23.8 0.7 collective-permute-start.1
  24.8 0.7 collective-permute-start.4
  25.4 0.7 collective-permute-start.3
  26.4 1.3 %collective-permute-start.6 = (f32[32,128]{1,0:T(8,128)S(1)}, f32[32,128]{1,0:T(8,128)S(1)}, u32[]{:S(2)}, u32[]{:S(2)}) collective-permute-start(f32[32,128]{1,0:T(8,128)S(1)} %next_write.3._), channel_id=1, source_target_pairs={{256,384},{264,392},{272,400},{280,408},{288,416},{296,424},{304,4... | collective-permute-start | bytes 49160 | tf_op jit(solution)/shard_map/ppermute | solution.py:443
  27.7 3.4 %collective-permute-start.5 = (f32[160,128]{1,0:T(8,128)S(1)}, f32[160,128]{1,0:T(8,128)S(1)}, u32[]{:S(2)}, u32[]{:S(2)}) collective-permute-start(f32[160,128]{1,0:T(8,128)S(1)} %offer.5), channel_id=1, source_target_pairs={{384,448},{392,456},{400,464},{408,472},{416,480},{424,488},{432,4... | collective-permute-start | bytes 245768 | tf_op jit(solution)/shard_map/ppermute | solution.py:430
  31.1 13.2 %collective-permute-done.6.in_ref._ = f32[32,128]{1,0:T(8,128)S(1)} collective-permute-done((f32[32,128]{1,0:T(8,128)S(1)}, f32[32,128]{1,0:T(8,128)S(1)}, u32[]{:S(2)}, u32[]{:S(2)}) %collective-permute-start.6) | collective-permute-done | bytes 16416 | tf_op jit(solution)/shard_map/ppermute | solution.py:443
  44.3 1.1 %start_states.1 = f32[8,32,128]{2,1,0:T(8,128)} custom-call(s32[1]{0:T(128)} %bitcast.7.place_ref, f32[160,128]{1,0:T(8,128)S(1)} %get-tuple-element.24.own_ref.in_ref, f32[160,128]{1,0:T(8,128)S(1)} %collective-permute-done.arrived_ref.refs_0_, f32[160,128]{1,0:T(8,128)S(1)} %collective-permute-done.1.arrived_ref.refs_1_, ...), custom_call_target="tpu_custom_call" | custom-call | bytes 1048576 | tf_op jit(solution)/shard_map/start_states/pallas_call | solution.py:446
  45.4 4.1 %all-to-all-start.1 = ((f32[8,32,128]{2,1,0:T(8,128)}), f32[8,32,128]{2,1,0:T(8,128)S(1)}, u32[]{:S(2)}, u32[]{:S(2)}) async-start(f32[8,32,128]{2,1,0:T(8,128)} %start_states.1), calls=%async_computation.1 | async-start | bytes 262144 | tf_op jit(solution)/shard_map/all_to_all | solution.py:452
  49.5 1.3 %copy-done = f32[256,2048]{1,0:T(8,128)} copy-done((f32[256,2048]{1,0:T(8,128)}, f32[256,2048]{1,0:T(8,128)S(1)}, u32[]{:S(2)}) %copy-start) | copy-done | bytes 2097176
  50.8 1.6 %copy-done.1 = f32[256,2048]{1,0:T(8,128)S(1)} copy-done((f32[256,2048]{1,0:T(8,128)S(1)}, f32[256,2048]{1,0:T(8,128)}, u32[]{:S(2)}) %copy-start.1) | copy-done | bytes 2097176
  52.4 1.2 %copy-done.3 = bf16[256,2048]{1,0:T(8,128)(2,1)S(1)} copy-done((bf16[256,2048]{1,0:T(8,128)(2,1)S(1)}, bf16[256,2048]{1,0:T(8,128)(2,1)}, u32[]{:S(2)}) %copy-start.3) | copy-done | bytes 1048600
  53.9 2.1 %all-to-all-done.1 = f32[8,32,128]{2,1,0:T(8,128)S(1)} async-done(((f32[8,32,128]{2,1,0:T(8,128)}), f32[8,32,128]{2,1,0:T(8,128)S(1)}, u32[]{:S(2)}, u32[]{:S(2)}) %all-to-all-start.1) | async-done | bytes 131104 | tf_op jit(solution)/shard_map/all_to_all | solution.py:452
  56.4 2.0 %all-gather = f32[256,256]{1,0:T(8,128)S(1)} all-gather(f32[128,256]{1,0:T(8,128)S(1)} %hidden.1), channel_id=2, replica_groups={{0,1},{2,3},{4,5},{6,7},{8,9},{10,11},{12,13},{14,15},{16,17},{18,19},{..., dimensions={0}, use_global_device_ids=true | all-gather | bytes 393216 | tf_op jit(solution)/shard_map/all_gather | solution.py:456
  58.9 13.9 %all_to_all.15 = f32[4,16,2048]{2,1,0:T(8,128)S(1)} all-to-all(f32[4,16,2048]{2,1,0:T(8,128)S(1)} %bitcast.12), channel_id=1, replica_groups={{0,2,4,6},{1,3,5,7},{8,10,12,14},{9,11,13,15},{16,18,20,22},{17,19,21,2..., dimensions={0} | all-to-all | bytes 1048576 | tf_op jit(solution)/shard_map/all_to_all | solution.py:464
  72.8 0.7 reduce_sum.9
  (38 shorter events, 3.1 us)
Async XLA Ops:
  6.0 15.6 %all-to-all-start = ((f32[8,160,128]{2,1,0:T(8,128)}), f32[8,160,128]{2,1,0:T(8,128)S(1)}, u32[]{:S(2)}, u32[]{:S(2)}) async-start(f32[8,160,128]{2,1,0:T(8,128)} %get-tuple-element.16), calls=%async_computation | async-start | bytes 1310720 | tf_op jit(solution)/shard_map/all_to_all | solution.py:399
  10.9 4.6 %copy-start.6 = (f32[128,2]{0,1:T(2,128)S(1)}, f32[128,2]{0,1:T(2,128)}, u32[]{:S(2)}) copy-start(f32[128,2]{0,1:T(2,128)} %param.11) | copy-start | bytes 3076
  10.9 1.2 %copy-start.2 = (bf16[256,2048]{1,0:T(8,128)(2,1)S(1)}, bf16[256,2048]{1,0:T(8,128)(2,1)}, u32[]{:S(2)}) copy-start(bf16[256,2048]{1,0:T(8,128)(2,1)} %own_ref) | copy-start | bytes 3145732
  12.2 3.4 %copy-start.8 = (f32[2,256,256]{2,1,0:T(8,128)S(1)}, f32[2,256,256]{2,1,0:T(8,128)}, u32[]{:S(2)}) copy-start(f32[2,256,256]{2,1,0:T(8,128)} %get-tuple-element.18.solved_ref) | copy-start | bytes 1572868
  12.2 3.4 %copy-start.9 = (f32[2,256,128]{2,1,0:T(8,128)S(1)}, f32[2,256,128]{2,1,0:T(8,128)}, u32[]{:S(2)}) copy-start(f32[2,256,128]{2,1,0:T(8,128)} %get-tuple-element.17.keys_ref) | copy-start | bytes 786436
  12.2 3.4 %copy-start.10 = (bf16[128,2,128]{2,1,0:T(2,128)(2,1)S(1)}, bf16[128,2,128]{2,1,0:T(2,128)(2,1)}, u32[]{:S(2)}) copy-start(bf16[128,2,128]{2,1,0:T(2,128)(2,1)} %param.7) | copy-start | bytes 196612
  13.6 35.8 %collective-permute-start.7 = (f32[256,2048]{1,0:T(8,128)}, f32[256,2048]{1,0:T(8,128)S(1)}, u32[]{:S(2)}, u32[]{:S(2)}) collective-permute-start(f32[256,2048]{1,0:T(8,128)} %widen.1), channel_id=1, source_target_pairs={{0,1},{1,0},{2,3},{3,2},{4,5},{5,4},{6,7},{7,6},{8,9},{9,8},{10,11... | collective-permute-start | bytes 6291464 | tf_op jit(solution)/shard_map/ppermute | solution.py:402
  16.2 0.6 copy-start.4
  22.2 0.7 collective-permute-start
  23.1 1.4 %collective-permute-start.2 = (f32[32,128]{1,0:T(8,128)S(1)}, f32[32,128]{1,0:T(8,128)S(1)}, u32[]{:S(2)}, u32[]{:S(2)}) collective-permute-start(f32[32,128]{1,0:T(8,128)S(1)} %first_write.1._), channel_id=1, source_target_pairs={{0,128},{8,136},{16,144},{24,152},{32,160},{40,168},{48,176},{56,1... | collective-permute-start | bytes 49160 | tf_op jit(solution)/shard_map/ppermute | solution.py:443
  23.8 0.7 collective-permute-start.1
  24.8 1.4 %collective-permute-start.4 = (f32[32,128]{1,0:T(8,128)S(1)}, f32[32,128]{1,0:T(8,128)S(1)}, u32[]{:S(2)}, u32[]{:S(2)}) collective-permute-start(f32[32,128]{1,0:T(8,128)S(1)} %next_write.2._), channel_id=1, source_target_pairs={{128,256},{136,264},{144,272},{152,280},{160,288},{168,296},{176,3... | collective-permute-start | bytes 49160 | tf_op jit(solution)/shard_map/ppermute | solution.py:443
  25.4 0.7 collective-permute-start.3
  26.4 17.9 %collective-permute-start.6 = (f32[32,128]{1,0:T(8,128)S(1)}, f32[32,128]{1,0:T(8,128)S(1)}, u32[]{:S(2)}, u32[]{:S(2)}) collective-permute-start(f32[32,128]{1,0:T(8,128)S(1)} %next_write.3._), channel_id=1, source_target_pairs={{256,384},{264,392},{272,400},{280,408},{288,416},{296,424},{304,4... | collective-permute-start | bytes 49160 | tf_op jit(solution)/shard_map/ppermute | solution.py:443
  27.7 16.6 %collective-permute-start.5 = (f32[160,128]{1,0:T(8,128)S(1)}, f32[160,128]{1,0:T(8,128)S(1)}, u32[]{:S(2)}, u32[]{:S(2)}) collective-permute-start(f32[160,128]{1,0:T(8,128)S(1)} %offer.5), channel_id=1, source_target_pairs={{384,448},{392,456},{400,464},{408,472},{416,480},{424,488},{432,4... | collective-permute-start | bytes 245768 | tf_op jit(solution)/shard_map/ppermute | solution.py:430
  45.4 10.6 %all-to-all-start.1 = ((f32[8,32,128]{2,1,0:T(8,128)}), f32[8,32,128]{2,1,0:T(8,128)S(1)}, u32[]{:S(2)}, u32[]{:S(2)}) async-start(f32[8,32,128]{2,1,0:T(8,128)} %start_states.1), calls=%async_computation.1 | async-start | bytes 262144 | tf_op jit(solution)/shard_map/all_to_all | solution.py:452
  49.5 1.3 %copy-start = (f32[256,2048]{1,0:T(8,128)}, f32[256,2048]{1,0:T(8,128)S(1)}, u32[]{:S(2)}) copy-start(f32[256,2048]{1,0:T(8,128)S(1)} %collective-permute-done.7.other_ref) | copy-start | bytes 6291460
  50.8 1.6 %copy-start.1 = (f32[256,2048]{1,0:T(8,128)S(1)}, f32[256,2048]{1,0:T(8,128)}, u32[]{:S(2)}) copy-start(f32[256,2048]{1,0:T(8,128)} %copy-done) | copy-start | bytes 6291460
  52.4 1.2 %copy-start.3 = (bf16[256,2048]{1,0:T(8,128)(2,1)S(1)}, bf16[256,2048]{1,0:T(8,128)(2,1)}, u32[]{:S(2)}) copy-start(bf16[256,2048]{1,0:T(8,128)(2,1)} %own_ref) | copy-start | bytes 3145732
  53.6 2.4 %copy-start.5 = (f32[128,256]{1,0:T(8,128)S(1)}, f32[128,256]{1,0:T(8,128)}, u32[]{:S(2)}) copy-start(f32[128,256]{1,0:T(8,128)} %copy-done.4) | copy-start | bytes 393220
  53.6 2.4 %copy-start.7 = (f32[2,128]{1,0:T(2,128)S(1)}, f32[2,128]{1,0:T(2,128)}, u32[]{:S(2)}) copy-start(f32[2,128]{1,0:T(2,128)} %gain_ref.1) | copy-start | bytes 3076

commit v6 on v5

--- a/solution.py
+++ b/solution.py
@@ -70,31 +70,30 @@
     return tuple(jnp.concatenate([piece] * count, axis=0) * mask for piece in halves(part))
 
 
+def small_inverses(lower, width):
+    lanes = 128
+    row = iota((width, lanes), 0)
+    lane = iota((width, lanes), 1)
+    tiles = []
+    for start in range(0, lower.shape[0], lanes):
+        part = jnp.zeros((width, lanes), F32)
+        for block in range(lanes // width):
+            first = start + block * width
+            part = jnp.where(lane // width == block, lower[first : first + width, start : start + lanes], part)
+        inverse = jnp.where(row == lane % width, 1.0, 0.0).astype(F32)
+        for column in range(width - 1):
+            factor = jnp.take_along_axis(part, lane - lane % width + column, axis=1)
+            inverse = inverse - factor * inverse[column : column + 1, :]
+        tiles.append(inverse)
+    return jnp.concatenate(tiles, axis=1)
+
+
 def inverse_blocks(lowers, stop):
     size = lowers[0].shape[0]
-    width = 8
-    lane = iota((width, size), 1)
-    row = iota((width, size), 0)
-    col = lane % width
+    width = 16
     rows = iota((size, size), 0)
     cols = iota((size, size), 1)
-    packed = []
-    for lower in lowers:
-        part = jnp.zeros((width, size), F32)
-        for block in range(size // width):
-            part = jnp.where(lane // width == block, lower[block * width : (block + 1) * width], part)
-        packed.append(part)
-    same = jnp.where(rows // width == cols // width, 1.0, 0.0).astype(BF16)
-    eye = jnp.where(row == col, 1.0, 0.0).astype(F32)
-    inverses = [eye - jnp.where(row // 2 == col // 2, part, 0.0) for part in packed]
-    count = size // width
-    for step in (2, 4):
-        below = (row // (2 * step) == col // (2 * step)) & (row // step != col // step)
-        corners = [halves(jnp.where(below, part, 0.0)) for part in packed]
-        inner = [dot_halves(c, blocks_of(t, count, same)) for c, t in zip(corners, inverses)]
-        inverses = [
-            t - dot_halves(halves(t), blocks_of(y, count, same)) for t, y in zip(inverses, inner)
-        ]
+    inverses = [small_inverses(lower, width) for lower in lowers]
     while width < stop:
         count = size // width
         lane = iota((width, size), 1) // width
@@ -262,24 +261,9 @@
         through_ref[:, lanes] = jnp.exp(cumul) * query - mixed[:, width:]
 
 
-def widen_kernel(in_ref, out_ref):
+def widen_kernel(in_ref, out_ref, copy_ref):
     out_ref[...] = in_ref[...].astype(F32)
-
-
-def weight_kernel(core_ref, own_ref, other_ref, both_ref):
-    rows = own_ref.shape[0]
-    other = other_ref[...].astype(BF16)
-    on_first = core_ref[0] == 0
-
-    @pl.when(on_first)
-    def _():
-        both_ref[:rows] = own_ref[...]
-        both_ref[rows:] = other
-
-    @pl.when(jnp.logical_not(on_first))
-    def _():
-        both_ref[:rows] = other
-        both_ref[rows:] = own_ref[...]
+    copy_ref[...] = in_ref[...]
 
 
 def compose(earlier, later, width):
@@ -346,15 +330,19 @@
         hidden_ref[:, lanes] = scaled.astype(BF16).astype(F32)
 
 
-def project_kernel(spread, core_ref, hidden_ref, weight_ref, out_ref):
+def project_kernel(spread, core_ref, hidden_ref, own_ref, other_ref, out_ref):
     share = hidden_ref.shape[1] // spread
+    on_first = core_ref[0] == 0
     kept = []
-    for i in range(0, spread, 2):
-        even = jnp.concatenate([hidden_ref[c, i * share : (i + 1) * share] for c in range(2)], axis=1)
-        odd = jnp.concatenate([hidden_ref[c, (i + 1) * share : (i + 2) * share] for c in range(2)], axis=1)
-        kept.append(jnp.where(core_ref[0] == 0, even, odd))
-    kept = jnp.concatenate(kept, axis=0).astype(BF16)
-    out_ref[...] = jnp.dot(kept, weight_ref[...], preferred_element_type=F32)
+    for core in range(2):
+        even = jnp.concatenate([hidden_ref[core, i * share : (i + 1) * share] for i in range(0, spread, 2)], axis=0)
+        odd = jnp.concatenate([hidden_ref[core, i * share : (i + 1) * share] for i in range(1, spread, 2)], axis=0)
+        kept.append(jnp.where(on_first, even, odd))
+    mine = jnp.where(on_first, kept[0], kept[1]).astype(BF16)
+    others = jnp.where(on_first, kept[1], kept[0]).astype(BF16)
+    out_ref[...] = jnp.dot(mine, own_ref[...], preferred_element_type=F32) + jnp.dot(
+        others, other_ref[...].astype(BF16), preferred_element_type=F32
+    )
 
 
 def per_device(queries, key_rows, value_rows, strengths, log_decay, norm_gain, out_weight):
@@ -396,17 +384,17 @@
         log_decay.T,
         strengths.transpose(1, 2, 0).reshape(2 * heads, tokens),
     )
+    place = (lax.axis_index("ctx") // GROUP).astype(jnp.int32).reshape(1)
+    msg, place, core = lax.optimization_barrier((msg, place, core))
     parts = lax.all_to_all(msg, "ctx", 0, 0, axis_index_groups=inner)
     late_weight, _ = lax.optimization_barrier((out_weight, solved))
-    wide = call(widen_kernel, array(*out_weight.shape), "widen", flops=10**9)(late_weight)
+    wide, held = call(
+        widen_kernel,
+        (array(*out_weight.shape), array(*out_weight.shape, dtype=BF16)),
+        "widen",
+        flops=10**9,
+    )(late_weight)
     other = lax.ppermute(wide, "head", [(i, i ^ 1) for i in range(spread)])
-    both = call(
-        weight_kernel,
-        array(2 * out_weight.shape[0], columns, dtype=BF16),
-        "chip_weight",
-        flops=10**9,
-        in_specs=[smem, vmem, vmem],
-    )(core, late_weight, other)
     own, through = call(
         functools.partial(own_kernel, heads),
         (array(tokens, heads * width), array(tokens, heads * width)),
@@ -423,7 +411,6 @@
     quarter = ctx // 4
     group = [[g * quarter + i for i in range(quarter)] for g in range(4)]
 
-    place = (lax.axis_index("ctx") // GROUP).astype(jnp.int32).reshape(1)
     state_shape = array(part_rows - width, width)
     swapped, arrived, offered = [], [], total
     for g in range(4):
@@ -458,8 +445,8 @@
         functools.partial(project_kernel, spread),
         array(tokens // 2, columns),
         "project",
-        in_specs=[smem, vmem, vmem],
-    )(core, hidden, both)
+        in_specs=[smem, vmem, vmem, vmem],
+    )(core, hidden, held, other)
     ring = [[i * 2 + c for i in range(spread // 2)] for c in range(2)]
     shares = lax.all_to_all(
         sums.reshape(spread // 2, tokens // spread, columns), "head", 0, 0, axis_index_groups=ring

time: 74 us -> 72.4 us (0.978)
  blocking collectives: 15.9 us -> 26.3 us
  starting transfers between devices: 18.9 us -> 14.8 us
  local copies, waits for them, and re-layouts: 6.02 us -> 2.22 us
  waiting for transfers between devices: 20.1 us -> 17.6 us
  Pallas kernels: 11.6 us -> 10.1 us
    all_to_all x0 -> x1, blocking collectives: none -> 10.5 us  [per_device(): states = lax.all_to_all(starts, 'ctx', 0, 0, axis_index_groups=inner)]
    all_to_all x1 -> x0, starting transfers between devices: 4.07 us -> none  [per_device(): states = lax.all_to_all(starts, 'ctx', 0, 0, axis_index_groups=inner)]
    unnamed x22 -> x16, local copies, waits for them, and re-layouts: 6.02 us -> 2.22 us
    all_to_all x1 -> x0, waiting for transfers between devices: 2.12 us -> none  [per_device(): states = lax.all_to_all(starts, 'ctx', 0, 0, axis_index_groups=inner)]
    pallas_call x2 -> x1, Pallas kernels: 1.76 us -> 1.55 us  [per_device(): call(widen_kernel, (array(*out_weight.shape), array(*out_weight.shape, dt...]
  transfers between devices with their start and end apart: 10 -> 9, of which waited for: 3 -> 2; matrix products, arithmetic and copies ran while one was open for 0% -> 0% of each run, Pallas kernels for 7% -> 6%
where the time goes in v6:
time: 72.4 us; the launch traced here: 71.9 us
  blocking collectives  26.3 us (36%)
  waiting for transfers between devices  17.6 us (24%)
  starting transfers between devices  14.8 us (20%)
  Pallas kernels  10.1 us (14%)
  local copies, waits for them, and re-layouts  2.22 us (3%)
    all_to_all x1, blocking collectives, per_device(): lax.all_to_all(sums.reshape(spread // 2, tokens // spread, columns), 'hea...  13.8 us
    ppermute x3, waiting for transfers between devices, per_device(): came = lax.ppermute(write, 'ctx', list(zip(group[g], group[g + 1])))  13.2 us
    all_to_all x1, blocking collectives, per_device(): states = lax.all_to_all(starts, 'ctx', 0, 0, axis_index_groups=inner)  10.5 us
    ppermute x4, starting transfers between devices, per_device(): lax.ppermute(offered, 'ctx', [(i, i ^ GROUP) for i in group[g]])  5.36 us
    pallas_call x1, Pallas kernels, local_call(): pl.pallas_call(functools.partial(local_kernel, heads), out_shape=(jax.Sha...  5.35 us
    all_to_all x1, starting transfers between devices, per_device(): parts = lax.all_to_all(msg, 'ctx', 0, 0, axis_index_groups=inner)  4.94 us
    all_to_all x1, waiting for transfers between devices, per_device(): parts = lax.all_to_all(msg, 'ctx', 0, 0, axis_index_groups=inner)  4.3 us
    ppermute x3, starting transfers between devices, per_device(): came = lax.ppermute(write, 'ctx', list(zip(group[g], group[g + 1])))  2.61 us
  transfers between devices with their start and end apart: 9, of which 2 were waited for; matrix products, arithmetic and copies ran while one was open for 0% of the time, Pallas kernels for 6%

profile of v6, /device:TPU:448, one launch (start us, length us, event | category | flops | bytes accessed | tf_op | source)
XLA Modules:
  0.0 71.9 jit_solution(9136624302591652149)
XLA Ops:
  0.0 5.4 %local_chunk.1 = (f32[8,160,128]{2,1,0:T(8,128)}, f32[2,256,256]{2,1,0:T(8,128)}, f32[2,256,128]{2,1,0:T(8,128)}) custom-call(bf16[512,128]{1,0:T(8,128)(2,1)} %bitcast.18, bf16[512,128]{1,0:T(8,128)(2,1)} %bitcast.19, f32[2,128]{1,0:T(2,128)} %bitcast.15, f32[4,128]{1,0:T(4,128)} %bitcast.20), custom_call_target="tpu_custom_call" | custom-call | tf_op jit(solution)/shard_map/local_chunk/pallas_call | solution.py:217
  5.4 4.9 %all-to-all-start = ((f32[8,160,128]{2,1,0:T(8,128)}), f32[8,160,128]{2,1,0:T(8,128)S(1)}, u32[]{:S(2)}, u32[]{:S(2)}) async-start(f32[8,160,128]{2,1,0:T(8,128)} %get-tuple-element.23), calls=%async_computation | async-start | bytes 1310720 | tf_op jit(solution)/shard_map/all_to_all | solution.py:389
  10.3 1.2 %copy-done.4 = bf16[256,2048]{1,0:T(8,128)(2,1)S(1)} copy-done((bf16[256,2048]{1,0:T(8,128)(2,1)S(1)}, bf16[256,2048]{1,0:T(8,128)(2,1)}, u32[]{:S(2)}) %copy-start.4) | copy-done | bytes 1048600
  11.6 1.5 %widen.1 = (f32[256,2048]{1,0:T(8,128)}, bf16[256,2048]{1,0:T(8,128)(2,1)S(1)}) custom-call(bf16[256,2048]{1,0:T(8,128)(2,1)S(1)} %copy-done.4), custom_call_target="tpu_custom_call" | custom-call | flops 1000000000 | bytes 1048576 | tf_op jit(solution)/shard_map/widen/pallas_call | solution.py:391
  13.1 1.0 %copy-done = bf16[256,2048]{1,0:T(8,128)(2,1)} copy-done((bf16[256,2048]{1,0:T(8,128)(2,1)}, bf16[256,2048]{1,0:T(8,128)(2,1)S(1)}, u32[]{:S(2)}) %copy-start) | copy-done | bytes 1048600
  14.1 1.9 %collective-permute-start.7 = (f32[256,2048]{1,0:T(8,128)}, f32[256,2048]{1,0:T(8,128)S(1)}, u32[]{:S(2)}, u32[]{:S(2)}) collective-permute-start(f32[256,2048]{1,0:T(8,128)} %get-tuple-element.36), channel_id=1, source_target_pairs={{0,1},{1,0},{2,3},{3,2},{4,5},{5,4},{6,7},{7,6},{8,9},{9,8},{10,11... | collective-permute-start | bytes 6291464 | tf_op jit(solution)/shard_map/ppermute | solution.py:397
  16.0 0.6 own_outputs.1
  16.6 4.3 %all-to-all-done.parts_ref = f32[8,160,128]{2,1,0:T(8,128)S(1)} async-done(((f32[8,160,128]{2,1,0:T(8,128)}), f32[8,160,128]{2,1,0:T(8,128)S(1)}, u32[]{:S(2)}, u32[]{:S(2)}) %all-to-all-start) | async-done | bytes 655392 | tf_op jit(solution)/shard_map/all_to_all | solution.py:389
  21.0 0.6 group_scan.1
  21.6 0.7 collective-permute-start
  22.4 0.7 collective-permute-start.2
  23.1 0.7 collective-permute-start.1
  24.1 0.7 collective-permute-start.4
  24.8 0.7 collective-permute-start.3
  25.8 1.3 %collective-permute-start.6 = (f32[32,128]{1,0:T(8,128)S(1)}, f32[32,128]{1,0:T(8,128)S(1)}, u32[]{:S(2)}, u32[]{:S(2)}) collective-permute-start(f32[32,128]{1,0:T(8,128)S(1)} %next_write.3._), channel_id=1, source_target_pairs={{256,384},{264,392},{272,400},{280,408},{288,416},{296,424},{304,4... | collective-permute-start | bytes 49160 | tf_op jit(solution)/shard_map/ppermute | solution.py:430
  27.1 3.4 %collective-permute-start.5 = (f32[160,128]{1,0:T(8,128)S(1)}, f32[160,128]{1,0:T(8,128)S(1)}, u32[]{:S(2)}, u32[]{:S(2)}) collective-permute-start(f32[160,128]{1,0:T(8,128)S(1)} %offer.5), channel_id=1, source_target_pairs={{384,448},{392,456},{400,464},{408,472},{416,480},{424,488},{432,4... | collective-permute-start | bytes 245768 | tf_op jit(solution)/shard_map/ppermute | solution.py:417
  30.5 13.2 %collective-permute-done.6.in_ref._ = f32[32,128]{1,0:T(8,128)S(1)} collective-permute-done((f32[32,128]{1,0:T(8,128)S(1)}, f32[32,128]{1,0:T(8,128)S(1)}, u32[]{:S(2)}, u32[]{:S(2)}) %collective-permute-start.6) | collective-permute-done | bytes 16416 | tf_op jit(solution)/shard_map/ppermute | solution.py:430
  43.7 0.4 start_states.1
  44.1 10.5 %all_to_all.15 = f32[8,32,128]{2,1,0:T(8,128)S(1)} all-to-all(f32[8,32,128]{2,1,0:T(8,128)S(1)} %start_states.1), channel_id=1, replica_groups={{0,8,16,24,32,40,48,56},{64,72,80,88,96,104,112,120},{128,136,144,152,1..., dimensions={0} | all-to-all | bytes 262144 | tf_op jit(solution)/shard_map/all_to_all | solution.py:439
  54.6 0.3 hidden.1
  55.0 2.0 %all-gather = f32[256,256]{1,0:T(8,128)S(1)} all-gather(f32[128,256]{1,0:T(8,128)S(1)} %hidden.1), channel_id=2, replica_groups={{0,1},{2,3},{4,5},{6,7},{8,9},{10,11},{12,13},{14,15},{16,17},{18,19},{..., dimensions={0}, use_global_device_ids=true | all-gather | bytes 393216 | tf_op jit(solution)/shard_map/all_gather | solution.py:443
  57.0 0.5 project.1
  57.5 13.8 %all_to_all.16 = f32[4,16,2048]{2,1,0:T(8,128)S(1)} all-to-all(f32[4,16,2048]{2,1,0:T(8,128)S(1)} %bitcast.12), channel_id=1, replica_groups={{0,2,4,6},{1,3,5,7},{8,10,12,14},{9,11,13,15},{16,18,20,22},{17,19,21,2..., dimensions={0} | all-to-all | bytes 1048576 | tf_op jit(solution)/shard_map/all_to_all | solution.py:451
  71.3 0.7 reduce_sum.9
  (30 shorter events, 0.8 us)
Async XLA Ops:
  5.4 15.6 %all-to-all-start = ((f32[8,160,128]{2,1,0:T(8,128)}), f32[8,160,128]{2,1,0:T(8,128)S(1)}, u32[]{:S(2)}, u32[]{:S(2)}) async-start(f32[8,160,128]{2,1,0:T(8,128)} %get-tuple-element.23), calls=%async_computation | async-start | bytes 1310720 | tf_op jit(solution)/shard_map/all_to_all | solution.py:389
  10.3 5.7 %copy-start.2 = (f32[128,2]{0,1:T(2,128)S(1)}, f32[128,2]{0,1:T(2,128)}, u32[]{:S(2)}) copy-start(f32[128,2]{0,1:T(2,128)} %param.11) | copy-start | bytes 3076
  10.3 1.2 %copy-start.4 = (bf16[256,2048]{1,0:T(8,128)(2,1)S(1)}, bf16[256,2048]{1,0:T(8,128)(2,1)}, u32[]{:S(2)}) copy-start(bf16[256,2048]{1,0:T(8,128)(2,1)} %in_ref) | copy-start | bytes 3145732
  11.5 4.4 %copy-start.5 = (f32[2,256,256]{2,1,0:T(8,128)S(1)}, f32[2,256,256]{2,1,0:T(8,128)}, u32[]{:S(2)}) copy-start(f32[2,256,256]{2,1,0:T(8,128)} %get-tuple-element.25.solved_ref) | copy-start | bytes 1572868
  11.5 4.5 %copy-start.6 = (f32[2,256,128]{2,1,0:T(8,128)S(1)}, f32[2,256,128]{2,1,0:T(8,128)}, u32[]{:S(2)}) copy-start(f32[2,256,128]{2,1,0:T(8,128)} %get-tuple-element.24.keys_ref) | copy-start | bytes 786436
  11.5 4.5 %copy-start.7 = (bf16[128,2,128]{2,1,0:T(2,128)(2,1)S(1)}, bf16[128,2,128]{2,1,0:T(2,128)(2,1)}, u32[]{:S(2)}) copy-start(bf16[128,2,128]{2,1,0:T(2,128)(2,1)} %param.7) | copy-start | bytes 196612
  13.1 1.0 %copy-start = (bf16[256,2048]{1,0:T(8,128)(2,1)}, bf16[256,2048]{1,0:T(8,128)(2,1)S(1)}, u32[]{:S(2)}) copy-start(bf16[256,2048]{1,0:T(8,128)(2,1)S(1)} %get-tuple-element.35.own_ref) | copy-start | bytes 3145732
  14.1 42.9 %collective-permute-start.7 = (f32[256,2048]{1,0:T(8,128)}, f32[256,2048]{1,0:T(8,128)S(1)}, u32[]{:S(2)}, u32[]{:S(2)}) collective-permute-start(f32[256,2048]{1,0:T(8,128)} %get-tuple-element.36), channel_id=1, source_target_pairs={{0,1},{1,0},{2,3},{3,2},{4,5},{5,4},{6,7},{7,6},{8,9},{9,8},{10,11... | collective-permute-start | bytes 6291464 | tf_op jit(solution)/shard_map/ppermute | solution.py:397
  21.6 0.7 collective-permute-start
  22.4 1.4 %collective-permute-start.2 = (f32[32,128]{1,0:T(8,128)S(1)}, f32[32,128]{1,0:T(8,128)S(1)}, u32[]{:S(2)}, u32[]{:S(2)}) collective-permute-start(f32[32,128]{1,0:T(8,128)S(1)} %first_write.1._), channel_id=1, source_target_pairs={{0,128},{8,136},{16,144},{24,152},{32,160},{40,168},{48,176},{56,1... | collective-permute-start | bytes 49160 | tf_op jit(solution)/shard_map/ppermute | solution.py:430
  23.1 0.7 collective-permute-start.1
  24.1 1.4 %collective-permute-start.4 = (f32[32,128]{1,0:T(8,128)S(1)}, f32[32,128]{1,0:T(8,128)S(1)}, u32[]{:S(2)}, u32[]{:S(2)}) collective-permute-start(f32[32,128]{1,0:T(8,128)S(1)} %next_write.2._), channel_id=1, source_target_pairs={{128,256},{136,264},{144,272},{152,280},{160,288},{168,296},{176,3... | collective-permute-start | bytes 49160 | tf_op jit(solution)/shard_map/ppermute | solution.py:430
  24.8 0.7 collective-permute-start.3
  25.8 17.9 %collective-permute-start.6 = (f32[32,128]{1,0:T(8,128)S(1)}, f32[32,128]{1,0:T(8,128)S(1)}, u32[]{:S(2)}, u32[]{:S(2)}) collective-permute-start(f32[32,128]{1,0:T(8,128)S(1)} %next_write.3._), channel_id=1, source_target_pairs={{256,384},{264,392},{272,400},{280,408},{288,416},{296,424},{304,4... | collective-permute-start | bytes 49160 | tf_op jit(solution)/shard_map/ppermute | solution.py:430
  27.1 27.5 %copy-start.3 = (f32[2,128]{1,0:T(2,128)S(1)}, f32[2,128]{1,0:T(2,128)}, u32[]{:S(2)}) copy-start(f32[2,128]{1,0:T(2,128)} %gain_ref.1) | copy-start | bytes 3076
  27.1 16.6 %collective-permute-start.5 = (f32[160,128]{1,0:T(8,128)S(1)}, f32[160,128]{1,0:T(8,128)S(1)}, u32[]{:S(2)}, u32[]{:S(2)}) collective-permute-start(f32[160,128]{1,0:T(8,128)S(1)} %offer.5), channel_id=1, source_target_pairs={{384,448},{392,456},{400,464},{408,472},{416,480},{424,488},{432,4... | collective-permute-start | bytes 245768 | tf_op jit(solution)/shard_map/ppermute | solution.py:417
  43.7 13.3 %copy-start.1 = (bf16[256,2048]{1,0:T(8,128)(2,1)S(1)}, bf16[256,2048]{1,0:T(8,128)(2,1)}, u32[]{:S(2)}) copy-start(bf16[256,2048]{1,0:T(8,128)(2,1)} %copy-done) | copy-start | bytes 3145732

commit v7 on v6

--- a/solution.py
+++ b/solution.py
@@ -427,7 +427,7 @@
                 in_specs=[smem, vmem, vmem, vmem],
             )(place, arrived[-1], total, swapped[g])
         if g < 3:
-            came = lax.ppermute(write, "ctx", list(zip(group[g], group[g + 1])))
+            came = lax.ppermute(write, "ctx", [(i, j ^ GROUP if g == 2 else j) for i, j in zip(group[g], group[g + 1])])
             arrived.append(call(copy_kernel, state_shape, "state", flops=10**9)(came, came))
             offered = call(copy_kernel, array(part_rows, width), "offer")(total, write)
     starts = call(

time: 72.4 us -> 71.5 us (0.988)
  the two profiles are of different devices: /device:TPU:448 before, /device:TPU:384 now
where the time goes in v7:
time: 71.5 us; the launch traced here: 71 us
  blocking collectives  26.3 us (37%)
  waiting for transfers between devices  16.7 us (23%)
  starting transfers between devices  14.8 us (21%)
  Pallas kernels  10.1 us (14%)
  local copies, waits for them, and re-layouts  2.22 us (3%)
    all_to_all x1, blocking collectives, per_device(): lax.all_to_all(sums.reshape(spread // 2, tokens // spread, columns), 'hea...  13.8 us
    ppermute x3, waiting for transfers between devices, per_device(): lax.ppermute(write, 'ctx', [(i, j ^ GROUP if g == 2 else j) for i, j in z...  12.3 us
    all_to_all x1, blocking collectives, per_device(): states = lax.all_to_all(starts, 'ctx', 0, 0, axis_index_groups=inner)  10.5 us
    ppermute x4, starting transfers between devices, per_device(): lax.ppermute(offered, 'ctx', [(i, i ^ GROUP) for i in group[g]])  5.38 us
    pallas_call x1, Pallas kernels, local_call(): pl.pallas_call(functools.partial(local_kernel, heads), out_shape=(jax.Sha...  5.36 us
    all_to_all x1, starting transfers between devices, per_device(): parts = lax.all_to_all(msg, 'ctx', 0, 0, axis_index_groups=inner)  4.93 us
    all_to_all x1, waiting for transfers between devices, per_device(): parts = lax.all_to_all(msg, 'ctx', 0, 0, axis_index_groups=inner)  4.31 us
    ppermute x3, starting transfers between devices, per_device(): lax.ppermute(write, 'ctx', [(i, j ^ GROUP if g == 2 else j) for i, j in z...  2.61 us
  transfers between devices with their start and end apart: 9, of which 2 were waited for; matrix products, arithmetic and copies ran while one was open for 0% of the time, Pallas kernels for 6%

profile of v7, /device:TPU:384, one launch (start us, length us, event | category | flops | bytes accessed | tf_op | source)
XLA Modules:
  0.0 71.0 jit_solution(5402207381553639289)
XLA Ops:
  0.0 5.4 %local_chunk.1 = (f32[8,160,128]{2,1,0:T(8,128)}, f32[2,256,256]{2,1,0:T(8,128)}, f32[2,256,128]{2,1,0:T(8,128)}) custom-call(bf16[512,128]{1,0:T(8,128)(2,1)} %bitcast.18, bf16[512,128]{1,0:T(8,128)(2,1)} %bitcast.19, f32[2,128]{1,0:T(2,128)} %bitcast.15, f32[4,128]{1,0:T(4,128)} %bitcast.20), custom_call_target="tpu_custom_call" | custom-call | tf_op jit(solution)/shard_map/local_chunk/pallas_call | solution.py:217
  5.4 4.9 %all-to-all-start = ((f32[8,160,128]{2,1,0:T(8,128)}), f32[8,160,128]{2,1,0:T(8,128)S(1)}, u32[]{:S(2)}, u32[]{:S(2)}) async-start(f32[8,160,128]{2,1,0:T(8,128)} %get-tuple-element.23), calls=%async_computation | async-start | bytes 1310720 | tf_op jit(solution)/shard_map/all_to_all | solution.py:389
  10.3 1.2 %copy-done.4 = bf16[256,2048]{1,0:T(8,128)(2,1)S(1)} copy-done((bf16[256,2048]{1,0:T(8,128)(2,1)S(1)}, bf16[256,2048]{1,0:T(8,128)(2,1)}, u32[]{:S(2)}) %copy-start.4) | copy-done | bytes 1048600
  11.5 1.5 %widen.1 = (f32[256,2048]{1,0:T(8,128)}, bf16[256,2048]{1,0:T(8,128)(2,1)S(1)}) custom-call(bf16[256,2048]{1,0:T(8,128)(2,1)S(1)} %copy-done.4), custom_call_target="tpu_custom_call" | custom-call | flops 1000000000 | bytes 1048576 | tf_op jit(solution)/shard_map/widen/pallas_call | solution.py:391
  13.1 1.0 %copy-done = bf16[256,2048]{1,0:T(8,128)(2,1)} copy-done((bf16[256,2048]{1,0:T(8,128)(2,1)}, bf16[256,2048]{1,0:T(8,128)(2,1)S(1)}, u32[]{:S(2)}) %copy-start) | copy-done | bytes 1048600
  14.1 1.9 %collective-permute-start.7 = (f32[256,2048]{1,0:T(8,128)}, f32[256,2048]{1,0:T(8,128)S(1)}, u32[]{:S(2)}, u32[]{:S(2)}) collective-permute-start(f32[256,2048]{1,0:T(8,128)} %get-tuple-element.36), channel_id=1, source_target_pairs={{0,1},{1,0},{2,3},{3,2},{4,5},{5,4},{6,7},{7,6},{8,9},{9,8},{10,11... | collective-permute-start | bytes 6291464 | tf_op jit(solution)/shard_map/ppermute | solution.py:397
  16.0 0.6 own_outputs.1
  16.6 4.3 %all-to-all-done.parts_ref = f32[8,160,128]{2,1,0:T(8,128)S(1)} async-done(((f32[8,160,128]{2,1,0:T(8,128)}), f32[8,160,128]{2,1,0:T(8,128)S(1)}, u32[]{:S(2)}, u32[]{:S(2)}) %all-to-all-start) | async-done | bytes 655392 | tf_op jit(solution)/shard_map/all_to_all | solution.py:389
  21.0 0.6 group_scan.1
  21.6 0.7 collective-permute-start
  22.4 0.7 collective-permute-start.2
  23.1 0.7 collective-permute-start.1
  24.1 0.7 collective-permute-start.4
  24.8 0.7 collective-permute-start.3
  25.8 1.3 %collective-permute-start.6 = (f32[32,128]{1,0:T(8,128)S(1)}, f32[32,128]{1,0:T(8,128)S(1)}, u32[]{:S(2)}, u32[]{:S(2)}) collective-permute-start(f32[32,128]{1,0:T(8,128)S(1)} %next_write.3._), channel_id=1, source_target_pairs={{256,448},{264,456},{272,464},{280,472},{288,480},{296,488},{304,4... | collective-permute-start | bytes 49160 | tf_op jit(solution)/shard_map/ppermute | solution.py:430
  27.1 3.4 %collective-permute-start.5 = (f32[160,128]{1,0:T(8,128)S(1)}, f32[160,128]{1,0:T(8,128)S(1)}, u32[]{:S(2)}, u32[]{:S(2)}) collective-permute-start(f32[160,128]{1,0:T(8,128)S(1)} %offer.5), channel_id=1, source_target_pairs={{384,448},{392,456},{400,464},{408,472},{416,480},{424,488},{432,4... | collective-permute-start | bytes 245768 | tf_op jit(solution)/shard_map/ppermute | solution.py:417
  30.5 12.3 %collective-permute-done.6.in_ref._ = f32[32,128]{1,0:T(8,128)S(1)} collective-permute-done((f32[32,128]{1,0:T(8,128)S(1)}, f32[32,128]{1,0:T(8,128)S(1)}, u32[]{:S(2)}, u32[]{:S(2)}) %collective-permute-start.6) | collective-permute-done | bytes 16416 | tf_op jit(solution)/shard_map/ppermute | solution.py:430
  42.8 0.4 start_states.1
  43.2 10.5 %all_to_all.15 = f32[8,32,128]{2,1,0:T(8,128)S(1)} all-to-all(f32[8,32,128]{2,1,0:T(8,128)S(1)} %start_states.1), channel_id=1, replica_groups={{0,8,16,24,32,40,48,56},{64,72,80,88,96,104,112,120},{128,136,144,152,1..., dimensions={0} | all-to-all | bytes 262144 | tf_op jit(solution)/shard_map/all_to_all | solution.py:439
  53.8 0.3 hidden.1
  54.1 2.0 %all-gather = f32[256,256]{1,0:T(8,128)S(1)} all-gather(f32[128,256]{1,0:T(8,128)S(1)} %hidden.1), channel_id=2, replica_groups={{0,1},{2,3},{4,5},{6,7},{8,9},{10,11},{12,13},{14,15},{16,17},{18,19},{..., dimensions={0}, use_global_device_ids=true | all-gather | bytes 393216 | tf_op jit(solution)/shard_map/all_gather | solution.py:443
  56.1 0.5 project.1
  56.6 13.8 %all_to_all.16 = f32[4,16,2048]{2,1,0:T(8,128)S(1)} all-to-all(f32[4,16,2048]{2,1,0:T(8,128)S(1)} %bitcast.12), channel_id=1, replica_groups={{0,2,4,6},{1,3,5,7},{8,10,12,14},{9,11,13,15},{16,18,20,22},{17,19,21,2..., dimensions={0} | all-to-all | bytes 1048576 | tf_op jit(solution)/shard_map/all_to_all | solution.py:451
  70.4 0.7 reduce_sum.9
  (30 shorter events, 0.8 us)
Async XLA Ops:
  5.4 15.6 %all-to-all-start = ((f32[8,160,128]{2,1,0:T(8,128)}), f32[8,160,128]{2,1,0:T(8,128)S(1)}, u32[]{:S(2)}, u32[]{:S(2)}) async-start(f32[8,160,128]{2,1,0:T(8,128)} %get-tuple-element.23), calls=%async_computation | async-start | bytes 1310720 | tf_op jit(solution)/shard_map/all_to_all | solution.py:389
  10.3 5.7 %copy-start.2 = (f32[128,2]{0,1:T(2,128)S(1)}, f32[128,2]{0,1:T(2,128)}, u32[]{:S(2)}) copy-start(f32[128,2]{0,1:T(2,128)} %param.11) | copy-start | bytes 3076
  10.3 1.2 %copy-start.4 = (bf16[256,2048]{1,0:T(8,128)(2,1)S(1)}, bf16[256,2048]{1,0:T(8,128)(2,1)}, u32[]{:S(2)}) copy-start(bf16[256,2048]{1,0:T(8,128)(2,1)} %in_ref) | copy-start | bytes 3145732
  11.5 4.4 %copy-start.5 = (f32[2,256,256]{2,1,0:T(8,128)S(1)}, f32[2,256,256]{2,1,0:T(8,128)}, u32[]{:S(2)}) copy-start(f32[2,256,256]{2,1,0:T(8,128)} %get-tuple-element.25.solved_ref) | copy-start | bytes 1572868
  11.5 4.5 %copy-start.6 = (f32[2,256,128]{2,1,0:T(8,128)S(1)}, f32[2,256,128]{2,1,0:T(8,128)}, u32[]{:S(2)}) copy-start(f32[2,256,128]{2,1,0:T(8,128)} %get-tuple-element.24.keys_ref) | copy-start | bytes 786436
  11.5 4.5 %copy-start.7 = (bf16[128,2,128]{2,1,0:T(2,128)(2,1)S(1)}, bf16[128,2,128]{2,1,0:T(2,128)(2,1)}, u32[]{:S(2)}) copy-start(bf16[128,2,128]{2,1,0:T(2,128)(2,1)} %param.7) | copy-start | bytes 196612
  13.1 1.0 %copy-start = (bf16[256,2048]{1,0:T(8,128)(2,1)}, bf16[256,2048]{1,0:T(8,128)(2,1)S(1)}, u32[]{:S(2)}) copy-start(bf16[256,2048]{1,0:T(8,128)(2,1)S(1)} %get-tuple-element.35.own_ref) | copy-start | bytes 3145732
  14.1 42.0 %collective-permute-start.7 = (f32[256,2048]{1,0:T(8,128)}, f32[256,2048]{1,0:T(8,128)S(1)}, u32[]{:S(2)}, u32[]{:S(2)}) collective-permute-start(f32[256,2048]{1,0:T(8,128)} %get-tuple-element.36), channel_id=1, source_target_pairs={{0,1},{1,0},{2,3},{3,2},{4,5},{5,4},{6,7},{7,6},{8,9},{9,8},{10,11... | collective-permute-start | bytes 6291464 | tf_op jit(solution)/shard_map/ppermute | solution.py:397
  21.6 0.7 collective-permute-start
  22.4 1.4 %collective-permute-start.2 = (f32[32,128]{1,0:T(8,128)S(1)}, f32[32,128]{1,0:T(8,128)S(1)}, u32[]{:S(2)}, u32[]{:S(2)}) collective-permute-start(f32[32,128]{1,0:T(8,128)S(1)} %first_write.1._), channel_id=1, source_target_pairs={{0,128},{8,136},{16,144},{24,152},{32,160},{40,168},{48,176},{56,1... | collective-permute-start | bytes 49160 | tf_op jit(solution)/shard_map/ppermute | solution.py:430
  23.1 0.7 collective-permute-start.1
  24.1 1.4 %collective-permute-start.4 = (f32[32,128]{1,0:T(8,128)S(1)}, f32[32,128]{1,0:T(8,128)S(1)}, u32[]{:S(2)}, u32[]{:S(2)}) collective-permute-start(f32[32,128]{1,0:T(8,128)S(1)} %next_write.2._), channel_id=1, source_target_pairs={{128,256},{136,264},{144,272},{152,280},{160,288},{168,296},{176,3... | collective-permute-start | bytes 49160 | tf_op jit(solution)/shard_map/ppermute | solution.py:430
  24.8 0.7 collective-permute-start.3
  25.8 17.0 %collective-permute-start.6 = (f32[32,128]{1,0:T(8,128)S(1)}, f32[32,128]{1,0:T(8,128)S(1)}, u32[]{:S(2)}, u32[]{:S(2)}) collective-permute-start(f32[32,128]{1,0:T(8,128)S(1)} %next_write.3._), channel_id=1, source_target_pairs={{256,448},{264,456},{272,464},{280,472},{288,480},{296,488},{304,4... | collective-permute-start | bytes 49160 | tf_op jit(solution)/shard_map/ppermute | solution.py:430
  27.1 26.7 %copy-start.3 = (f32[2,128]{1,0:T(2,128)S(1)}, f32[2,128]{1,0:T(2,128)}, u32[]{:S(2)}) copy-start(f32[2,128]{1,0:T(2,128)} %gain_ref.1) | copy-start | bytes 3076
  27.1 15.7 %collective-permute-start.5 = (f32[160,128]{1,0:T(8,128)S(1)}, f32[160,128]{1,0:T(8,128)S(1)}, u32[]{:S(2)}, u32[]{:S(2)}) collective-permute-start(f32[160,128]{1,0:T(8,128)S(1)} %offer.5), channel_id=1, source_target_pairs={{384,448},{392,456},{400,464},{408,472},{416,480},{424,488},{432,4... | collective-permute-start | bytes 245768 | tf_op jit(solution)/shard_map/ppermute | solution.py:417
  42.8 13.3 %copy-start.1 = (bf16[256,2048]{1,0:T(8,128)(2,1)S(1)}, bf16[256,2048]{1,0:T(8,128)(2,1)}, u32[]{:S(2)}) copy-start(bf16[256,2048]{1,0:T(8,128)(2,1)} %copy-done) | copy-start | bytes 3145732

commit v8 on v7

--- a/solution.py
+++ b/solution.py
@@ -320,29 +320,33 @@
     out_ref[...] = in_ref[...]
 
 
-def hidden_kernel(heads, own_ref, through_ref, state_ref, gain_ref, hidden_ref):
+def hidden_kernel(heads, spread, core_ref, own_ref, through_ref, state_ref, gain_ref, keep_ref, give_ref):
     width = own_ref.shape[1] // heads
+    share = own_ref.shape[0] // spread
+    on_first = core_ref[0] == 0
     for head in range(heads):
         lanes = slice(head * width, (head + 1) * width)
         outputs = own_ref[:, lanes] + dot(through_ref[:, lanes], state_ref[head], 1, 1)
         scale = lax.rsqrt(jnp.mean(outputs * outputs, axis=-1, keepdims=True) + 1e-05)
         scaled = outputs * scale * gain_ref[head : head + 1, :]
-        hidden_ref[:, lanes] = scaled.astype(BF16).astype(F32)
-
-
-def project_kernel(spread, core_ref, hidden_ref, own_ref, other_ref, out_ref):
-    share = hidden_ref.shape[1] // spread
-    on_first = core_ref[0] == 0
-    kept = []
-    for core in range(2):
-        even = jnp.concatenate([hidden_ref[core, i * share : (i + 1) * share] for i in range(0, spread, 2)], axis=0)
-        odd = jnp.concatenate([hidden_ref[core, i * share : (i + 1) * share] for i in range(1, spread, 2)], axis=0)
-        kept.append(jnp.where(on_first, even, odd))
-    mine = jnp.where(on_first, kept[0], kept[1]).astype(BF16)
-    others = jnp.where(on_first, kept[1], kept[0]).astype(BF16)
-    out_ref[...] = jnp.dot(mine, own_ref[...], preferred_element_type=F32) + jnp.dot(
-        others, other_ref[...].astype(BF16), preferred_element_type=F32
-    )
+        even = jnp.concatenate([scaled[i * share : (i + 1) * share] for i in range(0, spread, 2)], axis=0)
+        odd = jnp.concatenate([scaled[i * share : (i + 1) * share] for i in range(1, spread, 2)], axis=0)
+        keep_ref[:, lanes] = jnp.where(on_first, even, odd).astype(BF16)
+        give_ref[:, lanes] = jnp.where(on_first, odd, even).astype(BF16).astype(F32)
+
+
+def project_kernel(core_ref, keep_ref, both_ref, own_ref, other_ref, out_ref):
+    got = jnp.where(core_ref[0] == 0, both_ref[1], both_ref[0]).astype(BF16)
+    out_ref[...] = jnp.dot(keep_ref[...], own_ref[...], preferred_element_type=F32) + jnp.dot(
+        got, other_ref[...].astype(BF16), preferred_element_type=F32
+    )
+
+
+def sum_kernel(shares_ref, out_ref):
+    total = shares_ref[0]
+    for i in range(1, shares_ref.shape[0]):
+        total = total + shares_ref[i]
+    out_ref[...] = total.astype(BF16)
 
 
 def per_device(queries, key_rows, value_rows, strengths, log_decay, norm_gain, out_weight):
@@ -437,21 +441,24 @@
         in_specs=[smem] + [vmem] * 9,
     )(place, total, *swapped, *arrived, prefix)
     states = lax.all_to_all(starts, "ctx", 0, 0, axis_index_groups=inner)
-    hidden = call(
-        functools.partial(hidden_kernel, heads), array(tokens, heads * width), "hidden"
-    )(own, through, states.reshape(heads, width, width), norm_gain)
-    hidden = lax.all_gather(hidden, "head", axis_index_groups=cores)
+    keep, give = call(
+        functools.partial(hidden_kernel, heads, spread),
+        (array(tokens // 2, heads * width, dtype=BF16), array(tokens // 2, heads * width)),
+        "hidden",
+        in_specs=[smem] + [vmem] * 4,
+    )(core, own, through, states.reshape(heads, width, width), norm_gain)
+    given = lax.all_gather(give, "head", axis_index_groups=cores)
     sums = call(
-        functools.partial(project_kernel, spread),
+        project_kernel,
         array(tokens // 2, columns),
         "project",
-        in_specs=[smem, vmem, vmem, vmem],
-    )(core, hidden, held, other)
+        in_specs=[smem] + [vmem] * 4,
+    )(core, keep, given, held, other)
     ring = [[i * 2 + c for i in range(spread // 2)] for c in range(2)]
     shares = lax.all_to_all(
         sums.reshape(spread // 2, tokens // spread, columns), "head", 0, 0, axis_index_groups=ring
     )
-    return jnp.sum(shares, axis=0).astype(BF16)
+    return call(sum_kernel, array(tokens // spread, columns, dtype=BF16), "row_sums")(shares)
 
 
 def solution(mesh):

time: 71.5 us -> 71.4 us (level)
    pallas_call x2 -> x3, Pallas kernels: 0.8 us -> 1.46 us  [the longest x1 0.66 us: per_device(): call(sum_kernel, array(tokens // spread, columns, dtype=BF16), 'row_sums')]
where the time goes in v8:
time: 71.4 us; the launch traced here: 71 us
  blocking collectives  26.3 us (37%)
  waiting for transfers between devices  16.5 us (23%)
  starting transfers between devices  15 us (21%)
  Pallas kernels  10.8 us (15%)
  local copies, waits for them, and re-layouts  2.24 us (3%)
    all_to_all x1, blocking collectives, per_device(): lax.all_to_all(sums.reshape(spread // 2, tokens // spread, columns), 'hea...  13.9 us
    ppermute x3, waiting for transfers between devices, per_device(): lax.ppermute(write, 'ctx', [(i, j ^ GROUP if g == 2 else j) for i, j in z...  12.2 us
    all_to_all x1, blocking collectives, per_device(): states = lax.all_to_all(starts, 'ctx', 0, 0, axis_index_groups=inner)  10.5 us
    ppermute x4, starting transfers between devices, per_device(): lax.ppermute(offered, 'ctx', [(i, i ^ GROUP) for i in group[g]])  5.51 us
    pallas_call x1, Pallas kernels, local_call(): pl.pallas_call(functools.partial(local_kernel, heads), out_shape=(jax.Sha...  5.37 us
    all_to_all x1, starting transfers between devices, per_device(): parts = lax.all_to_all(msg, 'ctx', 0, 0, axis_index_groups=inner)  4.93 us
    all_to_all x1, waiting for transfers between devices, per_device(): parts = lax.all_to_all(msg, 'ctx', 0, 0, axis_index_groups=inner)  4.31 us
    ppermute x3, starting transfers between devices, per_device(): lax.ppermute(write, 'ctx', [(i, j ^ GROUP if g == 2 else j) for i, j in z...  2.61 us
  transfers between devices with their start and end apart: 9, of which 2 were waited for; matrix products, arithmetic and copies ran while one was open for 0% of the time, Pallas kernels for 6%

profile of v8, /device:TPU:384, one launch (start us, length us, event | category | flops | bytes accessed | tf_op | source)
XLA Modules:
  0.0 71.0 jit_solution(2142370535425401529)
XLA Ops:
  0.0 5.4 %local_chunk.1 = (f32[8,160,128]{2,1,0:T(8,128)}, f32[2,256,256]{2,1,0:T(8,128)}, f32[2,256,128]{2,1,0:T(8,128)}) custom-call(bf16[512,128]{1,0:T(8,128)(2,1)} %bitcast.18, bf16[512,128]{1,0:T(8,128)(2,1)} %bitcast.19, f32[2,128]{1,0:T(2,128)} %bitcast.15, f32[4,128]{1,0:T(4,128)} %bitcast.20), custom_call_target="tpu_custom_call" | custom-call | tf_op jit(solution)/shard_map/local_chunk/pallas_call | solution.py:217
  5.4 4.9 %all-to-all-start = ((f32[8,160,128]{2,1,0:T(8,128)}), f32[8,160,128]{2,1,0:T(8,128)S(1)}, u32[]{:S(2)}, u32[]{:S(2)}) async-start(f32[8,160,128]{2,1,0:T(8,128)} %get-tuple-element.25), calls=%async_computation | async-start | bytes 1310720 | tf_op jit(solution)/shard_map/all_to_all | solution.py:393
  10.3 1.2 %copy-done.4 = bf16[256,2048]{1,0:T(8,128)(2,1)S(1)} copy-done((bf16[256,2048]{1,0:T(8,128)(2,1)S(1)}, bf16[256,2048]{1,0:T(8,128)(2,1)}, u32[]{:S(2)}) %copy-start.4) | copy-done | bytes 1048600
  11.6 1.5 %widen.1 = (f32[256,2048]{1,0:T(8,128)}, bf16[256,2048]{1,0:T(8,128)(2,1)S(1)}) custom-call(bf16[256,2048]{1,0:T(8,128)(2,1)S(1)} %copy-done.4), custom_call_target="tpu_custom_call" | custom-call | flops 1000000000 | bytes 1048576 | tf_op jit(solution)/shard_map/widen/pallas_call | solution.py:395
  13.1 1.0 %copy-done = bf16[256,2048]{1,0:T(8,128)(2,1)} copy-done((bf16[256,2048]{1,0:T(8,128)(2,1)}, bf16[256,2048]{1,0:T(8,128)(2,1)S(1)}, u32[]{:S(2)}) %copy-start) | copy-done | bytes 1048600
  14.1 1.9 %collective-permute-start.7 = (f32[256,2048]{1,0:T(8,128)}, f32[256,2048]{1,0:T(8,128)S(1)}, u32[]{:S(2)}, u32[]{:S(2)}) collective-permute-start(f32[256,2048]{1,0:T(8,128)} %get-tuple-element.40), channel_id=1, source_target_pairs={{0,1},{1,0},{2,3},{3,2},{4,5},{5,4},{6,7},{7,6},{8,9},{9,8},{10,11... | collective-permute-start | bytes 6291464 | tf_op jit(solution)/shard_map/ppermute | solution.py:401
  16.0 0.6 own_outputs.1
  16.7 4.3 %all-to-all-done.parts_ref = f32[8,160,128]{2,1,0:T(8,128)S(1)} async-done(((f32[8,160,128]{2,1,0:T(8,128)}), f32[8,160,128]{2,1,0:T(8,128)S(1)}, u32[]{:S(2)}, u32[]{:S(2)}) %all-to-all-start) | async-done | bytes 655392 | tf_op jit(solution)/shard_map/all_to_all | solution.py:393
  21.0 0.6 group_scan.1
  21.6 0.7 collective-permute-start
  22.4 0.7 collective-permute-start.2
  23.1 0.7 collective-permute-start.1
  24.1 0.7 collective-permute-start.4
  24.8 0.7 collective-permute-start.3
  25.8 1.3 %collective-permute-start.6 = (f32[32,128]{1,0:T(8,128)S(1)}, f32[32,128]{1,0:T(8,128)S(1)}, u32[]{:S(2)}, u32[]{:S(2)}) collective-permute-start(f32[32,128]{1,0:T(8,128)S(1)} %next_write.3._), channel_id=1, source_target_pairs={{256,448},{264,456},{272,464},{280,472},{288,480},{296,488},{304,4... | collective-permute-start | bytes 49160 | tf_op jit(solution)/shard_map/ppermute | solution.py:434
  27.1 3.5 %collective-permute-start.5 = (f32[160,128]{1,0:T(8,128)S(1)}, f32[160,128]{1,0:T(8,128)S(1)}, u32[]{:S(2)}, u32[]{:S(2)}) collective-permute-start(f32[160,128]{1,0:T(8,128)S(1)} %offer.5), channel_id=1, source_target_pairs={{384,448},{392,456},{400,464},{408,472},{416,480},{424,488},{432,4... | collective-permute-start | bytes 245768 | tf_op jit(solution)/shard_map/ppermute | solution.py:421
  30.7 12.2 %collective-permute-done.6.in_ref._ = f32[32,128]{1,0:T(8,128)S(1)} collective-permute-done((f32[32,128]{1,0:T(8,128)S(1)}, f32[32,128]{1,0:T(8,128)S(1)}, u32[]{:S(2)}, u32[]{:S(2)}) %collective-permute-start.6) | collective-permute-done | bytes 16416 | tf_op jit(solution)/shard_map/ppermute | solution.py:434
  42.8 0.4 start_states.1
  43.2 10.5 %all_to_all.15 = f32[8,32,128]{2,1,0:T(8,128)S(1)} all-to-all(f32[8,32,128]{2,1,0:T(8,128)S(1)} %start_states.1), channel_id=1, replica_groups={{0,8,16,24,32,40,48,56},{64,72,80,88,96,104,112,120},{128,136,144,152,1..., dimensions={0} | all-to-all | bytes 262144 | tf_op jit(solution)/shard_map/all_to_all | solution.py:443
  53.8 0.3 hidden.1
  54.1 1.9 %all-gather = f32[128,256]{1,0:T(8,128)S(1)} all-gather(f32[64,256]{1,0:T(8,128)S(1)} %get-tuple-element.37), channel_id=2, replica_groups={{0,1},{2,3},{4,5},{6,7},{8,9},{10,11},{12,13},{14,15},{16,17},{18,19},{..., dimensions={0}, use_global_device_ids=true | all-gather | bytes 196608 | tf_op jit(solution)/shard_map/all_gather | solution.py:450
  56.0 0.5 project.1
  56.5 13.9 %all_to_all.16.shares_ref = f32[4,16,2048]{2,1,0:T(8,128)S(1)} all-to-all(f32[4,16,2048]{2,1,0:T(8,128)S(1)} %bitcast.12), channel_id=1, replica_groups={{0,2,4,6},{1,3,5,7},{8,10,12,14},{9,11,13,15},{16,18,20,22},{17,19,21,2..., dimensions={0} | all-to-all | bytes 1048576 | tf_op jit(solution)/shard_map/all_to_all | solution.py:458
  70.3 0.7 row_sums.1
  (30 shorter events, 0.8 us)
Async XLA Ops:
  5.4 15.6 %all-to-all-start = ((f32[8,160,128]{2,1,0:T(8,128)}), f32[8,160,128]{2,1,0:T(8,128)S(1)}, u32[]{:S(2)}, u32[]{:S(2)}) async-start(f32[8,160,128]{2,1,0:T(8,128)} %get-tuple-element.25), calls=%async_computation | async-start | bytes 1310720 | tf_op jit(solution)/shard_map/all_to_all | solution.py:393
  10.3 5.7 %copy-start.2 = (f32[128,2]{0,1:T(2,128)S(1)}, f32[128,2]{0,1:T(2,128)}, u32[]{:S(2)}) copy-start(f32[128,2]{0,1:T(2,128)} %param.11) | copy-start | bytes 3076
  10.3 1.2 %copy-start.4 = (bf16[256,2048]{1,0:T(8,128)(2,1)S(1)}, bf16[256,2048]{1,0:T(8,128)(2,1)}, u32[]{:S(2)}) copy-start(bf16[256,2048]{1,0:T(8,128)(2,1)} %in_ref) | copy-start | bytes 3145732
  11.5 4.4 %copy-start.5 = (f32[2,256,256]{2,1,0:T(8,128)S(1)}, f32[2,256,256]{2,1,0:T(8,128)}, u32[]{:S(2)}) copy-start(f32[2,256,256]{2,1,0:T(8,128)} %get-tuple-element.27.solved_ref) | copy-start | bytes 1572868
  11.6 4.5 %copy-start.6 = (f32[2,256,128]{2,1,0:T(8,128)S(1)}, f32[2,256,128]{2,1,0:T(8,128)}, u32[]{:S(2)}) copy-start(f32[2,256,128]{2,1,0:T(8,128)} %get-tuple-element.26.keys_ref) | copy-start | bytes 786436
  11.6 4.5 %copy-start.7 = (bf16[128,2,128]{2,1,0:T(2,128)(2,1)S(1)}, bf16[128,2,128]{2,1,0:T(2,128)(2,1)}, u32[]{:S(2)}) copy-start(bf16[128,2,128]{2,1,0:T(2,128)(2,1)} %param.7) | copy-start | bytes 196612
  13.1 1.0 %copy-start = (bf16[256,2048]{1,0:T(8,128)(2,1)}, bf16[256,2048]{1,0:T(8,128)(2,1)S(1)}, u32[]{:S(2)}) copy-start(bf16[256,2048]{1,0:T(8,128)(2,1)S(1)} %get-tuple-element.39.own_ref) | copy-start | bytes 3145732
  14.1 41.9 %collective-permute-start.7 = (f32[256,2048]{1,0:T(8,128)}, f32[256,2048]{1,0:T(8,128)S(1)}, u32[]{:S(2)}, u32[]{:S(2)}) collective-permute-start(f32[256,2048]{1,0:T(8,128)} %get-tuple-element.40), channel_id=1, source_target_pairs={{0,1},{1,0},{2,3},{3,2},{4,5},{5,4},{6,7},{7,6},{8,9},{9,8},{10,11... | collective-permute-start | bytes 6291464 | tf_op jit(solution)/shard_map/ppermute | solution.py:401
  21.6 0.7 collective-permute-start
  22.4 1.4 %collective-permute-start.2 = (f32[32,128]{1,0:T(8,128)S(1)}, f32[32,128]{1,0:T(8,128)S(1)}, u32[]{:S(2)}, u32[]{:S(2)}) collective-permute-start(f32[32,128]{1,0:T(8,128)S(1)} %first_write.1._), channel_id=1, source_target_pairs={{0,128},{8,136},{16,144},{24,152},{32,160},{40,168},{48,176},{56,1... | collective-permute-start | bytes 49160 | tf_op jit(solution)/shard_map/ppermute | solution.py:434
  23.1 0.7 collective-permute-start.1
  24.1 1.4 %collective-permute-start.4 = (f32[32,128]{1,0:T(8,128)S(1)}, f32[32,128]{1,0:T(8,128)S(1)}, u32[]{:S(2)}, u32[]{:S(2)}) collective-permute-start(f32[32,128]{1,0:T(8,128)S(1)} %next_write.2._), channel_id=1, source_target_pairs={{128,256},{136,264},{144,272},{152,280},{160,288},{168,296},{176,3... | collective-permute-start | bytes 49160 | tf_op jit(solution)/shard_map/ppermute | solution.py:434
  24.8 0.7 collective-permute-start.3
  25.8 17.0 %collective-permute-start.6 = (f32[32,128]{1,0:T(8,128)S(1)}, f32[32,128]{1,0:T(8,128)S(1)}, u32[]{:S(2)}, u32[]{:S(2)}) collective-permute-start(f32[32,128]{1,0:T(8,128)S(1)} %next_write.3._), channel_id=1, source_target_pairs={{256,448},{264,456},{272,464},{280,472},{288,480},{296,488},{304,4... | collective-permute-start | bytes 49160 | tf_op jit(solution)/shard_map/ppermute | solution.py:434
  27.1 26.6 %copy-start.3 = (f32[2,128]{1,0:T(2,128)S(1)}, f32[2,128]{1,0:T(2,128)}, u32[]{:S(2)}) copy-start(f32[2,128]{1,0:T(2,128)} %gain_ref.1) | copy-start | bytes 3076
  27.1 28.9 %copy-start.1 = (bf16[256,2048]{1,0:T(8,128)(2,1)S(1)}, bf16[256,2048]{1,0:T(8,128)(2,1)}, u32[]{:S(2)}) copy-start(bf16[256,2048]{1,0:T(8,128)(2,1)} %copy-done) | copy-start | bytes 3145732
  27.1 15.7 %collective-permute-start.5 = (f32[160,128]{1,0:T(8,128)S(1)}, f32[160,128]{1,0:T(8,128)S(1)}, u32[]{:S(2)}, u32[]{:S(2)}) collective-permute-start(f32[160,128]{1,0:T(8,128)S(1)} %offer.5), channel_id=1, source_target_pairs={{384,448},{392,456},{400,464},{408,472},{416,480},{424,488},{432,4... | collective-permute-start | bytes 245768 | tf_op jit(solution)/shard_map/ppermute | solution.py:421

commit v9 on v8

--- a/solution.py
+++ b/solution.py
@@ -330,7 +330,7 @@
         scale = lax.rsqrt(jnp.mean(outputs * outputs, axis=-1, keepdims=True) + 1e-05)
         scaled = outputs * scale * gain_ref[head : head + 1, :]
         even = jnp.concatenate([scaled[i * share : (i + 1) * share] for i in range(0, spread, 2)], axis=0)
-        odd = jnp.concatenate([scaled[i * share : (i + 1) * share] for i in range(1, spread, 2)], axis=0)
+        odd = jnp.concatenate([scaled[i * share : (i + 1) * share] for i in range(spread - 1, 0, -2)], axis=0)
         keep_ref[:, lanes] = jnp.where(on_first, even, odd).astype(BF16)
         give_ref[:, lanes] = jnp.where(on_first, odd, even).astype(BF16).astype(F32)
 
@@ -454,7 +454,7 @@
         "project",
         in_specs=[smem] + [vmem] * 4,
     )(core, keep, given, held, other)
-    ring = [[i * 2 + c for i in range(spread // 2)] for c in range(2)]
+    ring = [list(range(0, spread, 2)), list(range(spread - 1, 0, -2))]
     shares = lax.all_to_all(
         sums.reshape(spread // 2, tokens // spread, columns), "head", 0, 0, axis_index_groups=ring
     )

time: 71.4 us -> 70.7 us (level)
  blocking collectives: 26.3 us -> 25.5 us
    all_to_all x1, blocking collectives: 13.9 us -> 13.1 us  [per_device(): lax.all_to_all(sums.reshape(spread // 2, tokens // spread, columns), 'hea...]
where the time goes in v9:
time: 70.7 us; the launch traced here: 70.3 us
  blocking collectives  25.5 us (36%)
  waiting for transfers between devices  16.5 us (23%)
  starting transfers between devices  15 us (21%)
  Pallas kernels  10.8 us (15%)
  local copies, waits for them, and re-layouts  2.24 us (3%)
    all_to_all x1, blocking collectives, per_device(): lax.all_to_all(sums.reshape(spread // 2, tokens // spread, columns), 'hea...  13.1 us
    ppermute x3, waiting for transfers between devices, per_device(): lax.ppermute(write, 'ctx', [(i, j ^ GROUP if g == 2 else j) for i, j in z...  12.2 us
    all_to_all x1, blocking collectives, per_device(): states = lax.all_to_all(starts, 'ctx', 0, 0, axis_index_groups=inner)  10.5 us
    ppermute x4, starting transfers between devices, per_device(): lax.ppermute(offered, 'ctx', [(i, i ^ GROUP) for i in group[g]])  5.51 us
    pallas_call x1, Pallas kernels, local_call(): pl.pallas_call(functools.partial(local_kernel, heads), out_shape=(jax.Sha...  5.37 us
    all_to_all x1, starting transfers between devices, per_device(): parts = lax.all_to_all(msg, 'ctx', 0, 0, axis_index_groups=inner)  4.93 us
    all_to_all x1, waiting for transfers between devices, per_device(): parts = lax.all_to_all(msg, 'ctx', 0, 0, axis_index_groups=inner)  4.31 us
    ppermute x3, starting transfers between devices, per_device(): lax.ppermute(write, 'ctx', [(i, j ^ GROUP if g == 2 else j) for i, j in z...  2.61 us
  transfers between devices with their start and end apart: 9, of which 2 were waited for; matrix products, arithmetic and copies ran while one was open for 0% of the time, Pallas kernels for 6%

profile of v9, /device:TPU:384, one launch (start us, length us, event | category | flops | bytes accessed | tf_op | source)
XLA Modules:
  0.0 70.3 jit_solution(10365718795585204817)
XLA Ops:
  0.0 5.4 %local_chunk.1 = (f32[8,160,128]{2,1,0:T(8,128)}, f32[2,256,256]{2,1,0:T(8,128)}, f32[2,256,128]{2,1,0:T(8,128)}) custom-call(bf16[512,128]{1,0:T(8,128)(2,1)} %bitcast.18, bf16[512,128]{1,0:T(8,128)(2,1)} %bitcast.19, f32[2,128]{1,0:T(2,128)} %bitcast.15, f32[4,128]{1,0:T(4,128)} %bitcast.20), custom_call_target="tpu_custom_call" | custom-call | tf_op jit(solution)/shard_map/local_chunk/pallas_call | solution.py:217
  5.4 4.9 %all-to-all-start = ((f32[8,160,128]{2,1,0:T(8,128)}), f32[8,160,128]{2,1,0:T(8,128)S(1)}, u32[]{:S(2)}, u32[]{:S(2)}) async-start(f32[8,160,128]{2,1,0:T(8,128)} %get-tuple-element.25), calls=%async_computation | async-start | bytes 1310720 | tf_op jit(solution)/shard_map/all_to_all | solution.py:393
  10.3 1.2 %copy-done.4 = bf16[256,2048]{1,0:T(8,128)(2,1)S(1)} copy-done((bf16[256,2048]{1,0:T(8,128)(2,1)S(1)}, bf16[256,2048]{1,0:T(8,128)(2,1)}, u32[]{:S(2)}) %copy-start.4) | copy-done | bytes 1048600
  11.6 1.5 %widen.1 = (f32[256,2048]{1,0:T(8,128)}, bf16[256,2048]{1,0:T(8,128)(2,1)S(1)}) custom-call(bf16[256,2048]{1,0:T(8,128)(2,1)S(1)} %copy-done.4), custom_call_target="tpu_custom_call" | custom-call | flops 1000000000 | bytes 1048576 | tf_op jit(solution)/shard_map/widen/pallas_call | solution.py:395
  13.1 1.0 %copy-done = bf16[256,2048]{1,0:T(8,128)(2,1)} copy-done((bf16[256,2048]{1,0:T(8,128)(2,1)}, bf16[256,2048]{1,0:T(8,128)(2,1)S(1)}, u32[]{:S(2)}) %copy-start) | copy-done | bytes 1048600
  14.1 1.9 %collective-permute-start.7 = (f32[256,2048]{1,0:T(8,128)}, f32[256,2048]{1,0:T(8,128)S(1)}, u32[]{:S(2)}, u32[]{:S(2)}) collective-permute-start(f32[256,2048]{1,0:T(8,128)} %get-tuple-element.40), channel_id=1, source_target_pairs={{0,1},{1,0},{2,3},{3,2},{4,5},{5,4},{6,7},{7,6},{8,9},{9,8},{10,11... | collective-permute-start | bytes 6291464 | tf_op jit(solution)/shard_map/ppermute | solution.py:401
  16.0 0.6 own_outputs.1
  16.7 4.3 %all-to-all-done.parts_ref = f32[8,160,128]{2,1,0:T(8,128)S(1)} async-done(((f32[8,160,128]{2,1,0:T(8,128)}), f32[8,160,128]{2,1,0:T(8,128)S(1)}, u32[]{:S(2)}, u32[]{:S(2)}) %all-to-all-start) | async-done | bytes 655392 | tf_op jit(solution)/shard_map/all_to_all | solution.py:393
  21.0 0.6 group_scan.1
  21.6 0.7 collective-permute-start
  22.4 0.7 collective-permute-start.2
  23.1 0.7 collective-permute-start.1
  24.1 0.7 collective-permute-start.4
  24.8 0.7 collective-permute-start.3
  25.8 1.3 %collective-permute-start.6 = (f32[32,128]{1,0:T(8,128)S(1)}, f32[32,128]{1,0:T(8,128)S(1)}, u32[]{:S(2)}, u32[]{:S(2)}) collective-permute-start(f32[32,128]{1,0:T(8,128)S(1)} %next_write.3._), channel_id=1, source_target_pairs={{256,448},{264,456},{272,464},{280,472},{288,480},{296,488},{304,4... | collective-permute-start | bytes 49160 | tf_op jit(solution)/shard_map/ppermute | solution.py:434
  27.1 3.5 %collective-permute-start.5 = (f32[160,128]{1,0:T(8,128)S(1)}, f32[160,128]{1,0:T(8,128)S(1)}, u32[]{:S(2)}, u32[]{:S(2)}) collective-permute-start(f32[160,128]{1,0:T(8,128)S(1)} %offer.5), channel_id=1, source_target_pairs={{384,448},{392,456},{400,464},{408,472},{416,480},{424,488},{432,4... | collective-permute-start | bytes 245768 | tf_op jit(solution)/shard_map/ppermute | solution.py:421
  30.7 12.2 %collective-permute-done.6.in_ref._ = f32[32,128]{1,0:T(8,128)S(1)} collective-permute-done((f32[32,128]{1,0:T(8,128)S(1)}, f32[32,128]{1,0:T(8,128)S(1)}, u32[]{:S(2)}, u32[]{:S(2)}) %collective-permute-start.6) | collective-permute-done | bytes 16416 | tf_op jit(solution)/shard_map/ppermute | solution.py:434
  42.8 0.4 start_states.1
  43.2 10.5 %all_to_all.15 = f32[8,32,128]{2,1,0:T(8,128)S(1)} all-to-all(f32[8,32,128]{2,1,0:T(8,128)S(1)} %start_states.1), channel_id=1, replica_groups={{0,8,16,24,32,40,48,56},{64,72,80,88,96,104,112,120},{128,136,144,152,1..., dimensions={0} | all-to-all | bytes 262144 | tf_op jit(solution)/shard_map/all_to_all | solution.py:443
  53.8 0.3 hidden.1
  54.1 1.9 %all-gather = f32[128,256]{1,0:T(8,128)S(1)} all-gather(f32[64,256]{1,0:T(8,128)S(1)} %get-tuple-element.37), channel_id=2, replica_groups={{0,1},{2,3},{4,5},{6,7},{8,9},{10,11},{12,13},{14,15},{16,17},{18,19},{..., dimensions={0}, use_global_device_ids=true | all-gather | bytes 196608 | tf_op jit(solution)/shard_map/all_gather | solution.py:450
  56.0 0.5 project.1
  56.5 13.1 %all_to_all.16.shares_ref = f32[4,16,2048]{2,1,0:T(8,128)S(1)} all-to-all(f32[4,16,2048]{2,1,0:T(8,128)S(1)} %bitcast.12), channel_id=1, replica_groups={{0,2,4,6},{7,5,3,1},{8,10,12,14},{15,13,11,9},{16,18,20,22},{23,21,19,1..., dimensions={0} | all-to-all | bytes 1048576 | tf_op jit(solution)/shard_map/all_to_all | solution.py:458
  69.6 0.7 row_sums.1
  (30 shorter events, 0.8 us)
Async XLA Ops:
  5.4 15.6 %all-to-all-start = ((f32[8,160,128]{2,1,0:T(8,128)}), f32[8,160,128]{2,1,0:T(8,128)S(1)}, u32[]{:S(2)}, u32[]{:S(2)}) async-start(f32[8,160,128]{2,1,0:T(8,128)} %get-tuple-element.25), calls=%async_computation | async-start | bytes 1310720 | tf_op jit(solution)/shard_map/all_to_all | solution.py:393
  10.3 5.7 %copy-start.2 = (f32[128,2]{0,1:T(2,128)S(1)}, f32[128,2]{0,1:T(2,128)}, u32[]{:S(2)}) copy-start(f32[128,2]{0,1:T(2,128)} %param.11) | copy-start | bytes 3076
  10.3 1.2 %copy-start.4 = (bf16[256,2048]{1,0:T(8,128)(2,1)S(1)}, bf16[256,2048]{1,0:T(8,128)(2,1)}, u32[]{:S(2)}) copy-start(bf16[256,2048]{1,0:T(8,128)(2,1)} %in_ref) | copy-start | bytes 3145732
  11.5 4.4 %copy-start.5 = (f32[2,256,256]{2,1,0:T(8,128)S(1)}, f32[2,256,256]{2,1,0:T(8,128)}, u32[]{:S(2)}) copy-start(f32[2,256,256]{2,1,0:T(8,128)} %get-tuple-element.27.solved_ref) | copy-start | bytes 1572868
  11.6 4.5 %copy-start.6 = (f32[2,256,128]{2,1,0:T(8,128)S(1)}, f32[2,256,128]{2,1,0:T(8,128)}, u32[]{:S(2)}) copy-start(f32[2,256,128]{2,1,0:T(8,128)} %get-tuple-element.26.keys_ref) | copy-start | bytes 786436
  11.6 4.5 %copy-start.7 = (bf16[128,2,128]{2,1,0:T(2,128)(2,1)S(1)}, bf16[128,2,128]{2,1,0:T(2,128)(2,1)}, u32[]{:S(2)}) copy-start(bf16[128,2,128]{2,1,0:T(2,128)(2,1)} %param.7) | copy-start | bytes 196612
  13.1 1.0 %copy-start = (bf16[256,2048]{1,0:T(8,128)(2,1)}, bf16[256,2048]{1,0:T(8,128)(2,1)S(1)}, u32[]{:S(2)}) copy-start(bf16[256,2048]{1,0:T(8,128)(2,1)S(1)} %get-tuple-element.39.own_ref) | copy-start | bytes 3145732
  14.1 41.9 %collective-permute-start.7 = (f32[256,2048]{1,0:T(8,128)}, f32[256,2048]{1,0:T(8,128)S(1)}, u32[]{:S(2)}, u32[]{:S(2)}) collective-permute-start(f32[256,2048]{1,0:T(8,128)} %get-tuple-element.40), channel_id=1, source_target_pairs={{0,1},{1,0},{2,3},{3,2},{4,5},{5,4},{6,7},{7,6},{8,9},{9,8},{10,11... | collective-permute-start | bytes 6291464 | tf_op jit(solution)/shard_map/ppermute | solution.py:401
  21.6 0.7 collective-permute-start
  22.4 1.4 %collective-permute-start.2 = (f32[32,128]{1,0:T(8,128)S(1)}, f32[32,128]{1,0:T(8,128)S(1)}, u32[]{:S(2)}, u32[]{:S(2)}) collective-permute-start(f32[32,128]{1,0:T(8,128)S(1)} %first_write.1._), channel_id=1, source_target_pairs={{0,128},{8,136},{16,144},{24,152},{32,160},{40,168},{48,176},{56,1... | collective-permute-start | bytes 49160 | tf_op jit(solution)/shard_map/ppermute | solution.py:434
  23.1 0.7 collective-permute-start.1
  24.1 1.4 %collective-permute-start.4 = (f32[32,128]{1,0:T(8,128)S(1)}, f32[32,128]{1,0:T(8,128)S(1)}, u32[]{:S(2)}, u32[]{:S(2)}) collective-permute-start(f32[32,128]{1,0:T(8,128)S(1)} %next_write.2._), channel_id=1, source_target_pairs={{128,256},{136,264},{144,272},{152,280},{160,288},{168,296},{176,3... | collective-permute-start | bytes 49160 | tf_op jit(solution)/shard_map/ppermute | solution.py:434
  24.8 0.7 collective-permute-start.3
  25.8 17.0 %collective-permute-start.6 = (f32[32,128]{1,0:T(8,128)S(1)}, f32[32,128]{1,0:T(8,128)S(1)}, u32[]{:S(2)}, u32[]{:S(2)}) collective-permute-start(f32[32,128]{1,0:T(8,128)S(1)} %next_write.3._), channel_id=1, source_target_pairs={{256,448},{264,456},{272,464},{280,472},{288,480},{296,488},{304,4... | collective-permute-start | bytes 49160 | tf_op jit(solution)/shard_map/ppermute | solution.py:434
  27.1 26.6 %copy-start.3 = (f32[2,128]{1,0:T(2,128)S(1)}, f32[2,128]{1,0:T(2,128)}, u32[]{:S(2)}) copy-start(f32[2,128]{1,0:T(2,128)} %gain_ref.1) | copy-start | bytes 3076
  27.1 28.9 %copy-start.1 = (bf16[256,2048]{1,0:T(8,128)(2,1)S(1)}, bf16[256,2048]{1,0:T(8,128)(2,1)}, u32[]{:S(2)}) copy-start(bf16[256,2048]{1,0:T(8,128)(2,1)} %copy-done) | copy-start | bytes 3145732
  27.1 15.7 %collective-permute-start.5 = (f32[160,128]{1,0:T(8,128)S(1)}, f32[160,128]{1,0:T(8,128)S(1)}, u32[]{:S(2)}, u32[]{:S(2)}) collective-permute-start(f32[160,128]{1,0:T(8,128)S(1)} %offer.5), channel_id=1, source_target_pairs={{384,448},{392,456},{400,464},{408,472},{416,480},{424,488},{432,4... | collective-permute-start | bytes 245768 | tf_op jit(solution)/shard_map/ppermute | solution.py:421

commit v10 on v9

--- a/solution.py
+++ b/solution.py
@@ -116,8 +116,12 @@
     return inverses
 
 
+def slot(core_ref, member):
+    return jnp.where(core_ref[0] == 0, member, GROUP - 1 - member)
+
+
 def local_kernel(
-    heads, k_hbm, v_hbm, decay_hbm, beta_hbm, msg_hbm, solved_hbm, keys_hbm,
+    heads, core_ref, k_hbm, v_hbm, decay_hbm, beta_hbm, msg_hbm, solved_hbm, keys_hbm,
     k_ref, v_ref, small_ref, spread_k, spread_v, keys_ref, solved_ref, carry_ref, write_ref, in_sems, out_sems,
 ):
     rows = k_ref.shape[0] // heads
@@ -203,14 +207,14 @@
         write_ref[head] = pair[:width]
         carry_ref[head] = jnp.exp(last) * eye_k - pair[width:]
         for part in range(GROUP // heads):
-            member = head * (GROUP // heads) + part
+            member = slot(core_ref, head * (GROUP // heads) + part)
             send(carry_ref.at[head], msg_hbm.at[member, :width])
             send(write_ref.at[head, part * quarter : (part + 1) * quarter], msg_hbm.at[member, width:])
     for copy in sends:
         copy.wait()
 
 
-def local_call(keys, values, decay, beta):
+def local_call(core, keys, values, decay, beta):
     heads, tokens = decay.shape
     rows, width = keys.shape[0] // heads, keys.shape[1]
     any_space = pl.BlockSpec(memory_space=pl.ANY)
@@ -221,7 +225,7 @@
             jax.ShapeDtypeStruct((heads, rows, 2 * width), F32),
             jax.ShapeDtypeStruct((heads, rows, width), F32),
         ),
-        in_specs=[any_space] * 4,
+        in_specs=[pl.BlockSpec(memory_space=pltpu.SMEM)] + [any_space] * 4,
         out_specs=(any_space,) * 3,
         scratch_shapes=[
             pltpu.VMEM(keys.shape, BF16),
@@ -238,7 +242,7 @@
         ],
         compiler_params=pltpu.CompilerParams(vmem_limit_bytes=60 * 1024 * 1024),
         name="local_chunk",
-    )(keys, values, decay, beta)
+    )(core, keys, values, decay, beta)
 
 
 def own_kernel(heads, q_ref, keys_ref, decay_ref, solved_ref, own_ref, through_ref, spread_q):
@@ -271,9 +275,9 @@
     return jnp.concatenate([both[:width], both[width:] + later[width:]], axis=0)
 
 
-def group_kernel(width, parts_ref, prefix_ref, total_ref):
+def group_kernel(width, core_ref, parts_ref, prefix_ref, total_ref):
     count = parts_ref.shape[0]
-    runs = [parts_ref[i] for i in range(count)]
+    runs = [parts_ref[slot(core_ref, i)] for i in range(count)]
     step = 1
     while step < count:
         for start in range(step, count, 2 * step):
@@ -383,6 +387,7 @@
     core = (lax.axis_index("head") % 2).astype(jnp.int32).reshape(1)
 
     msg, solved, keys = local_call(
+        core,
         key_rows.reshape(heads * rows, width),
         value_rows.reshape(heads * rows, width),
         log_decay.T,
@@ -390,7 +395,10 @@
     )
     place = (lax.axis_index("ctx") // GROUP).astype(jnp.int32).reshape(1)
     msg, place, core = lax.optimization_barrier((msg, place, core))
-    parts = lax.all_to_all(msg, "ctx", 0, 0, axis_index_groups=inner)
+    both_ways = [
+        [i * spread + h for i in (members[::-1] if h % 2 else members)] for members in inner for h in range(spread)
+    ]
+    parts = lax.all_to_all(msg, ("ctx", "head"), 0, 0, axis_index_groups=both_ways)
     late_weight, _ = lax.optimization_barrier((out_weight, solved))
     wide, held = call(
         widen_kernel,
@@ -411,7 +419,8 @@
         functools.partial(group_kernel, width),
         (array(GROUP - 1, part_rows, width), array(part_rows, width)),
         "group_scan",
-    )(parts)
+        in_specs=[smem, vmem],
+    )(core, parts)
     quarter = ctx // 4
     group = [[g * quarter + i for i in range(quarter)] for g in range(4)]
 

time: 70.7 us -> 71.1 us (level)
  waiting for transfers between devices: 16.5 us -> 14.7 us
  starting transfers between devices: 15 us -> 16.5 us
    all_to_all x1, waiting for transfers between devices: 4.31 us -> 2.28 us  [per_device(): lax.all_to_all(msg, ('ctx', 'head'), 0, 0, axis_index_groups=both_ways)]
    ppermute x1, starting transfers between devices: 1.91 us -> 3.49 us  [per_device(): other = lax.ppermute(wide, 'head', [(i, i ^ 1) for i in range(spread)])]
where the time goes in v10:
time: 71.1 us; the launch traced here: 70.7 us
  blocking collectives  26.2 us (37%)
  starting transfers between devices  16.5 us (23%)
  waiting for transfers between devices  14.7 us (21%)
  Pallas kernels  10.8 us (15%)
  local copies, waits for them, and re-layouts  2.24 us (3%)
    all_to_all x1, blocking collectives, per_device(): lax.all_to_all(sums.reshape(spread // 2, tokens // spread, columns), 'hea...  13.2 us
    ppermute x3, waiting for transfers between devices, per_device(): lax.ppermute(write, 'ctx', [(i, j ^ GROUP if g == 2 else j) for i, j in z...  12.4 us
    all_to_all x1, blocking collectives, per_device(): states = lax.all_to_all(starts, 'ctx', 0, 0, axis_index_groups=inner)  11.1 us
    ppermute x4, starting transfers between devices, per_device(): lax.ppermute(offered, 'ctx', [(i, i ^ GROUP) for i in group[g]])  5.51 us
    pallas_call x1, Pallas kernels, local_call(): pl.pallas_call(functools.partial(local_kernel, heads), out_shape=(jax.Sha...  5.38 us
    all_to_all x1, starting transfers between devices, per_device(): lax.all_to_all(msg, ('ctx', 'head'), 0, 0, axis_index_groups=both_ways)  4.93 us
    ppermute x1, starting transfers between devices, per_device(): other = lax.ppermute(wide, 'head', [(i, i ^ 1) for i in range(spread)])  3.49 us
    ppermute x3, starting transfers between devices, per_device(): lax.ppermute(write, 'ctx', [(i, j ^ GROUP if g == 2 else j) for i, j in z...  2.61 us
  transfers between devices with their start and end apart: 9, of which 2 were waited for; matrix products, arithmetic and copies ran while one was open for 0% of the time, Pallas kernels for 6%

profile of v10, /device:TPU:384, one launch (start us, length us, event | category | flops | bytes accessed | tf_op | source)
XLA Modules:
  0.0 70.7 jit_solution(11797838450473192747)
XLA Ops:
  0.0 5.4 %local_chunk.1 = (f32[8,160,128]{2,1,0:T(8,128)}, f32[2,256,256]{2,1,0:T(8,128)}, f32[2,256,128]{2,1,0:T(8,128)}) custom-call(s32[1]{0:T(128)} %bitcast.core_ref, bf16[512,128]{1,0:T(8,128)(2,1)} %bitcast.18, bf16[512,128]{1,0:T(8,128)(2,1)} %bitcast.19, f32[2,128]{1,0:T(2,128)} %bitcast.15, f32[4,128]{1,0:T(4,128)} %bitcast.20), custom_call_target="tpu_custom_call" | custom-call | tf_op jit(solution)/shard_map/local_chunk/pallas_call | solution.py:221
  5.4 4.9 %all-to-all-start = ((f32[8,160,128]{2,1,0:T(8,128)}), f32[8,160,128]{2,1,0:T(8,128)S(1)}, u32[]{:S(2)}, u32[]{:S(2)}) async-start(f32[8,160,128]{2,1,0:T(8,128)} %get-tuple-element.25), calls=%async_computation | async-start | bytes 1310720 | tf_op jit(solution)/shard_map/all_to_all | solution.py:401
  10.3 1.2 %copy-done.4 = bf16[256,2048]{1,0:T(8,128)(2,1)S(1)} copy-done((bf16[256,2048]{1,0:T(8,128)(2,1)S(1)}, bf16[256,2048]{1,0:T(8,128)(2,1)}, u32[]{:S(2)}) %copy-start.4) | copy-done | bytes 1048600
  11.6 1.5 %widen.1 = (f32[256,2048]{1,0:T(8,128)}, bf16[256,2048]{1,0:T(8,128)(2,1)S(1)}) custom-call(bf16[256,2048]{1,0:T(8,128)(2,1)S(1)} %copy-done.4), custom_call_target="tpu_custom_call" | custom-call | flops 1000000000 | bytes 1048576 | tf_op jit(solution)/shard_map/widen/pallas_call | solution.py:403
  13.1 1.0 %copy-done = bf16[256,2048]{1,0:T(8,128)(2,1)} copy-done((bf16[256,2048]{1,0:T(8,128)(2,1)}, bf16[256,2048]{1,0:T(8,128)(2,1)S(1)}, u32[]{:S(2)}) %copy-start) | copy-done | bytes 1048600
  14.1 3.5 %collective-permute-start.7 = (f32[256,2048]{1,0:T(8,128)}, f32[256,2048]{1,0:T(8,128)S(1)}, u32[]{:S(2)}, u32[]{:S(2)}) collective-permute-start(f32[256,2048]{1,0:T(8,128)} %get-tuple-element.40), channel_id=1, source_target_pairs={{0,1},{1,0},{2,3},{3,2},{4,5},{5,4},{6,7},{7,6},{8,9},{9,8},{10,11... | collective-permute-start | bytes 6291464 | tf_op jit(solution)/shard_map/ppermute | solution.py:409
  17.6 0.6 own_outputs.1
  18.2 2.3 %all-to-all-done.parts_ref = f32[8,160,128]{2,1,0:T(8,128)S(1)} async-done(((f32[8,160,128]{2,1,0:T(8,128)}), f32[8,160,128]{2,1,0:T(8,128)S(1)}, u32[]{:S(2)}, u32[]{:S(2)}) %all-to-all-start) | async-done | bytes 655392 | tf_op jit(solution)/shard_map/all_to_all | solution.py:401
  20.5 0.6 group_scan.1
  21.2 0.7 collective-permute-start
  22.0 0.7 collective-permute-start.2
  22.7 0.7 collective-permute-start.1
  23.7 0.7 collective-permute-start.4
  24.4 0.7 collective-permute-start.3
  25.4 1.3 %collective-permute-start.6 = (f32[32,128]{1,0:T(8,128)S(1)}, f32[32,128]{1,0:T(8,128)S(1)}, u32[]{:S(2)}, u32[]{:S(2)}) collective-permute-start(f32[32,128]{1,0:T(8,128)S(1)} %next_write.3._), channel_id=1, source_target_pairs={{256,448},{264,456},{272,464},{280,472},{288,480},{296,488},{304,4... | collective-permute-start | bytes 49160 | tf_op jit(solution)/shard_map/ppermute | solution.py:443
  26.7 3.5 %collective-permute-start.5 = (f32[160,128]{1,0:T(8,128)S(1)}, f32[160,128]{1,0:T(8,128)S(1)}, u32[]{:S(2)}, u32[]{:S(2)}) collective-permute-start(f32[160,128]{1,0:T(8,128)S(1)} %offer.5), channel_id=1, source_target_pairs={{384,448},{392,456},{400,464},{408,472},{416,480},{424,488},{432,4... | collective-permute-start | bytes 245768 | tf_op jit(solution)/shard_map/ppermute | solution.py:430
  30.2 12.4 %collective-permute-done.6.in_ref._ = f32[32,128]{1,0:T(8,128)S(1)} collective-permute-done((f32[32,128]{1,0:T(8,128)S(1)}, f32[32,128]{1,0:T(8,128)S(1)}, u32[]{:S(2)}, u32[]{:S(2)}) %collective-permute-start.6) | collective-permute-done | bytes 16416 | tf_op jit(solution)/shard_map/ppermute | solution.py:443
  42.6 0.4 start_states.1
  43.0 11.1 %all_to_all.15 = f32[8,32,128]{2,1,0:T(8,128)S(1)} all-to-all(f32[8,32,128]{2,1,0:T(8,128)S(1)} %start_states.1), channel_id=1, replica_groups={{0,8,16,24,32,40,48,56},{64,72,80,88,96,104,112,120},{128,136,144,152,1..., dimensions={0} | all-to-all | bytes 262144 | tf_op jit(solution)/shard_map/all_to_all | solution.py:452
  54.1 0.3 hidden.1
  54.5 1.9 %all-gather = f32[128,256]{1,0:T(8,128)S(1)} all-gather(f32[64,256]{1,0:T(8,128)S(1)} %get-tuple-element.37), channel_id=2, replica_groups={{0,1},{2,3},{4,5},{6,7},{8,9},{10,11},{12,13},{14,15},{16,17},{18,19},{..., dimensions={0}, use_global_device_ids=true | all-gather | bytes 196608 | tf_op jit(solution)/shard_map/all_gather | solution.py:459
  56.4 0.5 project.1
  56.9 13.2 %all_to_all.16.shares_ref = f32[4,16,2048]{2,1,0:T(8,128)S(1)} all-to-all(f32[4,16,2048]{2,1,0:T(8,128)S(1)} %bitcast.12), channel_id=1, replica_groups={{0,2,4,6},{7,5,3,1},{8,10,12,14},{15,13,11,9},{16,18,20,22},{23,21,19,1..., dimensions={0} | all-to-all | bytes 1048576 | tf_op jit(solution)/shard_map/all_to_all | solution.py:467
  70.0 0.7 row_sums.1
  (30 shorter events, 0.8 us)
Async XLA Ops:
  5.4 15.1 %all-to-all-start = ((f32[8,160,128]{2,1,0:T(8,128)}), f32[8,160,128]{2,1,0:T(8,128)S(1)}, u32[]{:S(2)}, u32[]{:S(2)}) async-start(f32[8,160,128]{2,1,0:T(8,128)} %get-tuple-element.25), calls=%async_computation | async-start | bytes 1310720 | tf_op jit(solution)/shard_map/all_to_all | solution.py:401
  10.3 7.3 %copy-start.2 = (f32[128,2]{0,1:T(2,128)S(1)}, f32[128,2]{0,1:T(2,128)}, u32[]{:S(2)}) copy-start(f32[128,2]{0,1:T(2,128)} %param.11) | copy-start | bytes 3076
  10.3 1.2 %copy-start.4 = (bf16[256,2048]{1,0:T(8,128)(2,1)S(1)}, bf16[256,2048]{1,0:T(8,128)(2,1)}, u32[]{:S(2)}) copy-start(bf16[256,2048]{1,0:T(8,128)(2,1)} %in_ref) | copy-start | bytes 3145732
  11.6 6.0 %copy-start.5 = (f32[2,256,256]{2,1,0:T(8,128)S(1)}, f32[2,256,256]{2,1,0:T(8,128)}, u32[]{:S(2)}) copy-start(f32[2,256,256]{2,1,0:T(8,128)} %get-tuple-element.27.solved_ref) | copy-start | bytes 1572868
  11.6 6.0 %copy-start.6 = (f32[2,256,128]{2,1,0:T(8,128)S(1)}, f32[2,256,128]{2,1,0:T(8,128)}, u32[]{:S(2)}) copy-start(f32[2,256,128]{2,1,0:T(8,128)} %get-tuple-element.26.keys_ref) | copy-start | bytes 786436
  11.6 6.0 %copy-start.7 = (bf16[128,2,128]{2,1,0:T(2,128)(2,1)S(1)}, bf16[128,2,128]{2,1,0:T(2,128)(2,1)}, u32[]{:S(2)}) copy-start(bf16[128,2,128]{2,1,0:T(2,128)(2,1)} %param.7) | copy-start | bytes 196612
  13.1 1.0 %copy-start = (bf16[256,2048]{1,0:T(8,128)(2,1)}, bf16[256,2048]{1,0:T(8,128)(2,1)S(1)}, u32[]{:S(2)}) copy-start(bf16[256,2048]{1,0:T(8,128)(2,1)S(1)} %get-tuple-element.39.own_ref) | copy-start | bytes 3145732
  14.1 42.3 %collective-permute-start.7 = (f32[256,2048]{1,0:T(8,128)}, f32[256,2048]{1,0:T(8,128)S(1)}, u32[]{:S(2)}, u32[]{:S(2)}) collective-permute-start(f32[256,2048]{1,0:T(8,128)} %get-tuple-element.40), channel_id=1, source_target_pairs={{0,1},{1,0},{2,3},{3,2},{4,5},{5,4},{6,7},{7,6},{8,9},{9,8},{10,11... | collective-permute-start | bytes 6291464 | tf_op jit(solution)/shard_map/ppermute | solution.py:409
  21.2 0.7 collective-permute-start
  22.0 1.4 %collective-permute-start.2 = (f32[32,128]{1,0:T(8,128)S(1)}, f32[32,128]{1,0:T(8,128)S(1)}, u32[]{:S(2)}, u32[]{:S(2)}) collective-permute-start(f32[32,128]{1,0:T(8,128)S(1)} %first_write.1._), channel_id=1, source_target_pairs={{0,128},{8,136},{16,144},{24,152},{32,160},{40,168},{48,176},{56,1... | collective-permute-start | bytes 49160 | tf_op jit(solution)/shard_map/ppermute | solution.py:443
  22.7 0.7 collective-permute-start.1
  23.7 1.4 %collective-permute-start.4 = (f32[32,128]{1,0:T(8,128)S(1)}, f32[32,128]{1,0:T(8,128)S(1)}, u32[]{:S(2)}, u32[]{:S(2)}) collective-permute-start(f32[32,128]{1,0:T(8,128)S(1)} %next_write.2._), channel_id=1, source_target_pairs={{128,256},{136,264},{144,272},{152,280},{160,288},{168,296},{176,3... | collective-permute-start | bytes 49160 | tf_op jit(solution)/shard_map/ppermute | solution.py:443
  24.4 0.7 collective-permute-start.3
  25.4 17.3 %collective-permute-start.6 = (f32[32,128]{1,0:T(8,128)S(1)}, f32[32,128]{1,0:T(8,128)S(1)}, u32[]{:S(2)}, u32[]{:S(2)}) collective-permute-start(f32[32,128]{1,0:T(8,128)S(1)} %next_write.3._), channel_id=1, source_target_pairs={{256,448},{264,456},{272,464},{280,472},{288,480},{296,488},{304,4... | collective-permute-start | bytes 49160 | tf_op jit(solution)/shard_map/ppermute | solution.py:443
  26.7 27.5 %copy-start.3 = (f32[2,128]{1,0:T(2,128)S(1)}, f32[2,128]{1,0:T(2,128)}, u32[]{:S(2)}) copy-start(f32[2,128]{1,0:T(2,128)} %gain_ref.1) | copy-start | bytes 3076
  26.7 29.7 %copy-start.1 = (bf16[256,2048]{1,0:T(8,128)(2,1)S(1)}, bf16[256,2048]{1,0:T(8,128)(2,1)}, u32[]{:S(2)}) copy-start(bf16[256,2048]{1,0:T(8,128)(2,1)} %copy-done) | copy-start | bytes 3145732
  26.7 15.9 %collective-permute-start.5 = (f32[160,128]{1,0:T(8,128)S(1)}, f32[160,128]{1,0:T(8,128)S(1)}, u32[]{:S(2)}, u32[]{:S(2)}) collective-permute-start(f32[160,128]{1,0:T(8,128)S(1)} %offer.5), channel_id=1, source_target_pairs={{384,448},{392,456},{400,464},{408,472},{416,480},{424,488},{432,4... | collective-permute-start | bytes 245768 | tf_op jit(solution)/shard_map/ppermute | solution.py:430

commit v11 on v9

--- a/solution.py
+++ b/solution.py
@@ -192,14 +192,17 @@
         for lower, right, upper in zip(lowers, rights, uppers)
     ]
     unders = [dot(inverse[:, half:], rest) for inverse, rest in zip(inverses, moved)]
+    solveds, lasts, tails = [], [], []
     for head in range(heads):
-        solved = jnp.concatenate([uppers[head], unders[head]], axis=0)
-        solved_ref[head] = solved
+        solveds.append(jnp.concatenate([uppers[head], unders[head]], axis=0))
+        solved_ref[head] = solveds[head]
         send(solved_ref.at[head], solved_hbm.at[head])
         cumul = cumul_rows[:, head : head + 1]
-        last = cumul[rows - 1 : rows, :]
-        tail = jnp.exp(last - cumul) * keys[head]
-        pair = dot(solved, tail, 0, 0)
+        lasts.append(cumul[rows - 1 : rows, :])
+        tails.append(jnp.exp(lasts[head] - cumul) * keys[head])
+    couples = [dot(solved, tail, 0, 0) for solved, tail in zip(solveds, tails)]
+    for head in range(heads):
+        pair, last = couples[head], lasts[head]
         write_ref[head] = pair[:width]
         carry_ref[head] = jnp.exp(last) * eye_k - pair[width:]
         for part in range(GROUP // heads):

time: 70.7 us -> 70.6 us (level)
  no operation moved by 1% of the time
where the time goes in v11:
time: 70.6 us; the launch traced here: 70.2 us
  blocking collectives  25.5 us (36%)
  waiting for transfers between devices  16.5 us (23%)
  starting transfers between devices  15 us (21%)
  Pallas kernels  10.7 us (15%)
  local copies, waits for them, and re-layouts  2.24 us (3%)
    all_to_all x1, blocking collectives, per_device(): lax.all_to_all(sums.reshape(spread // 2, tokens // spread, columns), 'hea...  13.1 us
    ppermute x3, waiting for transfers between devices, per_device(): lax.ppermute(write, 'ctx', [(i, j ^ GROUP if g == 2 else j) for i, j in z...  12.2 us
    all_to_all x1, blocking collectives, per_device(): states = lax.all_to_all(starts, 'ctx', 0, 0, axis_index_groups=inner)  10.5 us
    ppermute x4, starting transfers between devices, per_device(): lax.ppermute(offered, 'ctx', [(i, i ^ GROUP) for i in group[g]])  5.51 us
    pallas_call x1, Pallas kernels, local_call(): pl.pallas_call(functools.partial(local_kernel, heads), out_shape=(jax.Sha...  5.3 us
    all_to_all x1, starting transfers between devices, per_device(): parts = lax.all_to_all(msg, 'ctx', 0, 0, axis_index_groups=inner)  4.93 us
    all_to_all x1, waiting for transfers between devices, per_device(): parts = lax.all_to_all(msg, 'ctx', 0, 0, axis_index_groups=inner)  4.31 us
    ppermute x3, starting transfers between devices, per_device(): lax.ppermute(write, 'ctx', [(i, j ^ GROUP if g == 2 else j) for i, j in z...  2.61 us
  transfers between devices with their start and end apart: 9, of which 2 were waited for; matrix products, arithmetic and copies ran while one was open for 0% of the time, Pallas kernels for 6%

profile of v11, /device:TPU:384, one launch (start us, length us, event | category | flops | bytes accessed | tf_op | source)
XLA Modules:
  0.0 70.2 jit_solution(15224268687954118483)
XLA Ops:
  0.0 5.3 %local_chunk.1 = (f32[8,160,128]{2,1,0:T(8,128)}, f32[2,256,256]{2,1,0:T(8,128)}, f32[2,256,128]{2,1,0:T(8,128)}) custom-call(bf16[512,128]{1,0:T(8,128)(2,1)} %bitcast.18, bf16[512,128]{1,0:T(8,128)(2,1)} %bitcast.19, f32[2,128]{1,0:T(2,128)} %bitcast.15, f32[4,128]{1,0:T(4,128)} %bitcast.20), custom_call_target="tpu_custom_call" | custom-call | tf_op jit(solution)/shard_map/local_chunk/pallas_call | solution.py:220
  5.3 4.9 %all-to-all-start = ((f32[8,160,128]{2,1,0:T(8,128)}), f32[8,160,128]{2,1,0:T(8,128)S(1)}, u32[]{:S(2)}, u32[]{:S(2)}) async-start(f32[8,160,128]{2,1,0:T(8,128)} %get-tuple-element.25), calls=%async_computation | async-start | bytes 1310720 | tf_op jit(solution)/shard_map/all_to_all | solution.py:396
  10.3 1.2 %copy-done.4 = bf16[256,2048]{1,0:T(8,128)(2,1)S(1)} copy-done((bf16[256,2048]{1,0:T(8,128)(2,1)S(1)}, bf16[256,2048]{1,0:T(8,128)(2,1)}, u32[]{:S(2)}) %copy-start.4) | copy-done | bytes 1048600
  11.5 1.5 %widen.1 = (f32[256,2048]{1,0:T(8,128)}, bf16[256,2048]{1,0:T(8,128)(2,1)S(1)}) custom-call(bf16[256,2048]{1,0:T(8,128)(2,1)S(1)} %copy-done.4), custom_call_target="tpu_custom_call" | custom-call | flops 1000000000 | bytes 1048576 | tf_op jit(solution)/shard_map/widen/pallas_call | solution.py:398
  13.0 1.0 %copy-done = bf16[256,2048]{1,0:T(8,128)(2,1)} copy-done((bf16[256,2048]{1,0:T(8,128)(2,1)}, bf16[256,2048]{1,0:T(8,128)(2,1)S(1)}, u32[]{:S(2)}) %copy-start) | copy-done | bytes 1048600
  14.0 1.9 %collective-permute-start.7 = (f32[256,2048]{1,0:T(8,128)}, f32[256,2048]{1,0:T(8,128)S(1)}, u32[]{:S(2)}, u32[]{:S(2)}) collective-permute-start(f32[256,2048]{1,0:T(8,128)} %get-tuple-element.40), channel_id=1, source_target_pairs={{0,1},{1,0},{2,3},{3,2},{4,5},{5,4},{6,7},{7,6},{8,9},{9,8},{10,11... | collective-permute-start | bytes 6291464 | tf_op jit(solution)/shard_map/ppermute | solution.py:404
  16.0 0.6 own_outputs.1
  16.6 4.3 %all-to-all-done.parts_ref = f32[8,160,128]{2,1,0:T(8,128)S(1)} async-done(((f32[8,160,128]{2,1,0:T(8,128)}), f32[8,160,128]{2,1,0:T(8,128)S(1)}, u32[]{:S(2)}, u32[]{:S(2)}) %all-to-all-start) | async-done | bytes 655392 | tf_op jit(solution)/shard_map/all_to_all | solution.py:396
  20.9 0.6 group_scan.1
  21.5 0.7 collective-permute-start
  22.4 0.7 collective-permute-start.2
  23.1 0.7 collective-permute-start.1
  24.0 0.7 collective-permute-start.4
  24.7 0.7 collective-permute-start.3
  25.7 1.3 %collective-permute-start.6 = (f32[32,128]{1,0:T(8,128)S(1)}, f32[32,128]{1,0:T(8,128)S(1)}, u32[]{:S(2)}, u32[]{:S(2)}) collective-permute-start(f32[32,128]{1,0:T(8,128)S(1)} %next_write.3._), channel_id=1, source_target_pairs={{256,448},{264,456},{272,464},{280,472},{288,480},{296,488},{304,4... | collective-permute-start | bytes 49160 | tf_op jit(solution)/shard_map/ppermute | solution.py:437
  27.1 3.5 %collective-permute-start.5 = (f32[160,128]{1,0:T(8,128)S(1)}, f32[160,128]{1,0:T(8,128)S(1)}, u32[]{:S(2)}, u32[]{:S(2)}) collective-permute-start(f32[160,128]{1,0:T(8,128)S(1)} %offer.5), channel_id=1, source_target_pairs={{384,448},{392,456},{400,464},{408,472},{416,480},{424,488},{432,4... | collective-permute-start | bytes 245768 | tf_op jit(solution)/shard_map/ppermute | solution.py:424
  30.6 12.2 %collective-permute-done.6.in_ref._ = f32[32,128]{1,0:T(8,128)S(1)} collective-permute-done((f32[32,128]{1,0:T(8,128)S(1)}, f32[32,128]{1,0:T(8,128)S(1)}, u32[]{:S(2)}, u32[]{:S(2)}) %collective-permute-start.6) | collective-permute-done | bytes 16416 | tf_op jit(solution)/shard_map/ppermute | solution.py:437
  42.8 0.4 start_states.1
  43.2 10.5 %all_to_all.15 = f32[8,32,128]{2,1,0:T(8,128)S(1)} all-to-all(f32[8,32,128]{2,1,0:T(8,128)S(1)} %start_states.1), channel_id=1, replica_groups={{0,8,16,24,32,40,48,56},{64,72,80,88,96,104,112,120},{128,136,144,152,1..., dimensions={0} | all-to-all | bytes 262144 | tf_op jit(solution)/shard_map/all_to_all | solution.py:446
  53.7 0.3 hidden.1
  54.0 1.9 %all-gather = f32[128,256]{1,0:T(8,128)S(1)} all-gather(f32[64,256]{1,0:T(8,128)S(1)} %get-tuple-element.37), channel_id=2, replica_groups={{0,1},{2,3},{4,5},{6,7},{8,9},{10,11},{12,13},{14,15},{16,17},{18,19},{..., dimensions={0}, use_global_device_ids=true | all-gather | bytes 196608 | tf_op jit(solution)/shard_map/all_gather | solution.py:453
  55.9 0.5 project.1
  56.4 13.1 %all_to_all.16.shares_ref = f32[4,16,2048]{2,1,0:T(8,128)S(1)} all-to-all(f32[4,16,2048]{2,1,0:T(8,128)S(1)} %bitcast.12), channel_id=1, replica_groups={{0,2,4,6},{7,5,3,1},{8,10,12,14},{15,13,11,9},{16,18,20,22},{23,21,19,1..., dimensions={0} | all-to-all | bytes 1048576 | tf_op jit(solution)/shard_map/all_to_all | solution.py:461
  69.5 0.7 row_sums.1
  (30 shorter events, 0.8 us)
Async XLA Ops:
  5.3 15.6 %all-to-all-start = ((f32[8,160,128]{2,1,0:T(8,128)}), f32[8,160,128]{2,1,0:T(8,128)S(1)}, u32[]{:S(2)}, u32[]{:S(2)}) async-start(f32[8,160,128]{2,1,0:T(8,128)} %get-tuple-element.25), calls=%async_computation | async-start | bytes 1310720 | tf_op jit(solution)/shard_map/all_to_all | solution.py:396
  10.2 5.7 %copy-start.2 = (f32[128,2]{0,1:T(2,128)S(1)}, f32[128,2]{0,1:T(2,128)}, u32[]{:S(2)}) copy-start(f32[128,2]{0,1:T(2,128)} %param.11) | copy-start | bytes 3076
  10.2 1.2 %copy-start.4 = (bf16[256,2048]{1,0:T(8,128)(2,1)S(1)}, bf16[256,2048]{1,0:T(8,128)(2,1)}, u32[]{:S(2)}) copy-start(bf16[256,2048]{1,0:T(8,128)(2,1)} %in_ref) | copy-start | bytes 3145732
  11.5 4.4 %copy-start.5 = (f32[2,256,256]{2,1,0:T(8,128)S(1)}, f32[2,256,256]{2,1,0:T(8,128)}, u32[]{:S(2)}) copy-start(f32[2,256,256]{2,1,0:T(8,128)} %get-tuple-element.27.solved_ref) | copy-start | bytes 1572868
  11.5 4.5 %copy-start.6 = (f32[2,256,128]{2,1,0:T(8,128)S(1)}, f32[2,256,128]{2,1,0:T(8,128)}, u32[]{:S(2)}) copy-start(f32[2,256,128]{2,1,0:T(8,128)} %get-tuple-element.26.keys_ref) | copy-start | bytes 786436
  11.5 4.5 %copy-start.7 = (bf16[128,2,128]{2,1,0:T(2,128)(2,1)S(1)}, bf16[128,2,128]{2,1,0:T(2,128)(2,1)}, u32[]{:S(2)}) copy-start(bf16[128,2,128]{2,1,0:T(2,128)(2,1)} %param.7) | copy-start | bytes 196612
  13.0 1.0 %copy-start = (bf16[256,2048]{1,0:T(8,128)(2,1)}, bf16[256,2048]{1,0:T(8,128)(2,1)S(1)}, u32[]{:S(2)}) copy-start(bf16[256,2048]{1,0:T(8,128)(2,1)S(1)} %get-tuple-element.39.own_ref) | copy-start | bytes 3145732
  14.0 41.9 %collective-permute-start.7 = (f32[256,2048]{1,0:T(8,128)}, f32[256,2048]{1,0:T(8,128)S(1)}, u32[]{:S(2)}, u32[]{:S(2)}) collective-permute-start(f32[256,2048]{1,0:T(8,128)} %get-tuple-element.40), channel_id=1, source_target_pairs={{0,1},{1,0},{2,3},{3,2},{4,5},{5,4},{6,7},{7,6},{8,9},{9,8},{10,11... | collective-permute-start | bytes 6291464 | tf_op jit(solution)/shard_map/ppermute | solution.py:404
  21.5 0.7 collective-permute-start
  22.4 1.4 %collective-permute-start.2 = (f32[32,128]{1,0:T(8,128)S(1)}, f32[32,128]{1,0:T(8,128)S(1)}, u32[]{:S(2)}, u32[]{:S(2)}) collective-permute-start(f32[32,128]{1,0:T(8,128)S(1)} %first_write.1._), channel_id=1, source_target_pairs={{0,128},{8,136},{16,144},{24,152},{32,160},{40,168},{48,176},{56,1... | collective-permute-start | bytes 49160 | tf_op jit(solution)/shard_map/ppermute | solution.py:437
  23.1 0.7 collective-permute-start.1
  24.0 1.4 %collective-permute-start.4 = (f32[32,128]{1,0:T(8,128)S(1)}, f32[32,128]{1,0:T(8,128)S(1)}, u32[]{:S(2)}, u32[]{:S(2)}) collective-permute-start(f32[32,128]{1,0:T(8,128)S(1)} %next_write.2._), channel_id=1, source_target_pairs={{128,256},{136,264},{144,272},{152,280},{160,288},{168,296},{176,3... | collective-permute-start | bytes 49160 | tf_op jit(solution)/shard_map/ppermute | solution.py:437
  24.7 0.7 collective-permute-start.3
  25.7 17.0 %collective-permute-start.6 = (f32[32,128]{1,0:T(8,128)S(1)}, f32[32,128]{1,0:T(8,128)S(1)}, u32[]{:S(2)}, u32[]{:S(2)}) collective-permute-start(f32[32,128]{1,0:T(8,128)S(1)} %next_write.3._), channel_id=1, source_target_pairs={{256,448},{264,456},{272,464},{280,472},{288,480},{296,488},{304,4... | collective-permute-start | bytes 49160 | tf_op jit(solution)/shard_map/ppermute | solution.py:437
  27.0 26.6 %copy-start.3 = (f32[2,128]{1,0:T(2,128)S(1)}, f32[2,128]{1,0:T(2,128)}, u32[]{:S(2)}) copy-start(f32[2,128]{1,0:T(2,128)} %gain_ref.1) | copy-start | bytes 3076
  27.1 28.9 %copy-start.1 = (bf16[256,2048]{1,0:T(8,128)(2,1)S(1)}, bf16[256,2048]{1,0:T(8,128)(2,1)}, u32[]{:S(2)}) copy-start(bf16[256,2048]{1,0:T(8,128)(2,1)} %copy-done) | copy-start | bytes 3145732
  27.1 15.7 %collective-permute-start.5 = (f32[160,128]{1,0:T(8,128)S(1)}, f32[160,128]{1,0:T(8,128)S(1)}, u32[]{:S(2)}, u32[]{:S(2)}) collective-permute-start(f32[160,128]{1,0:T(8,128)S(1)} %offer.5), channel_id=1, source_target_pairs={{384,448},{392,456},{400,464},{408,472},{416,480},{424,488},{432,4... | collective-permute-start | bytes 245768 | tf_op jit(solution)/shard_map/ppermute | solution.py:424
